TPU v7x, 32 devices: a whole 2x2x4 slice. The times are simulated.
32 devices in a mesh: expert: 2 (over x), context: 4 (over y, core), dp: 4 (over z).
Axes of the slice: x: 2, y: 2, z: 4, core: 2. Of those that a mesh axis runs over, the one named last changes fastest.
Arguments:
- tokens: bfloat16 [8, 1024, 768], P(('expert', 'dp'), 'context'), may hold values from -6 to 6
- doc_ids: int32 [8, 1024], P(('expert', 'dp')), may hold values from 0 to 1, never falling along the last dimension, each value on 1 to 768 neighbouring positions
- routes: int32 [8, 1024, 2], P(('expert', 'dp'), 'context'), may hold values from 0 to 7, all different within a row; in each aligned block of 256 rows (0 to 255, 256 to 511, ..., all dimensions but the last counted through in order) at most 64 rows name the same one
- prev_logits: float32 [8, 1024, 8], P(('expert', 'dp'), 'context'), may hold values from -3 to 3
- cotangent: float32 [8, 1024, 768], P(('expert', 'dp'), 'context'), may hold values from -6 to 6
- w_query: float32 [768, 768], P(('expert', 'context', 'dp')), may hold values from -0.21875 to 0.21875
- w_key: float32 [768, 768], P(('expert', 'context', 'dp')), may hold values from -0.21875 to 0.21875
- w_value: float32 [768, 768], P(('expert', 'context', 'dp')), may hold values from -0.21875 to 0.21875
- w_out: float32 [768, 768], P(('expert', 'context', 'dp')), may hold values from -0.625 to 0.625
- w_router: float32 [768, 8], P(('expert', 'context', 'dp')), may hold values from -0.15625 to 0.15625
- const_coef: float32 [768, 4], P(('expert', 'context', 'dp')), may hold values from -0.21875 to 0.21875
- const_value: float32 [768, 2], P(('expert', 'context', 'dp')), may hold values from -5 to 5
- norm_gains: float32 [768, 2], P(('expert', 'context', 'dp')), may hold values from 0.5 to 1.5
- expert_gate: float32 [4, 768, 2048], P('expert', None, ('context', 'dp')), may hold values from -0.21875 to 0.21875
- expert_up: float32 [4, 768, 2048], P('expert', None, ('context', 'dp')), may hold values from -0.21875 to 0.21875
- expert_down: float32 [4, 768, 2048], P('expert', None, ('context', 'dp')), may hold values from -0.25 to 0.25
Outputs:
- block_out: float32 [8, 1024, 768], P(('expert', 'dp'), 'context')
- grad_tokens: float32 [8, 1024, 768], P(('expert', 'dp'), 'context')
- grad_prev: float32 [8, 1024, 8], P(('expert', 'dp'), 'context')
- grad_query: float32 [768, 768], P(('expert', 'context', 'dp'))
- grad_key: float32 [768, 768], P(('expert', 'context', 'dp'))
- grad_value: float32 [768, 768], P(('expert', 'context', 'dp'))
- grad_out: float32 [768, 768], P(('expert', 'context', 'dp'))
- grad_router: float32 [768, 8], P(('expert', 'context', 'dp'))
- grad_coef: float32 [768, 4], P(('expert', 'context', 'dp'))
- grad_constant: float32 [768, 2], P(('expert', 'context', 'dp'))
- grad_gains: float32 [768, 2], P(('expert', 'context', 'dp'))
- grad_gate: float32 [4, 768, 2048], P('expert', None, ('context', 'dp'))
- grad_up: float32 [4, 768, 2048], P('expert', None, ('context', 'dp'))
- grad_down: float32 [4, 768, 2048], P('expert', None, ('context', 'dp'))
Inputs may be any that keep to these rules, and one draw needn't show every extreme that they name: `routes`: each row names 2 different numbers: below 4 a feed-forward expert, 4 the zero expert, 5 the copy expert, 6 and 7 the constant experts. In the rows of one device no number is named by more than 64 rows. `doc_ids`: within a sequence the document number never falls.
All inputs are finite; a program needn't handle non-finite values.
Results may differ from a plain program's by a relative error of at most 0.015.
Values may be sent and summed in bfloat16 or wider, within the bound.
A program may use at most 192 MiB of HBM per device.

v0:
```python
import jax
import jax.numpy as jnp
from jax import lax
from jax.sharding import PartitionSpec as P

D = 768
HEADS = 12
HEAD_DIM = 64


EPS = 1e-06


def contract_rows(left_side, right_side):
    return lax.dot_general(
        left_side, right_side, (((0,), (0,)), ((), ())), preferred_element_type=jnp.float32
    )


def times_transposed(left_side, right_side):
    return lax.dot_general(
        left_side, right_side, (((1,), (1,)), ((), ())), preferred_element_type=jnp.float32
    )


def soft_last(scores):
    row_top = jnp.max(scores, axis=-1, keepdims=True)
    exponent = jnp.exp(scores - row_top)
    return exponent / jnp.sum(exponent, axis=-1, keepdims=True)


def norm_back(inputs, inverse, gain_row, upstream):
    scaled = gain_row * upstream
    return inverse * scaled - inputs * inverse**3 * jnp.mean(
        scaled * inputs, axis=-1, keepdims=True
    )


def split_heads(matrix):
    return matrix.reshape(matrix.shape[0], HEADS, HEAD_DIM).transpose(1, 0, 2)


def join_heads(stacked):
    return stacked.transpose(1, 0, 2).reshape(stacked.shape[1], HEADS * HEAD_DIM)


def body(
    tokens,
    doc_ids,
    routes,
    prev_logits,
    cotangent,
    w_query,
    w_key,
    w_value,
    w_out,
    w_router,
    const_coef,
    const_value,
    norm_gains,
    expert_gate,
    expert_up,
    expert_down,
):
    q_weight, k_weight, v_weight, o_weight, r_weight, c_weight, c_value, gain_pair = (
        lax.all_gather(
            w_query.astype(jnp.bfloat16), ("expert", "context", "dp"), axis=0, tiled=True
        ),
        lax.all_gather(w_key.astype(jnp.bfloat16), ("expert", "context", "dp"), axis=0, tiled=True),
        lax.all_gather(
            w_value.astype(jnp.bfloat16), ("expert", "context", "dp"), axis=0, tiled=True
        ),
        lax.all_gather(w_out.astype(jnp.bfloat16), ("expert", "context", "dp"), axis=0, tiled=True),
        lax.all_gather(
            w_router.astype(jnp.bfloat16), ("expert", "context", "dp"), axis=0, tiled=True
        ),
        lax.all_gather(
            const_coef.astype(jnp.bfloat16), ("expert", "context", "dp"), axis=0, tiled=True
        ),
        lax.all_gather(
            const_value.astype(jnp.bfloat16), ("expert", "context", "dp"), axis=0, tiled=True
        ),
        lax.all_gather(
            norm_gains.astype(jnp.bfloat16), ("expert", "context", "dp"), axis=0, tiled=True
        ),
    )
    e_gate, e_up, e_down = (
        lax.all_gather(expert_gate.astype(jnp.bfloat16), ("context", "dp"), axis=2, tiled=True),
        lax.all_gather(expert_up.astype(jnp.bfloat16), ("context", "dp"), axis=2, tiled=True),
        lax.all_gather(expert_down.astype(jnp.bfloat16), ("context", "dp"), axis=2, tiled=True),
    )
    row_count = tokens.shape[1]
    seq_len = doc_ids.shape[1]
    softmax_scale = HEAD_DIM ** (-0.5)
    x_rows = tokens[0].astype(jnp.float32)
    gain_one = gain_pair[:, 0].astype(jnp.float32)
    gain_two = gain_pair[:, 1].astype(jnp.float32)
    inverse_one = lax.rsqrt(jnp.mean(x_rows * x_rows, axis=-1, keepdims=True) + EPS)
    normed_one = (x_rows * inverse_one * gain_one).astype(jnp.bfloat16)
    query_rows = jnp.dot(normed_one, q_weight, preferred_element_type=jnp.float32).astype(
        jnp.bfloat16
    )
    key_rows = jnp.dot(normed_one, k_weight, preferred_element_type=jnp.float32).astype(
        jnp.bfloat16
    )
    value_rows = jnp.dot(normed_one, v_weight, preferred_element_type=jnp.float32).astype(
        jnp.bfloat16
    )
    all_keys, all_values = (
        lax.all_gather(key_rows, "context", axis=0, tiled=True),
        lax.all_gather(value_rows, "context", axis=0, tiled=True),
    )
    row_start = lax.axis_index("context") * row_count
    q_place = row_start + jnp.arange(row_count, dtype=jnp.int32)
    k_place = jnp.arange(seq_len, dtype=jnp.int32)
    documents = doc_ids[0]
    q_docs = lax.dynamic_slice_in_dim(documents, row_start, row_count)
    allowed = (q_docs[:, None] == documents[None, :]) & (q_place[:, None] >= k_place[None, :])
    q_heads = split_heads(query_rows)

    def head_forward(operands):
        q_head, k_head, v_head = operands
        scores = jnp.where(allowed, times_transposed(q_head, k_head) * softmax_scale, -1e30)
        row_top = jnp.max(scores, axis=-1, keepdims=True)
        exponent = jnp.exp(scores - row_top)
        row_total = jnp.sum(exponent, axis=-1, keepdims=True)
        rounded = (exponent / row_total).astype(jnp.bfloat16)
        attended = jnp.dot(rounded, v_head, preferred_element_type=jnp.float32)
        return (attended, (row_top + jnp.log(row_total))[:, 0])

    attended, log_total = lax.map(
        head_forward, (q_heads, split_heads(all_keys), split_heads(all_values))
    )
    mixed_rows = join_heads(attended).astype(jnp.bfloat16)
    h_rows = x_rows + jnp.dot(mixed_rows, o_weight, preferred_element_type=jnp.float32)
    inverse_two = lax.rsqrt(jnp.mean(h_rows * h_rows, axis=-1, keepdims=True) + EPS)
    normed_two = (h_rows * inverse_two * gain_two).astype(jnp.bfloat16)
    a_two = normed_two.astype(jnp.float32)
    n_expert = lax.axis_size("expert")
    local_experts = expert_gate.shape[0]
    experts = local_experts * n_expert
    slot_most = row_count // 4
    route_pair = routes[0]
    route_ids = route_pair.reshape(-1)
    route_hot = (route_ids[:, None] == jnp.arange(experts, dtype=jnp.int32)[None, :]).astype(
        jnp.int32
    )
    slot_rank = jnp.sum((jnp.cumsum(route_hot, axis=0) - route_hot) * route_hot, axis=1)
    slot_index = jnp.where(
        route_ids < experts, route_ids * slot_most + slot_rank, experts * slot_most
    )
    route_number = jnp.arange(2 * row_count, dtype=jnp.int32)
    source = (
        jnp.zeros((experts * slot_most + 1,), jnp.int32).at[slot_index].set(route_number // 2)[:-1]
    )
    route_of = (
        jnp.zeros((experts * slot_most + 1,), jnp.int32).at[slot_index].set(route_number)[:-1]
    )
    filled = jnp.zeros((experts * slot_most + 1,), jnp.float32).at[slot_index].set(1.0)[:-1]
    filled_b = filled[:, None].astype(jnp.bfloat16)
    slot_pair = slot_index.reshape(row_count, 2)
    send_rows = (normed_two[source] * filled_b).reshape(n_expert, local_experts, slot_most, D)
    arriving = lax.all_to_all(send_rows, "expert", split_axis=0, concat_axis=0, tiled=True)
    gate_pre = jnp.einsum("serd,edf->serf", arriving, e_gate, preferred_element_type=jnp.float32)
    up_pre = jnp.einsum("serd,edf->serf", arriving, e_up, preferred_element_type=jnp.float32)
    sig_gate = jax.nn.sigmoid(gate_pre)
    hidden_units = (gate_pre * sig_gate * up_pre).astype(jnp.bfloat16)
    result = jnp.einsum(
        "serf,edf->serd", hidden_units, e_down, preferred_element_type=jnp.float32
    ).astype(jnp.bfloat16)
    returned = lax.all_to_all(result, "expert", split_axis=0, concat_axis=0, tiled=True).reshape(
        experts * slot_most, D
    )
    padded = jnp.concatenate([returned.astype(jnp.float32), jnp.zeros((1, D), jnp.float32)], axis=0)
    routed = padded[slot_pair]
    logits = jnp.dot(normed_two, r_weight, preferred_element_type=jnp.float32) + prev_logits[0]
    choice_hot = (
        route_pair[:, :, None] == jnp.arange(experts + 4, dtype=jnp.int32)[None, None, :]
    ).astype(jnp.float32)
    chosen = jnp.sum(choice_hot * logits[:, None, :], axis=-1)
    gate_w = soft_last(chosen)
    coef_logits = jnp.dot(normed_two, c_weight, preferred_element_type=jnp.float32)
    first = soft_last(coef_logits[:, 0:2])
    second = soft_last(coef_logits[:, 2:4])
    value_f = c_value.astype(jnp.float32)
    const_one = first[:, 0:1] * a_two + first[:, 1:2] * value_f[:, 0][None, :]
    const_two = second[:, 0:1] * a_two + second[:, 1:2] * value_f[:, 1][None, :]
    route_cube = route_pair[:, :, None]
    picked = jnp.where(
        route_cube < experts,
        routed,
        jnp.where(
            route_cube == experts,
            jnp.zeros_like(routed),
            jnp.where(
                route_cube == experts + 1,
                a_two[:, None, :],
                jnp.where(route_cube == experts + 2, const_one[:, None, :], const_two[:, None, :]),
            ),
        ),
    )
    block_rows = h_rows + jnp.sum(gate_w[:, :, None] * picked, axis=1)
    upstream = cotangent[0]
    d_picked = gate_w[:, :, None] * upstream[:, None, :]
    d_gate_w = jnp.sum(upstream[:, None, :] * picked, axis=-1)
    d_chosen = gate_w * (d_gate_w - jnp.sum(gate_w * d_gate_w, axis=-1, keepdims=True))
    d_logits = jnp.sum(choice_hot * d_chosen[:, :, None], axis=1)
    d_logits_b = d_logits.astype(jnp.bfloat16)
    d_picked_b = d_picked.reshape(2 * row_count, D).astype(jnp.bfloat16)
    d_slots = (d_picked_b[route_of] * filled_b).reshape(n_expert, local_experts, slot_most, D)
    d_result = lax.all_to_all(d_slots, "expert", split_axis=0, concat_axis=0, tiled=True)
    b_gate, b_up, b_down = (
        lax.all_gather(expert_gate.astype(jnp.bfloat16), ("context", "dp"), axis=2, tiled=True),
        lax.all_gather(expert_up.astype(jnp.bfloat16), ("context", "dp"), axis=2, tiled=True),
        lax.all_gather(expert_down.astype(jnp.bfloat16), ("context", "dp"), axis=2, tiled=True),
    )
    d_hidden = jnp.einsum("serd,edf->serf", d_result, b_down, preferred_element_type=jnp.float32)
    d_gate_pre = (d_hidden * up_pre * sig_gate * (1.0 + gate_pre * (1.0 - sig_gate))).astype(
        jnp.bfloat16
    )
    d_up_pre = (d_hidden * gate_pre * sig_gate).astype(jnp.bfloat16)
    local_gate = jnp.einsum(
        "serd,serf->edf", arriving, d_gate_pre, preferred_element_type=jnp.float32
    )
    local_up = jnp.einsum("serd,serf->edf", arriving, d_up_pre, preferred_element_type=jnp.float32)
    local_down = jnp.einsum(
        "serd,serf->edf", d_result, hidden_units, preferred_element_type=jnp.float32
    )
    d_arriving = (
        jnp.einsum("serf,edf->serd", d_gate_pre, b_gate, preferred_element_type=jnp.float32)
        + jnp.einsum("serf,edf->serd", d_up_pre, b_up, preferred_element_type=jnp.float32)
    ).astype(jnp.bfloat16)
    d_back = lax.all_to_all(d_arriving, "expert", split_axis=0, concat_axis=0, tiled=True).reshape(
        experts * slot_most, D
    )
    grad_gate, grad_up, grad_down = (
        lax.psum_scatter(local_gate, ("context", "dp"), scatter_dimension=2, tiled=True),
        lax.psum_scatter(local_up, ("context", "dp"), scatter_dimension=2, tiled=True),
        lax.psum_scatter(local_down, ("context", "dp"), scatter_dimension=2, tiled=True),
    )
    d_padded = jnp.concatenate([d_back.astype(jnp.float32), jnp.zeros((1, D), jnp.float32)], axis=0)
    d_routed = d_padded[slot_pair]
    d_copy = jnp.sum(jnp.where(route_cube == experts + 1, d_picked, 0.0), axis=1)
    d_first = jnp.sum(jnp.where(route_cube == experts + 2, d_picked, 0.0), axis=1)
    d_second = jnp.sum(jnp.where(route_cube == experts + 3, d_picked, 0.0), axis=1)
    dc_first = jnp.stack(
        [jnp.sum(d_first * a_two, axis=-1), jnp.sum(d_first * value_f[:, 0][None, :], axis=-1)],
        axis=-1,
    )
    dc_second = jnp.stack(
        [jnp.sum(d_second * a_two, axis=-1), jnp.sum(d_second * value_f[:, 1][None, :], axis=-1)],
        axis=-1,
    )
    dcl_first = first * (dc_first - jnp.sum(first * dc_first, axis=-1, keepdims=True))
    dcl_second = second * (dc_second - jnp.sum(second * dc_second, axis=-1, keepdims=True))
    d_coef_b = jnp.concatenate([dcl_first, dcl_second], axis=-1).astype(jnp.bfloat16)
    grad_constant = jnp.stack(
        [jnp.sum(d_first * first[:, 1:2], axis=0), jnp.sum(d_second * second[:, 1:2], axis=0)],
        axis=-1,
    )
    grad_coef = contract_rows(normed_two, d_coef_b)
    grad_router = contract_rows(normed_two, d_logits_b)
    d_a_two = (
        jnp.sum(d_routed, axis=1)
        + d_copy
        + first[:, 0:1] * d_first
        + second[:, 0:1] * d_second
        + times_transposed(d_coef_b, c_weight)
        + times_transposed(d_logits_b, r_weight)
    )
    gain_grad_two = jnp.sum(d_a_two * h_rows * inverse_two, axis=0)
    d_h = upstream + norm_back(h_rows, inverse_two, gain_two, d_a_two)
    d_h_b = d_h.astype(jnp.bfloat16)
    grad_o = contract_rows(mixed_rows, d_h_b)
    d_mixed = times_transposed(d_h_b, o_weight).astype(jnp.bfloat16)

    def head_backward(operands):
        q_head, k_head, v_head, d_head, lse_row = operands
        scores = times_transposed(q_head, k_head) * softmax_scale
        prob_rows = jnp.where(allowed, jnp.exp(scores - lse_row[:, None]), 0.0)
        rounded = prob_rows.astype(jnp.bfloat16)
        d_prob = times_transposed(d_head, v_head)
        delta = jnp.sum(prob_rows * d_prob, axis=-1, keepdims=True)
        d_scores = (prob_rows * (d_prob - delta)).astype(jnp.bfloat16)
        d_q = jnp.dot(d_scores, k_head, preferred_element_type=jnp.float32) * softmax_scale
        d_k = contract_rows(d_scores, q_head) * softmax_scale
        d_v = contract_rows(rounded, d_head)
        return (d_q, d_k, d_v)

    d_q_heads, d_k_heads, d_v_heads = lax.map(
        head_backward,
        (q_heads, split_heads(all_keys), split_heads(all_values), split_heads(d_mixed), log_total),
    )
    d_keys, d_values = (
        lax.psum_scatter(
            join_heads(d_k_heads).astype(jnp.bfloat16), "context", scatter_dimension=0, tiled=True
        ).astype(jnp.float32),
        lax.psum_scatter(
            join_heads(d_v_heads).astype(jnp.bfloat16), "context", scatter_dimension=0, tiled=True
        ).astype(jnp.float32),
    )
    d_query_b = join_heads(d_q_heads).astype(jnp.bfloat16)
    d_keys_b = d_keys.astype(jnp.bfloat16)
    d_values_b = d_values.astype(jnp.bfloat16)
    grad_q = contract_rows(normed_one, d_query_b)
    grad_k = contract_rows(normed_one, d_keys_b)
    grad_v = contract_rows(normed_one, d_values_b)
    d_a_one = (
        times_transposed(d_query_b, q_weight)
        + times_transposed(d_keys_b, k_weight)
        + times_transposed(d_values_b, v_weight)
    )
    gain_grad_one = jnp.sum(d_a_one * x_rows * inverse_one, axis=0)
    d_x = d_h + norm_back(x_rows, inverse_one, gain_one, d_a_one)
    grad_gain_pair = jnp.stack([gain_grad_one, gain_grad_two], axis=-1)
    s_query, s_key, s_value, s_out, s_router, s_coef, s_constant, s_gains = (
        lax.psum_scatter(grad_q, ("expert", "context", "dp"), scatter_dimension=0, tiled=True),
        lax.psum_scatter(grad_k, ("expert", "context", "dp"), scatter_dimension=0, tiled=True),
        lax.psum_scatter(grad_v, ("expert", "context", "dp"), scatter_dimension=0, tiled=True),
        lax.psum_scatter(grad_o, ("expert", "context", "dp"), scatter_dimension=0, tiled=True),
        lax.psum_scatter(grad_router, ("expert", "context", "dp"), scatter_dimension=0, tiled=True),
        lax.psum_scatter(grad_coef, ("expert", "context", "dp"), scatter_dimension=0, tiled=True),
        lax.psum_scatter(
            grad_constant, ("expert", "context", "dp"), scatter_dimension=0, tiled=True
        ),
        lax.psum_scatter(
            grad_gain_pair, ("expert", "context", "dp"), scatter_dimension=0, tiled=True
        ),
    )
    return (
        block_rows[None],
        d_x[None],
        d_logits[None],
        s_query,
        s_key,
        s_value,
        s_out,
        s_router,
        s_coef,
        s_constant,
        s_gains,
        grad_gate,
        grad_up,
        grad_down,
    )


def solution(mesh):
    return jax.shard_map(
        body,
        mesh=mesh,
        in_specs=(
            P(("expert", "dp"), "context", None),
            P(("expert", "dp"), None),
            P(("expert", "dp"), "context", None),
            P(("expert", "dp"), "context", None),
            P(("expert", "dp"), "context", None),
            P(("expert", "context", "dp"), None),
            P(("expert", "context", "dp"), None),
            P(("expert", "context", "dp"), None),
            P(("expert", "context", "dp"), None),
            P(("expert", "context", "dp"), None),
            P(("expert", "context", "dp"), None),
            P(("expert", "context", "dp"), None),
            P(("expert", "context", "dp"), None),
            P("expert", None, ("context", "dp")),
            P("expert", None, ("context", "dp")),
            P("expert", None, ("context", "dp")),
        ),
        out_specs=(
            P(("expert", "dp"), "context", None),
            P(("expert", "dp"), "context", None),
            P(("expert", "dp"), "context", None),
            P(("expert", "context", "dp"), None),
            P(("expert", "context", "dp"), None),
            P(("expert", "context", "dp"), None),
            P(("expert", "context", "dp"), None),
            P(("expert", "context", "dp"), None),
            P(("expert", "context", "dp"), None),
            P(("expert", "context", "dp"), None),
            P(("expert", "context", "dp"), None),
            P("expert", None, ("context", "dp")),
            P("expert", None, ("context", "dp")),
            P("expert", None, ("context", "dp")),
        ),
        check_vma=False,
    )
```

profile of v0, /device:TPU:1, one launch (start us, length us, event | category | flops | bytes accessed | tf_op | source)
XLA Modules:
  0.0 1544.3 jit_solution(6302447493774515337)
XLA Ops:
  12.7 64.1 %all-gather = bf16[32,24,2]{1,2,0:T(2,128)(2,1)S(1)} all-gather(bf16[1,24,2]{1,2,0:T(2,128)(2,1)S(1)} %convert_bitcast_fusion.4), channel_id=1, replica_groups=mesh['expert'=2,'context'=4,'dp'=4] {'expert','context','dp'}, dimensions={0}, use_global_device_ids=true | all-gather | bytes 3168 | tf_op jit(solution)/shard_map/all_gather | solution.py:83
  81.4 43.3 %all-gather.20.cloned.1.call-done = bf16[768,768]{1,0:T(8,128)(2,1)} async-done(((bf16[24,768]{1,0:T(8,128)(2,1)}), bf16[768,768]{1,0:T(8,128)(2,1)}) %all-gather.20.cloned.1.call-update) | async-done | bytes 1179664 | tf_op jit(solution)/shard_map/all_gather | solution.py:70
  131.3 61.7 %all-gather.2 = bf16[32,24,4]{1,2,0:T(4,128)(2,1)S(1)} all-gather(bf16[1,24,4]{1,2,0:T(4,128)(2,1)S(1)} %convert_bitcast_fusion.2), channel_id=1, replica_groups=mesh['expert'=2,'context'=4,'dp'=4] {'expert','context','dp'}, dimensions={0}, use_global_device_ids=true | all-gather | bytes 6336 | tf_op jit(solution)/shard_map/all_gather | solution.py:77
  193.2 63.7 %all-gather.1 = bf16[32,24,8]{1,2,0:T(8,128)(2,1)S(1)} all-gather(bf16[1,24,8]{1,2,0:T(8,128)(2,1)S(1)} %convert_bitcast_fusion.1), channel_id=1, replica_groups=mesh['expert'=2,'context'=4,'dp'=4] {'expert','context','dp'}, dimensions={0}, use_global_device_ids=true | all-gather | bytes 12672 | tf_op jit(solution)/shard_map/all_gather | solution.py:74
  270.4 66.8 %all-gather.3 = bf16[32,24,2]{1,2,0:T(2,128)(2,1)S(1)} all-gather(bf16[1,24,2]{1,2,0:T(2,128)(2,1)S(1)} %convert_bitcast_fusion.3), channel_id=1, replica_groups=mesh['expert'=2,'context'=4,'dp'=4] {'expert','context','dp'}, dimensions={0}, use_global_device_ids=true | all-gather | bytes 3168 | tf_op jit(solution)/shard_map/all_gather | solution.py:80
  350.4 53.1 %while.28 = (s32[]{:T(128)}, bf16[12,256,64]{1,2,0:T(8,128)(2,1)S(1)}, f32[12,256]{1,0:T(8,128)}, bf16[12,256,64]{2,1,0:T(8,128)(2,1)S(1)}, bf16[12,1024,64]{2,1...) while((s32[]{:T(128)}, ...), condition=%wide.region_4.5_spmd.clone, body=%wide.region_1.4_spmd.clone.sunk | while | flops 69992192 | bytes 3819641 | solution.py:131
  417.3 4.3 all-to-all-done.2
  425.1 5.2 fusion.60
  430.4 5.2 fusion.66
  435.6 45.4 %all-gather.26.cloned.1.call-done = bf16[2,768,2048]{2,1,0:T(8,128)(2,1)} async-done(((bf16[2,768,128]{2,1,0:T(8,128)(2,1)}), bf16[2,768,2048]{2,1,0:T(8,128)(2,1)}) %all-gather.26.cloned.1.call-update) | async-done | bytes 6291472 | tf_op jit(solution)/shard_map/all_gather | solution.py:88
  481.0 7.5 multiply_convert_fusion.2
  488.4 5.4 fusion.81
  494.6 4.6 all-to-all-start.1
  499.2 5.4 fusion.48
  504.6 5.0 fusion.84
  510.4 4.2 all-to-all-start.3
  529.5 14.3 multiply_reduce_fusion.1
  544.0 4.2 reduce_sum.275
  555.3 92.1 %while.29 = (s32[]{:T(128)}, bf16[12,256,64]{1,2,0:T(8,128)(2,1)S(1)}, bf16[12,1024,64]{1,2,0:T(8,128)(2,1)}, bf16[12,1024,64]{1,2,0:T(8,128)(2,1)}, bf16[12,256...) while((s32[]{:T(128)}, ...), condition=%wide.region_36.37_spmd.clone, body=%wide.region_34.36_spmd.clone.sunk | while | flops 170999552 | bytes 9453705 | solution.py:290
  653.2 21.0 %reduce-scatter.14.cloned.1.call-done = bf16[256,768]{0,1:T(8,128)(2,1)} async-done(((bf16[1024,768]{0,1:T(8,128)(2,1)}), bf16[256,768]{0,1:T(8,128)(2,1)}) %reduce-scatter.14.cloned.1.call-update) | async-done | bytes 393232 | tf_op jit(solution)/shard_map/reduce_scatter | solution.py:295
  677.3 27.8 %reduce-scatter.16.cloned.1.call-done = bf16[256,768]{0,1:T(8,128)(2,1)} async-done(((bf16[1024,768]{0,1:T(8,128)(2,1)}), bf16[256,768]{0,1:T(8,128)(2,1)}) %reduce-scatter.16.cloned.1.call-update) | async-done | bytes 393232 | tf_op jit(solution)/shard_map/reduce_scatter | solution.py:298
  708.2 7.6 convolution_bitcast_fusion.4
  715.9 7.6 convolution_bitcast_fusion.3
  724.7 6.4 convolution_bitcast_fusion.2
  735.3 39.7 %all-reduce.6 = (f32[768,8]{0,1:T(8,128)S(1)}, f32[768,4]{0,1:T(4,128)S(1)}, f32[768,2]{0,1:T(2,128)S(1)}, f32[768,2]{0,1:T(2,128)S(1)}) all-reduce(f32[768,8]{0,1:T(8,128)S(1)} %fusion.127, f32[768,4]{0,1:T(4,128)S(1)} %fusion.139, ...), channel_id=8, replica_groups=mesh['expert'=2,'context'=4,'dp'=4] {'expert','context','dp'}, use_global_device_ids=true, to_apply=%region_44.45.clone | all-reduce | flops 12288 | bytes 98304
  778.7 29.6 %reduce-scatter.18.cloned.1.call-done = f32[24,768]{1,0:T(8,128)} async-done(((f32[768,768]{1,0:T(8,128)}), f32[24,768]{1,0:T(8,128)}) %reduce-scatter.18.cloned.1.call-update) | async-done | bytes 73744 | tf_op jit(solution)/shard_map/reduce_scatter | solution.py:317
  808.3 104.9 %reduce-scatter.24.cloned.1.call-done = f32[24,768]{1,0:T(8,128)} async-done(((f32[768,768]{1,0:T(8,128)}), f32[24,768]{1,0:T(8,128)}) %reduce-scatter.24.cloned.1.call-update) | async-done | bytes 73744 | tf_op jit(solution)/shard_map/reduce_scatter | solution.py:320
  913.2 103.7 %reduce-scatter.20.cloned.1.call-done = f32[24,768]{1,0:T(8,128)} async-done(((f32[768,768]{1,0:T(8,128)}), f32[24,768]{1,0:T(8,128)}) %reduce-scatter.20.cloned.1.call-update) | async-done | bytes 73744 | tf_op jit(solution)/shard_map/reduce_scatter | solution.py:318
  1016.9 104.8 %reduce-scatter.22.cloned.1.call-done = f32[24,768]{1,0:T(8,128)} async-done(((f32[768,768]{1,0:T(8,128)}), f32[24,768]{1,0:T(8,128)}) %reduce-scatter.22.cloned.1.call-update) | async-done | bytes 73744 | tf_op jit(solution)/shard_map/reduce_scatter | solution.py:319
  1121.7 138.9 %reduce-scatter.26.cloned.1.call-done = f32[2,768,128]{2,1,0:T(8,128)} async-done(((f32[2,768,2048]{2,1,0:T(8,128)}), f32[2,768,128]{2,1,0:T(8,128)}) %reduce-scatter.26.cloned.1.call-update) | async-done | bytes 786448 | tf_op jit(solution)/shard_map/reduce_scatter | solution.py:237
  1260.6 138.4 %reduce-scatter.28.cloned.1.call-done = f32[2,768,128]{2,1,0:T(8,128)} async-done(((f32[2,768,2048]{2,1,0:T(8,128)}), f32[2,768,128]{2,1,0:T(8,128)}) %reduce-scatter.28.cloned.1.call-update) | async-done | bytes 786448 | tf_op jit(solution)/shard_map/reduce_scatter | solution.py:238
  1398.9 138.4 %reduce-scatter.30.cloned.1.call-done = f32[2,768,128]{2,1,0:T(8,128)} async-done(((f32[2,768,2048]{2,1,0:T(8,128)}), f32[2,768,128]{2,1,0:T(8,128)}) %reduce-scatter.30.cloned.1.call-update) | async-done | bytes 786448 | tf_op jit(solution)/shard_map/reduce_scatter | solution.py:239
  (468 shorter events, 249.4 us)
Async XLA Ops:
  7.2 71.5 %all-gather.16.cloned.1.call-start = ((), (), s32[]{:S(2)}) async-start(), calls=%async_computation.14 | async-start | bytes 1216512 | tf_op jit(solution)/shard_map/all_gather | solution.py:69
  8.8 116.0 %all-gather.20.cloned.1.call-start = ((), (), s32[]{:S(2)}) async-start(), calls=%async_computation.16 | async-start | bytes 1216512 | tf_op jit(solution)/shard_map/all_gather | solution.py:70
  10.3 328.6 %all-gather.14.cloned.1.call-start = ((), (), s32[]{:S(2)}) async-start(), calls=%async_computation.13 | async-start | bytes 1216512 | tf_op jit(solution)/shard_map/all_gather | solution.py:66
  11.9 112.8 %copy-start = (bf16[1,256,768]{2,1,0:T(8,128)(2,1)S(1)}, bf16[1,256,768]{2,1,0:T(8,128)(2,1)}, u32[]{:S(2)}) copy-start(bf16[1,256,768]{2,1,0:T(8,128)(2,1)} %param.20) | copy-start | bytes 1179652
  11.9 329.4 %all-gather.18.cloned.1.call-start = ((), (), s32[]{:S(2)}) async-start(), calls=%async_computation.15 | async-start | bytes 1966080 | tf_op jit(solution)/shard_map/all_gather | solution.py:110
  77.0 329.5 %copy-start.25 = (f32[768]{0:T(1024)}, f32[768]{0:T(1024)S(1)}, u32[]{:S(2)}) copy-start(f32[768]{0:T(1024)S(1)} %get-tuple-element.289) | copy-start | bytes 9220
  78.7 260.3 %copy-start.29 = (f32[256]{0:T(256)}, f32[256]{0:T(256)S(1)}, u32[]{:S(2)}) copy-start(f32[256]{0:T(256)S(1)} %get-tuple-element.367) | copy-start | bytes 3076
  81.4 264.5 %all-gather.22.cloned.1.call-start = ((), (), s32[]{:S(2)}) async-start(), calls=%async_computation.17 | async-start | bytes 1966080 | tf_op jit(solution)/shard_map/all_gather | solution.py:111
  127.3 276.2 %all-gather.24.cloned.1.call-start = ((), (), s32[]{:S(2)}) async-start(), calls=%async_computation.18 | async-start | bytes 1216512 | tf_op jit(solution)/shard_map/all_gather | solution.py:73
  128.0 297.1 %all-gather.30.cloned.1.call-start = ((), (), s32[]{:S(2)}) async-start(), calls=%async_computation.21 | async-start | bytes 6684672 | tf_op jit(solution)/shard_map/all_gather | solution.py:90
  128.9 301.4 %all-gather.28.cloned.1.call-start = ((), (), s32[]{:S(2)}) async-start(), calls=%async_computation.20 | async-start | bytes 6684672 | tf_op jit(solution)/shard_map/all_gather | solution.py:89
  129.8 127.7 %copy-start.2 = (f32[1,256,768]{2,1,0:T(8,128)S(1)}, f32[1,256,768]{2,1,0:T(8,128)}, u32[]{:S(2)}) copy-start(f32[1,256,768]{2,1,0:T(8,128)} %param.24) | copy-start | bytes 2359300
  129.8 351.2 %all-gather.26.cloned.1.call-start = ((), (), s32[]{:S(2)}) async-start(), calls=%async_computation.19 | async-start | bytes 6684672 | tf_op jit(solution)/shard_map/all_gather | solution.py:88
  193.1 223.8 %copy-start.27 = (bf16[768,4]{0,1:T(4,128)(2,1)}, bf16[768,4]{0,1:T(4,128)(2,1)S(1)}, u32[]{:S(2)}) copy-start(bf16[768,4]{0,1:T(4,128)(2,1)S(1)} %reshape.492) | copy-start | bytes 18436
  337.4 177.2 %copy-start.31 = (f32[768]{0:T(1024)}, f32[768]{0:T(1024)S(1)}, u32[]{:S(2)}) copy-start(f32[768]{0:T(1024)S(1)} %get-tuple-element.283) | copy-start | bytes 9220
  337.4 177.2 %copy-start.33 = (f32[768]{0:T(1024)}, f32[768]{0:T(1024)S(1)}, u32[]{:S(2)}) copy-start(f32[768]{0:T(1024)S(1)} %get-tuple-element.284) | copy-start | bytes 9220
  413.4 8.2 all-to-all-start.2
  417.3 97.3 %copy-start.47 = (f32[256,1]{0,1:T(1,128)}, f32[256,1]{0,1:T(1,128)S(1)}, u32[]{:S(2)}) copy-start(f32[256,1]{0,1:T(1,128)S(1)} %get-tuple-element.362) | copy-start | bytes 3076
  417.3 97.3 %copy-start.51 = (f32[256,1]{0,1:T(1,128)}, f32[256,1]{0,1:T(1,128)S(1)}, u32[]{:S(2)}) copy-start(f32[256,1]{0,1:T(1,128)S(1)} %get-tuple-element.363) | copy-start | bytes 3076
  421.6 8.7 all-to-all-start
  494.6 15.8 %all-to-all-start.1 = ((bf16[2,2,64,768]{3,2,1,0:T(8,128)(2,1)}), bf16[2,2,64,768]{3,2,1,0:T(8,128)(2,1)}, u32[]{:S(2)}, u32[]{:S(2)}) async-start(bf16[2,2,64,768]{3,2,1,0:T(8,128)(2,1)} %copy.192), calls=%async_computation.1 | async-start | bytes 786432 | tf_op jit(solution)/shard_map/all_to_all | solution.py:171
  510.4 12.4 all-to-all-start.3
  514.5 159.6 %reduce-scatter.14.cloned.1.call-start = ((), (), s32[]{:S(2)}) async-start(), calls=%async_computation.22 | async-start | bytes 1966080 | tf_op jit(solution)/shard_map/reduce_scatter | solution.py:295
  544.0 187.4 %copy-start.23 = (f32[256,8]{0,1:T(8,128)}, f32[256,8]{0,1:T(8,128)S(1)}, u32[]{:S(2)}) copy-start(f32[256,8]{0,1:T(8,128)S(1)} %select_reduce_fusion) | copy-start | bytes 24580
  647.4 57.7 %reduce-scatter.16.cloned.1.call-start = ((), (), s32[]{:S(2)}) async-start(), calls=%async_computation.23 | async-start | bytes 1966080 | tf_op jit(solution)/shard_map/reduce_scatter | solution.py:298
  648.1 160.2 %reduce-scatter.18.cloned.1.call-start = ((), (), s32[]{:S(2)}) async-start(), calls=%async_computation.24 | async-start | bytes 2433024 | tf_op jit(solution)/shard_map/reduce_scatter | solution.py:317
  650.2 262.9 %reduce-scatter.24.cloned.1.call-start = ((), (), s32[]{:S(2)}) async-start(), calls=%async_computation.27 | async-start | bytes 2433024 | tf_op jit(solution)/shard_map/reduce_scatter | solution.py:320
  653.2 363.8 %reduce-scatter.20.cloned.1.call-start = ((), (), s32[]{:S(2)}) async-start(), calls=%async_computation.25 | async-start | bytes 2433024 | tf_op jit(solution)/shard_map/reduce_scatter | solution.py:318
  677.2 444.4 %reduce-scatter.22.cloned.1.call-start = ((), (), s32[]{:S(2)}) async-start(), calls=%async_computation.26 | async-start | bytes 2433024 | tf_op jit(solution)/shard_map/reduce_scatter | solution.py:319
  708.2 552.4 %reduce-scatter.26.cloned.1.call-start = ((), (), s32[]{:S(2)}) async-start(), calls=%async_computation.28 | async-start | bytes 13369344 | tf_op jit(solution)/shard_map/reduce_scatter | solution.py:237
  715.9 683.0 %reduce-scatter.28.cloned.1.call-start = ((), (), s32[]{:S(2)}) async-start(), calls=%async_computation.29 | async-start | bytes 13369344 | tf_op jit(solution)/shard_map/reduce_scatter | solution.py:238
  723.5 813.8 %reduce-scatter.30.cloned.1.call-start = ((), (), s32[]{:S(2)}) async-start(), calls=%async_computation.30 | async-start | bytes 13369344 | tf_op jit(solution)/shard_map/reduce_scatter | solution.py:239
  (57 other events, 646.4 us)
Sparse Core Ops, SparseCore 0:
  11.5 56.6 all-gather.15
  71.6 53.0 all-gather.19
  128.2 53.0 all-gather.13
  183.3 18.6 all-gather.17
  203.9 19.7 all-gather.21
  227.0 54.2 all-gather.23
  284.0 64.5 all-gather.29
  351.2 63.7 all-gather.27
  417.1 63.8 all-gather.25
  647.5 26.6 reduce-scatter.13
  676.9 28.1 reduce-scatter.15
  710.8 97.4 reduce-scatter.17
  815.0 98.1 reduce-scatter.23
  918.9 97.9 reduce-scatter.19
  1023.5 98.1 reduce-scatter.21
  1126.2 134.3 reduce-scatter.25
  1265.0 133.8 reduce-scatter.27
  1403.4 133.8 reduce-scatter.29
where the time goes:
time: 1560 us; the launch traced here: 1540 us
  waiting for transfers between devices  901 us (58%)
  blocking collectives  296 us (19%)
  matrix products  194 us (12%)
  local copies, waits for them, and re-layouts  71.9 us (5%)
  other arithmetic  48 us (3%)
  starting transfers between devices  16.6 us (1%)
  between operations  15.8 us (1%)
    reduce_scatter x1, waiting for transfers between devices, body(): lax.psum_scatter(local_gate, ('context', 'dp'), scatter_dimension=2, tile...  139 us
    reduce_scatter x1, waiting for transfers between devices, body(): lax.psum_scatter(local_down, ('context', 'dp'), scatter_dimension=2, tile...  138 us
    reduce_scatter x1, waiting for transfers between devices, body(): lax.psum_scatter(local_up, ('context', 'dp'), scatter_dimension=2, tiled=...  138 us
    reduce_scatter x1, waiting for transfers between devices, body(): lax.psum_scatter(grad_o, ('expert', 'context', 'dp'), scatter_dimension=0...  105 us
    reduce_scatter x1, waiting for transfers between devices, body(): lax.psum_scatter(grad_v, ('expert', 'context', 'dp'), scatter_dimension=0...  105 us
    reduce_scatter x1, waiting for transfers between devices, body(): lax.psum_scatter(grad_k, ('expert', 'context', 'dp'), scatter_dimension=0...  104 us
    all_gather x1, blocking collectives, body(): lax.all_gather(const_value.astype(jnp.bfloat16), ('expert', 'context', 'd...  66.8 us
    all_gather x1, blocking collectives, body(): lax.all_gather(norm_gains.astype(jnp.bfloat16), ('expert', 'context', 'dp...  64.1 us
  transfers between devices with their start and end apart: 22, of which 12 were waited for; matrix products, arithmetic and copies ran while one was open for 11% of the time, Pallas kernels for 0%

commit v1 on v0

v1 whole, which is shorter than its diff:
```python
import functools

import jax
import jax.numpy as jnp
from jax import lax
from jax.experimental import pallas as pl
from jax.experimental.pallas import tpu as pltpu
from jax.sharding import PartitionSpec as P

D = 768
HEADS = 12
HEAD_DIM = 64
EPS = 1e-06
SMALL = 64
LANES = 128
VMEM_LIMIT = 60 * 2**20
MESH = pl.DeviceIdType.MESH
F32 = jnp.float32
BF16 = jnp.bfloat16
ALL_AXES = ("expert", "context", "dp")


def dot(left, right, left_dim=1, right_dim=0):
    return lax.dot_general(
        left, right, (((left_dim,), (right_dim,)), ((), ())), preferred_element_type=F32
    )


def position():
    return lax.axis_index("expert"), lax.axis_index("context"), lax.axis_index("dp")


def remote(src, dst, send_sem, recv_sem, device):
    return pltpu.make_async_remote_copy(
        src_ref=src,
        dst_ref=dst,
        send_sem=send_sem,
        recv_sem=recv_sem,
        device_id=device,
        device_id_type=MESH,
    )


def greet(devices):
    barrier = pltpu.get_barrier_semaphore()
    for device in devices:
        pl.semaphore_signal(barrier, inc=1, device_id=device, device_id_type=MESH)
    pl.semaphore_wait(barrier, len(devices))


def context_peers(sizes, place):
    e, c, d = place
    pairs = sizes[1] // 2
    outer, inner = c // 2, c % 2
    peers = [(e, outer * 2 + 1 - inner, d)]
    for k in range(1, pairs):
        peers.append((e, lax.rem(outer + k, pairs) * 2 + inner, d))
    return peers


def expert_peers(sizes, place):
    e, c, d = place
    return [(lax.rem(e + j, sizes[0]), c, d) for j in range(1, sizes[0])]


class ContextGather:
    def __init__(self, sizes, place, own, slot, send, recv):
        e, c, d = place
        self.pairs = sizes[1] // 2
        self.place, self.own, self.slot = place, own, slot
        self.send, self.recv = send, recv
        self.outer, self.inner = c // 2, c % 2
        self.peers = context_peers(sizes, place)
        self.copies = []
        self.forwards = []

    def start(self):
        for k in [*range(1, self.pairs), 0]:
            copy = remote(
                self.own, self.slot(self.place[1]), self.send(k), self.recv(k), self.peers[k]
            )
            copy.start()
            self.copies.append((k, copy))

    def origin(self, k):
        return lax.rem(self.outer - k + self.pairs, self.pairs) * 2 + self.inner

    def forward(self):
        for k, copy in self.copies:
            if k > 0:
                copy.wait_recv()
                block = self.slot(self.origin(k))
                n = self.pairs - 1 + k
                onward = remote(block, block, self.send(n), self.recv(n), self.peers[0])
                onward.start()
                self.forwards.append(onward)

    def finish(self):
        for k, copy in self.copies:
            if k == 0:
                copy.wait_recv()
            copy.wait_send()
        for copy in self.forwards:
            copy.wait()


def gather_kernel(
    sizes, a_ref, o_ref, x_ref, ag_ref, og_ref, xg_ref, local, s_a, r_a, s_b, r_b, s_o, r_o, s_x, r_x
):
    n_e, n_c, n_d = sizes
    place = e, c, d = position()
    pairs = n_c // 2
    keep = [
        pltpu.make_async_copy(a_ref.at[c], ag_ref.at[e, c, d], local.at[0]),
        pltpu.make_async_copy(o_ref, og_ref.at[e, c, d], local.at[1]),
        pltpu.make_async_copy(x_ref, xg_ref.at[c], local.at[2]),
    ]
    for copy in keep:
        copy.start()
    c_peers = [(e, lax.rem(c + k, n_c), d) for k in range(1, n_c)]
    d_peers = [(e, c, lax.rem(d + k, n_d)) for k in range(1, n_d)]
    e_peers = expert_peers(sizes, place)
    greet(c_peers + d_peers + e_peers)
    turn = []
    for k in range(1, n_c):
        copy = remote(
            a_ref.at[lax.rem(c + k, n_c)],
            ag_ref.at[e, c, d],
            s_a.at[k - 1],
            r_a.at[k - 1],
            c_peers[k - 1],
        )
        copy.start()
        turn.append(copy)
    rows = ContextGather(
        sizes, place, x_ref, lambda j: xg_ref.at[j], lambda k: s_x.at[k], lambda k: r_x.at[k]
    )
    rows.start()

    def spread(own, slot, send, recv, base):
        along = []
        for k in range(1, n_d):
            copy = remote(
                own, slot(e, d), send.at[base + k - 1], recv.at[base + k - 1], d_peers[k - 1]
            )
            copy.start()
            along.append(copy)
        across = []
        for j in range(1, n_e):
            n = base + n_d - 1 + (j - 1) * n_d
            copy = remote(own, slot(e, d), send.at[n], recv.at[n], e_peers[j - 1])
            copy.start()
            across.append(copy)
        return along, across

    def onward(parts, slot, send, recv, base):
        along, across = parts
        for k in range(1, n_d):
            along[k - 1].wait_recv()
            block = slot(e, lax.rem(d - k + n_d, n_d))
            for j in range(1, n_e):
                n = base + n_d - 1 + (j - 1) * n_d + k
                copy = remote(block, block, send.at[n], recv.at[n], e_peers[j - 1])
                copy.start()
                across.append(copy)

    o_slot = lambda j, k: og_ref.at[j, c, k]
    a_slot = lambda j, k: ag_ref.at[j, :, k]
    o_parts = spread(o_ref, o_slot, s_o, r_o, 0)
    for copy in turn:
        copy.wait()
    for copy in keep:
        copy.wait()
    a_parts = spread(ag_ref.at[e, :, d], a_slot, s_b, r_b, 0)
    onward(o_parts, o_slot, s_o, r_o, 0)
    rows.forward()
    for copy in o_parts[1]:
        copy.wait_recv()
    base = (n_d - 1) + (n_e - 1) * n_d
    whole = ContextGather(
        sizes,
        place,
        og_ref.at[:, c],
        lambda j: og_ref.at[:, j],
        lambda k: s_o.at[base + k],
        lambda k: r_o.at[base + k],
    )
    whole.start()
    onward(a_parts, a_slot, s_b, r_b, 0)
    whole.forward()
    for copy in a_parts[1]:
        copy.wait()
    for copy in [*a_parts[0], *o_parts[0], *o_parts[1]]:
        copy.wait_send()
    rows.finish()
    whole.finish()


def gather_first(sizes, a_part, o_part, x_part):
    n_e, n_c, n_d = sizes
    dma = pltpu.SemaphoreType.DMA
    spread = (n_d - 1) + (n_e - 1) * n_d
    counts = [n_c - 1, n_c - 1, spread, spread, spread + n_c - 1, spread + n_c - 1, n_c - 1, n_c - 1]
    anywhere = pl.BlockSpec(memory_space=pl.ANY)
    return pl.pallas_call(
        functools.partial(gather_kernel, sizes),
        out_shape=(
            jax.ShapeDtypeStruct((n_e, n_c, n_d, *a_part.shape[1:]), BF16),
            jax.ShapeDtypeStruct((n_e, n_c, n_d, *o_part.shape), BF16),
            jax.ShapeDtypeStruct((n_c, *x_part.shape), BF16),
        ),
        in_specs=[anywhere] * 3,
        out_specs=(anywhere,) * 3,
        scratch_shapes=[dma((3,))] + [dma((n,)) for n in counts],
        compiler_params=pltpu.CompilerParams(collective_id=0, has_side_effects=True),
        name="gather_first",
    )(a_part, o_part, x_part)


def softmax_pair(left, right):
    top = jnp.maximum(left, right)
    left, right = jnp.exp(left - top), jnp.exp(right - top)
    total = left + right
    return left / total, right / total


def route_parts(routes_t, routes, small, n_ff, n_all, slots):
    rows = routes.shape[0]
    hot = lax.broadcasted_iota(jnp.int32, (LANES, rows), 0)
    marks = [(hot == routes_t[k : k + 1, :]) & (hot < n_ff) for k in range(2)]
    both = (marks[0] | marks[1]).astype(F32)
    earlier = lax.broadcasted_iota(jnp.int32, (rows, rows), 0) < lax.broadcasted_iota(
        jnp.int32, (rows, rows), 1
    )
    rank = dot(both.astype(BF16), earlier.astype(F32).astype(BF16))
    number = lax.broadcasted_iota(jnp.int32, (slots, rows), 0).astype(F32)
    tables = []
    for k in range(2):
        wanted = jnp.where(marks[k], rank, -1.0)
        tables.append(
            jnp.concatenate(
                [(number == wanted[j : j + 1, :]).astype(F32) for j in range(n_ff)], axis=0
            ).astype(BF16)
        )
    lane = lax.broadcasted_iota(jnp.int32, (rows, LANES), 1)
    picks = [(lane == routes[:, k : k + 1]).astype(F32) for k in range(2)]
    chosen = [
        jnp.sum(jnp.where(picks[k] > 0, small, 0.0), axis=1, keepdims=True) for k in range(2)
    ]
    w_pair = softmax_pair(chosen[0], chosen[1])
    first = softmax_pair(small[:, n_all : n_all + 1], small[:, n_all + 1 : n_all + 2])
    second = softmax_pair(small[:, n_all + 2 : n_all + 3], small[:, n_all + 3 : n_all + 4])
    return tables, picks, w_pair, first, second


def front_kernel(
    sizes,
    cfg,
    xg_ref,
    xown_ref,
    wqkv_ref,
    wo_ref,
    wsm_ref,
    vec_ref,
    dcol_ref,
    drow_ref,
    routes_ref,
    routest_ref,
    prev_ref,
    g_ref,
    a1_ref,
    qt_ref,
    kh_ref,
    vh_ref,
    mixed_ref,
    h_ref,
    a2_ref,
    small_ref,
    p_ref,
    slots_ref,
    o_scr,
    vt_scr,
    p_scr,
    sbuf,
    xin,
    p_sem,
    s_o,
    r_o,
    s_x,
    r_x,
    s_g,
    r_g,
    l_g,
):
    n_e, n_c, n_d = sizes
    hp, n_ff, n_all, n_loc, slots = cfg
    hc = hp * HEAD_DIM
    place = e, c, d = position()
    length = xg_ref.shape[0]
    rows = length // n_c
    c_all = [(e, lax.rem(c + k, n_c), d) for k in range(1, n_c)]
    e_peers = expert_peers(sizes, place)
    greet(c_all + e_peers)

    gain_one = vec_ref[0:1, :]
    for b in range(n_c):
        part = pl.ds(b * rows, rows)
        x = xg_ref[part, :].astype(F32)
        inverse = lax.rsqrt(jnp.mean(x * x, axis=-1, keepdims=True) + EPS)
        a1_ref[part, :] = (x * inverse * gain_one).astype(BF16)
    a1 = a1_ref[...]
    wqkv = wqkv_ref[...]
    q_t = dot(wqkv[:, :hc], a1, 0, 1).astype(BF16) * jnp.asarray(HEAD_DIM**-0.5, BF16)
    qt_ref[...] = q_t
    kv = dot(a1, wqkv[:, hc:]).astype(BF16)
    for j in range(hp):
        kh_ref[j] = kv[:, j * HEAD_DIM : (j + 1) * HEAD_DIM]
        vh_ref[j] = kv[:, hc + j * HEAD_DIM : hc + (j + 1) * HEAD_DIM]
    vt_scr[...] = dot(wqkv[:, 2 * hc :], a1, 0, 1).astype(BF16)

    turn = 0
    p_copies = {}
    for b in reversed(range(n_c)):
        reach = (b + 1) * rows
        key_place = lax.broadcasted_iota(jnp.int32, (reach, rows), 0)
        q_place = lax.broadcasted_iota(jnp.int32, (reach, rows), 1) + b * rows
        allowed = (dcol_ref[:reach, :] == drow_ref[:, b * rows : reach]) & (key_place <= q_place)
        bias = jnp.where(allowed, 0.0, -1e30)
        for j in range(hp):
            head = slice(j * HEAD_DIM, (j + 1) * HEAD_DIM)
            scores = dot(kh_ref[j, :reach, :], qt_ref[head, b * rows : reach]) + bias
            top = jnp.max(scores, axis=0, keepdims=True)
            exponent = jnp.exp(scores - top)
            total = jnp.sum(exponent, axis=0, keepdims=True)
            rounded = (exponent * (1.0 / total)).astype(BF16)
            slot = turn % 2
            if turn >= 2:
                p_copies[turn - 2].wait()
            p_scr[slot, :reach, :] = rounded
            copy = pltpu.make_async_copy(
                p_scr.at[slot, pl.ds(0, reach)], p_ref.at[j, b, pl.ds(0, reach)], p_sem.at[slot]
            )
            copy.start()
            p_copies[turn] = copy
            turn += 1
            o_scr[b, head, :] = dot(vt_scr[head, :reach], rounded).astype(BF16)

        @pl.when(c != b)
        def _():
            remote(
                o_scr.at[b], mixed_ref.at[c], s_o.at[b], r_o.at[c], (e, b, d)
            ).start()

    for n in range(max(0, turn - 2), turn):
        p_copies[n].wait()
    mixed_ref[pl.ds(c, 1)] = o_scr[pl.ds(c, 1)]
    for b in range(n_c):

        @pl.when(c != b)
        def _():
            copy = remote(o_scr.at[b], mixed_ref.at[b], s_o.at[b], r_o.at[b], (e, b, d))
            copy.wait_send()
            copy.wait_recv()

    mixed = mixed_ref[...].reshape(n_c * hc, rows)
    h = xown_ref[...].astype(F32) + dot(mixed, wo_ref[...], 0, 0)
    h_ref[...] = h
    inverse = lax.rsqrt(jnp.mean(h * h, axis=-1, keepdims=True) + EPS)
    a2 = (h * inverse * vec_ref[1:2, :]).astype(BF16)
    a2_ref[...] = a2
    small = dot(a2, wsm_ref[...]) + prev_ref[...]
    small_ref[...] = small
    tables, _, w_pair, _, _ = route_parts(
        routest_ref[...], routes_ref[...], small, n_ff, n_all, slots
    )
    per = n_loc * slots
    crossing = {}
    gathers = {}
    g = g_ref[...]
    for t in range(2):
        if t == 0:
            block = dot(tables[0] + tables[1], a2).astype(BF16)
        else:
            block = dot(tables[0], (w_pair[0] * g).astype(BF16)) + dot(
                tables[1], (w_pair[1] * g).astype(BF16)
            )
            block = block.astype(BF16)
        for k in range(n_e):
            sbuf[t, k] = block[k * per : (k + 1) * per, :]
        for j in range(1, n_e):
            n = t * n_e + j
            copy = remote(
                sbuf.at[t, lax.rem(e + j, n_e)],
                xin.at[t, e],
                s_x.at[n],
                r_x.at[n],
                e_peers[j - 1],
            )
            copy.start()
            crossing[t, j] = copy

        def gather(j, own, t=t):
            src = lax.rem(e - j + n_e, n_e)
            base = (t * n_e + j) * (n_c - 1)
            keep = pltpu.make_async_copy(own, slots_ref.at[c, t, src], l_g.at[t * n_e + j])
            keep.start()
            made = ContextGather(
                sizes,
                place,
                own,
                lambda k: slots_ref.at[k, t, src],
                lambda k: s_g.at[base + k],
                lambda k: r_g.at[base + k],
            )
            made.start()
            gathers[t, j] = (made, keep)

        gather(0, sbuf.at[t, e])
        crossing[t, 0] = gather
    for t in range(2):
        for j in range(1, n_e):
            crossing[t, j].wait_recv()
            crossing[t, 0](j, xin.at[t, lax.rem(e - j + n_e, n_e)])
    for made, _ in gathers.values():
        made.forward()
    for made, keep in gathers.values():
        made.finish()
        keep.wait()
    for t in range(2):
        for j in range(1, n_e):
            crossing[t, j].wait_send()


def front(sizes, cfg, *operands):
    n_e, n_c, n_d = sizes
    hp, n_ff, n_all, n_loc, slots = cfg
    hc = hp * HEAD_DIM
    length = operands[0].shape[0]
    rows = length // n_c
    per = n_loc * slots
    dma = pltpu.SemaphoreType.DMA
    vmem = pl.BlockSpec(memory_space=pltpu.VMEM)
    anywhere = pl.BlockSpec(memory_space=pl.ANY)
    shape = jax.ShapeDtypeStruct
    gathers = 2 * n_e * (n_c - 1)
    return pl.pallas_call(
        functools.partial(front_kernel, sizes, cfg),
        out_shape=(
            shape((length, D), BF16),
            shape((hc, length), BF16),
            shape((hp, length, HEAD_DIM), BF16),
            shape((hp, length, HEAD_DIM), BF16),
            shape((n_c, hc, rows), BF16),
            shape((rows, D), F32),
            shape((rows, D), BF16),
            shape((rows, LANES), F32),
            shape((hp, n_c, length, rows), BF16),
            shape((n_c, 2, n_e, per, D), BF16),
        ),
        in_specs=[vmem] * len(operands),
        out_specs=(vmem,) * 8 + (anywhere,) * 2,
        scratch_shapes=[
            pltpu.VMEM((n_c, hc, rows), BF16),
            pltpu.VMEM((hc, length), BF16),
            pltpu.VMEM((2, length, rows), BF16),
            pltpu.VMEM((2, n_e, per, D), BF16),
            pltpu.VMEM((2, n_e, per, D), BF16),
            dma((2,)),
            dma((n_c,)),
            dma((n_c,)),
            dma((2 * n_e,)),
            dma((2 * n_e,)),
            dma((gathers,)),
            dma((gathers,)),
            dma((2 * n_e,)),
        ],
        compiler_params=pltpu.CompilerParams(
            collective_id=1, has_side_effects=True, vmem_limit_bytes=VMEM_LIMIT
        ),
        name="front",
    )(*operands)


def expert_kernel(x_ref, dy_ref, w_ref, out_ref, gw_ref, total):
    step = pl.program_id(1)
    parts = w_ref.shape[0]
    x = x_ref[...].reshape(-1, D)
    dy = dy_ref[...].reshape(-1, D)
    block = out_ref.shape[0:1] + out_ref.shape[2:]
    gate, up, down = [
        jnp.concatenate([w_ref[k, n, 0] for k in range(parts)], axis=1) for n in range(3)
    ]
    gate_pre = dot(x, gate)
    up_pre = dot(x, up)
    sig = jax.nn.sigmoid(gate_pre)
    hidden = (gate_pre * sig * up_pre).astype(BF16)
    result = dot(hidden, down, 1, 1).astype(BF16)
    out_ref[:, 0] = result.reshape(block)
    d_hidden = dot(dy, down)
    d_gate = (d_hidden * up_pre * sig * (1.0 + gate_pre * (1.0 - sig))).astype(BF16)
    d_up = (d_hidden * gate_pre * sig).astype(BF16)
    d_x = dot(d_gate, gate, 1, 1) + dot(d_up, up, 1, 1)
    out_ref[:, 1] = d_x.astype(BF16).reshape(block)
    grads = (dot(x, d_gate, 0, 0), dot(x, d_up, 0, 0), dot(dy, hidden, 0, 0))

    @pl.when(step == 0)
    def _():
        for n in range(3):
            total[n] = grads[n]

    @pl.when(step > 0)
    def _():
        for n in range(3):
            total[n] += grads[n]

    @pl.when(step == pl.num_programs(1) - 1)
    def _():
        width = gate.shape[1] // parts
        for n in range(3):
            for k in range(parts):
                gw_ref[k, n, 0] = total[n, :, k * width : (k + 1) * width].astype(BF16)


def experts_pass(gathered, weights):
    n_c, _, n_e, n_loc, slots, _ = gathered.shape
    parts, _, _, _, units = weights.shape
    take = max(1, min(n_c, 512 // (n_e * slots)))
    return pl.pallas_call(
        expert_kernel,
        grid=(n_loc, n_c // take),
        out_shape=(
            jax.ShapeDtypeStruct(gathered.shape, BF16),
            jax.ShapeDtypeStruct(weights.shape, BF16),
        ),
        in_specs=[
            pl.BlockSpec((take, 1, n_e, 1, slots, D), lambda i, j: (j, 0, 0, i, 0, 0)),
            pl.BlockSpec((take, 1, n_e, 1, slots, D), lambda i, j: (j, 1, 0, i, 0, 0)),
            pl.BlockSpec((parts, 3, 1, D, units), lambda i, j: (0, 0, i, 0, 0)),
        ],
        out_specs=(
            pl.BlockSpec((take, 2, n_e, 1, slots, D), lambda i, j: (j, 0, 0, i, 0, 0)),
            pl.BlockSpec((parts, 3, 1, D, units), lambda i, j: (0, 0, i, 0, 0)),
        ),
        scratch_shapes=[pltpu.VMEM((3, D, parts * units), F32)],
        compiler_params=pltpu.CompilerParams(
            dimension_semantics=("arbitrary", "arbitrary"), vmem_limit_bytes=VMEM_LIMIT
        ),
        name="experts_pass",
    )(gathered, gathered, weights)


def back_kernel(
    sizes,
    cfg,
    res_ref,
    h_ref,
    a2_ref,
    small_ref,
    g_ref,
    routes_ref,
    routest_ref,
    wo_ref,
    wqkv_ref,
    wsm_ref,
    vec_ref,
    mixed_ref,
    a1_ref,
    qt_ref,
    kh_ref,
    vh_ref,
    p_ref,
    x_ref,
    block_ref,
    dx_ref,
    dprev_ref,
    gqkv_ref,
    go_ref,
    gsmall_ref,
    inn,
    osum,
    outr,
    back,
    xsum,
    stage,
    dhg,
    dht_scr,
    p_scr,
    dk_acc,
    dv_acc,
    dqt,
    dqkv,
    da_in,
    da_sum,
    da_out,
    l_sem,
    s_in,
    r_in,
    s_out,
    r_out,
    s_x,
    r_x,
    s_g,
    r_g,
    p_sem,
    s_d,
    r_d,
):
    n_e, n_c, n_d = sizes
    hp, n_ff, n_all, n_loc, slots = cfg
    hc = hp * HEAD_DIM
    place = e, c, d = position()
    pairs = n_c // 2
    outer, inner = c // 2, c % 2
    rows = h_ref.shape[0]
    length = rows * n_c
    peers = context_peers(sizes, place)
    e_peers = expert_peers(sizes, place)

    in_vmem = len(stage.shape) == 5
    if in_vmem:
        take = pltpu.make_async_copy(res_ref.at[:, inner], stage, l_sem.at[0])
        take.start()
    greet(peers + e_peers)

    def load(ref, slot=0):
        if in_vmem:
            return ref[...].astype(F32)
        copy = pltpu.make_async_copy(ref, stage.at[slot], l_sem.at[0])
        copy.start()
        copy.wait()
        return stage[slot].astype(F32)

    def own_part(there, t, src):
        if in_vmem:
            return stage[there, t, src].astype(F32)
        return load(res_ref.at[there, inner, t, src])

    def store(ref, value):
        if in_vmem:
            ref[...] = value
        else:
            stage[3] = value
            copy = pltpu.make_async_copy(stage.at[3], ref, l_sem.at[0])
            copy.start()
            copy.wait()

    pieces = [(t, j) for j in [*range(1, n_e), 0] for t in range(2)]
    first_copies = {}
    for t, j in pieces:
        src = lax.rem(e + j, n_e)
        for k in [*range(1, pairs), 0]:
            n = (t * n_e + j) * pairs + k
            there = lax.rem(outer + k, pairs)
            copy = remote(
                res_ref.at[there, 1 - inner, t, src],
                inn.at[there, t, src],
                s_in.at[n],
                r_in.at[n],
                peers[0],
            )
            copy.start()
            first_copies[t, j, k] = copy
    if in_vmem:
        take.wait()
    second = {}
    for t, j in pieces:
        src = lax.rem(e + j, n_e)
        for k in range(1, pairs):
            n = (t * n_e + j) * pairs + k
            there = lax.rem(outer + k, pairs)
            first_copies[t, j, k].wait_recv()
            total = own_part(there, t, src) + load(inn.at[there, t, src], 1)
            store(osum.at[k - 1, t, src], total.astype(BF16))
            copy = remote(
                osum.at[k - 1, t, src], outr.at[k - 1, t, src], s_out.at[n], r_out.at[n], peers[k]
            )
            copy.start()
            second[t, j, k] = copy
    home = {}
    for t, j in pieces:
        src = lax.rem(e + j, n_e)
        first_copies[t, j, 0].wait_recv()
        total = own_part(outer, t, src) + load(inn.at[outer, t, src], 1)
        for k in range(1, pairs):
            second[t, j, k].wait_recv()
            total = total + load(outr.at[k - 1, t, src], 2)
        if j == 0:
            back[t, e] = total.astype(BF16)
        else:
            xsum[t, src] = total.astype(BF16)
            n = t * n_e + j
            copy = remote(
                xsum.at[t, src], back.at[t, e], s_x.at[n], r_x.at[n], e_peers[j - 1]
            )
            copy.start()
            home[t, j] = copy

    h = h_ref[...]
    a2 = a2_ref[...].astype(F32)
    g = g_ref[...]
    small = small_ref[...]
    value_one, value_two = vec_ref[2:3, :], vec_ref[3:4, :]
    tables, picks, w_pair, first, other = route_parts(
        routest_ref[...], routes_ref[...], small, n_ff, n_all, slots
    )
    copy_on, one_on, two_on = [
        [picks[k][:, n_ff + n : n_ff + n + 1] for k in range(2)] for n in (1, 2, 3)
    ]
    g_a2 = jnp.sum(g * a2, axis=1, keepdims=True)
    g_one = jnp.sum(g * value_one, axis=1, keepdims=True)
    g_two = jnp.sum(g * value_two, axis=1, keepdims=True)
    alpha = [copy_on[k] + one_on[k] * first[0] + two_on[k] * other[0] for k in range(2)]
    a_weight = alpha[0] * w_pair[0] + alpha[1] * w_pair[1]
    one_weight = one_on[0] * w_pair[0] + one_on[1] * w_pair[1]
    two_weight = two_on[0] * w_pair[0] + two_on[1] * w_pair[1]
    for copy in home.values():
        copy.wait_recv()
    returned = [back[t].reshape(n_ff * slots, D) for t in range(2)]
    block = h
    d_weight = []
    for k in range(2):
        routed = dot(tables[k], returned[0], 0, 0)
        picked = (
            routed
            + alpha[k] * a2
            + (one_on[k] * first[1]) * value_one
            + (two_on[k] * other[1]) * value_two
        )
        block = block + w_pair[k] * picked
        d_weight.append(jnp.sum(g * picked, axis=1, keepdims=True))
    block_ref[...] = block
    center = w_pair[0] * d_weight[0] + w_pair[1] * d_weight[1]
    d_logits = (
        picks[0] * (w_pair[0] * (d_weight[0] - center))
        + picks[1] * (w_pair[1] * (d_weight[1] - center))
    )
    dprev_ref[...] = d_logits
    lane = lax.broadcasted_iota(jnp.int32, (rows, LANES), 1)
    d_small = d_logits
    for base, pair, weight, g_value in (
        (n_all, first, one_weight, g_one),
        (n_all + 2, other, two_weight, g_two),
    ):
        d_pair = (weight * g_a2, weight * g_value)
        middle = pair[0] * d_pair[0] + pair[1] * d_pair[1]
        for k in range(2):
            d_small = d_small + jnp.where(lane == base + k, pair[k] * (d_pair[k] - middle), 0.0)
    d_small = d_small.astype(BF16)
    d_const_one = jnp.sum((first[1] * one_weight) * g, axis=0, keepdims=True)
    d_const_two = jnp.sum((other[1] * two_weight) * g, axis=0, keepdims=True)
    d_a2 = (
        dot(tables[0] + tables[1], returned[1], 0, 0)
        + a_weight * g
        + dot(d_small, wsm_ref[...], 1, 1)
    )
    gain_two = vec_ref[1:2, :]
    inverse_two = lax.rsqrt(jnp.mean(h * h, axis=-1, keepdims=True) + EPS)
    d_gain_two = jnp.sum(d_a2 * h * inverse_two, axis=0, keepdims=True)
    scaled = gain_two * d_a2
    d_h = (
        g
        + inverse_two * scaled
        - h * inverse_two**3 * jnp.mean(scaled * h, axis=-1, keepdims=True)
    )
    d_hb = d_h.astype(BF16)
    dhg[pl.ds(c, 1)] = d_hb[None]
    gather = ContextGather(
        sizes,
        place,
        dhg.at[c],
        lambda k: dhg.at[k],
        lambda k: s_g.at[k],
        lambda k: r_g.at[k],
    )
    gather.start()
    dx_ref[...] = d_h
    go_ref[...] = dot(mixed_ref[...].reshape(n_c * hc, rows), d_hb)[:D]
    g_small = dot(a2_ref[...], d_small, 0, 0)
    dk_acc[...] = jnp.zeros_like(dk_acc)
    dv_acc[...] = jnp.zeros_like(dv_acc)
    order = [(b, j) for b in reversed(range(n_c)) for j in range(hp)]

    def fetch(n):
        b, j = order[n]
        reach = pl.ds(0, (b + 1) * rows)
        return pltpu.make_async_copy(p_ref.at[j, b, reach], p_scr.at[n % 2, reach], p_sem.at[n % 2])

    fetch(0).start()
    gather.forward()
    gather.finish()
    wo_part = wo_ref[pl.ds(pl.multiple_of(c * hc, hc), hc), :]
    for b in range(n_c):
        dht_scr[:, b * rows : (b + 1) * rows] = dot(wo_part, dhg[b], 1, 1).astype(BF16)
    for n, (b, j) in enumerate(order):
        reach = (b + 1) * rows
        head = slice(j * HEAD_DIM, (j + 1) * HEAD_DIM)
        mine_q = slice(b * rows, reach)
        if n + 1 < len(order):
            fetch(n + 1).start()
        fetch(n).wait()
        rounded = p_scr[n % 2, :reach, :]
        prob = rounded.astype(F32)
        d_o = dht_scr[head, mine_q]
        d_prob = dot(vh_ref[j, :reach, :], d_o)
        delta = jnp.sum(prob * d_prob, axis=0, keepdims=True)
        d_scores = (prob * (d_prob - delta)).astype(BF16)
        dqt[head, mine_q] = dot(kh_ref[j, :reach, :], d_scores, 0, 0) * HEAD_DIM**-0.5
        dk_acc[j, :reach, :] += dot(d_scores, qt_ref[head, mine_q], 1, 1)
        dv_acc[j, :reach, :] += dot(rounded, d_o, 1, 1)
    dqkv[:, :hc] = dqt[...].T.astype(BF16)
    for j in range(hp):
        at = j * HEAD_DIM
        dqkv[:, hc + at : hc + at + HEAD_DIM] = dk_acc[j].astype(BF16)
        dqkv[:, 2 * hc + at : 2 * hc + at + HEAD_DIM] = dv_acc[j].astype(BF16)
    d_all = dqkv[...]
    wqkv = wqkv_ref[...]
    for b in range(n_c):
        dhg[b] = dot(d_all[b * rows : (b + 1) * rows], wqkv, 1, 1).astype(BF16)
    to_pair = []
    for k in [*range(1, pairs), 0]:
        there = lax.rem(outer + k, pairs)
        copy = remote(
            dhg.at[there * 2 + 1 - inner], da_in.at[there], s_d.at[k], r_d.at[k], peers[0]
        )
        copy.start()
        to_pair.append((k, copy))
    along = []
    for k, copy in to_pair:
        if k == 0:
            continue
        there = lax.rem(outer + k, pairs)
        copy.wait_recv()
        da_sum[k - 1] = (
            dhg[there * 2 + inner].astype(F32) + da_in[there].astype(F32)
        ).astype(BF16)
        onward = remote(
            da_sum.at[k - 1],
            da_out.at[k - 1],
            s_d.at[pairs + k - 1],
            r_d.at[pairs + k - 1],
            peers[k],
        )
        onward.start()
        along.append(onward)
    gqkv_ref[...] = dot(a1_ref[...], d_all, 0, 0)
    to_pair[-1][1].wait_recv()
    d_a1 = dhg[c].astype(F32) + da_in[outer].astype(F32)
    for k, copy in enumerate(along):
        copy.wait_recv()
        d_a1 = d_a1 + da_out[k].astype(F32)
    x = x_ref[...].astype(F32)
    gain_one = vec_ref[0:1, :]
    inverse_one = lax.rsqrt(jnp.mean(x * x, axis=-1, keepdims=True) + EPS)
    d_gain_one = jnp.sum(d_a1 * x * inverse_one, axis=0, keepdims=True)
    scaled = gain_one * d_a1
    dx_ref[...] += inverse_one * scaled - x * inverse_one**3 * jnp.mean(
        scaled * x, axis=-1, keepdims=True
    )
    spot = lax.broadcasted_iota(jnp.int32, (LANES, D), 0)
    tall = jnp.zeros((LANES, D), F32)
    for n, row in enumerate((d_const_one, d_const_two, d_gain_one, d_gain_two)):
        tall = tall + jnp.where(spot == n_all + 4 + n, row, 0.0)
    gsmall_ref[...] = g_small + tall.T
    for copy in first_copies.values():
        copy.wait_send()
    for copy in second.values():
        copy.wait_send()
    for copy in home.values():
        copy.wait_send()
    for _, copy in to_pair:
        copy.wait_send()
    for copy in along:
        copy.wait_send()


def backward(sizes, cfg, *operands):
    n_e, n_c, n_d = sizes
    hp, n_ff, n_all, n_loc, slots = cfg
    hc = hp * HEAD_DIM
    rows = operands[1].shape[0]
    length = rows * n_c
    pairs = n_c // 2
    per = n_loc * slots
    dma = pltpu.SemaphoreType.DMA
    vmem = pl.BlockSpec(memory_space=pltpu.VMEM)
    anywhere = pl.BlockSpec(memory_space=pl.ANY)
    shape = jax.ShapeDtypeStruct
    n_in = 2 * n_e * pairs
    n_more = max(1, pairs - 1)
    in_specs = [vmem] * len(operands)
    in_specs[0] = anywhere
    in_specs[16] = anywhere
    arriving = [(pairs, 2, n_e, per, D), (n_more, 2, n_e, per, D), (n_more, 2, n_e, per, D)]
    roomy = 2 * pairs * n_e * per * D <= 2**21
    held = [pltpu.VMEM(dims, BF16) for dims in arriving] if roomy else []
    extra = [] if roomy else [shape(dims, BF16) for dims in arriving]
    stage = pltpu.VMEM(arriving[0] if roomy else (4, per, D), BF16)
    return pl.pallas_call(
        functools.partial(back_kernel, sizes, cfg),
        out_shape=(
            shape((rows, D), F32),
            shape((rows, D), F32),
            shape((rows, LANES), F32),
            shape((D, 3 * hc), F32),
            shape((D, D), F32),
            shape((D, LANES), F32),
            *extra,
        ),
        in_specs=in_specs,
        out_specs=(vmem,) * 6 + (anywhere,) * len(extra),
        scratch_shapes=[
            *held,
            pltpu.VMEM((2, n_e, per, D), BF16),
            pltpu.VMEM((2, n_e, per, D), BF16),
            stage,
            pltpu.VMEM((n_c, rows, D), BF16),
            pltpu.VMEM((hc, length), BF16),
            pltpu.VMEM((2, length, rows), BF16),
            pltpu.VMEM((hp, length, HEAD_DIM), F32),
            pltpu.VMEM((hp, length, HEAD_DIM), F32),
            pltpu.VMEM((hc, length), F32),
            pltpu.VMEM((length, 3 * hc), BF16),
            pltpu.VMEM((pairs, rows, D), BF16),
            pltpu.VMEM((n_more, rows, D), BF16),
            pltpu.VMEM((n_more, rows, D), BF16),
            dma((1,)),
            dma((n_in,)),
            dma((n_in,)),
            dma((n_in,)),
            dma((n_in,)),
            dma((2 * n_e,)),
            dma((2 * n_e,)),
            dma((n_c - 1,)),
            dma((n_c - 1,)),
            dma((2,)),
            dma((n_c,)),
            dma((n_c,)),
        ],
        compiler_params=pltpu.CompilerParams(
            collective_id=2, has_side_effects=True, vmem_limit_bytes=VMEM_LIMIT
        ),
        name="backward",
    )(*operands)[:6]


def pad_to(array, axis, size):
    widths = [(0, 0)] * array.ndim
    widths[axis] = (0, size - array.shape[axis])
    return jnp.pad(array, widths)


def body(
    tokens,
    doc_ids,
    routes,
    prev_logits,
    cotangent,
    w_query,
    w_key,
    w_value,
    w_out,
    w_router,
    const_coef,
    const_value,
    norm_gains,
    expert_gate,
    expert_up,
    expert_down,
):
    sizes = n_e, n_c, n_d = tuple(lax.axis_size(axis) for axis in ALL_AXES)
    rows = tokens.shape[1]
    length = doc_ids.shape[1]
    n_loc, _, units = expert_gate.shape
    n_ff = n_loc * n_e
    n_all = w_router.shape[1]
    slots = rows // 4
    hp = -(-HEADS // n_c)
    hc = hp * HEAD_DIM
    cfg = (hp, n_ff, n_all, n_loc, slots)
    w_rows = w_query.shape[0]
    w_pad = -(-w_rows // 16) * 16
    width = -(-(3 * hc + SMALL) // LANES) * LANES

    pieces = jnp.stack([expert_gate, expert_up, expert_down]).astype(BF16)
    gathered_w = lax.all_gather(pieces, "dp", axis=0)

    small_w = jnp.concatenate([w_router, const_coef, const_value, norm_gains], axis=1).astype(BF16)
    slices = [
        pad_to(w.astype(BF16), 1, n_c * hc).reshape(w_rows, n_c, hc)
        for w in (w_query, w_key, w_value)
    ]
    slices.append(
        jnp.broadcast_to(
            pad_to(small_w, 1, width - 3 * hc)[:, None, :], (w_rows, n_c, width - 3 * hc)
        )
    )
    a_part = pad_to(jnp.concatenate(slices, axis=2).transpose(1, 0, 2), 1, w_pad)
    o_part = pad_to(w_out.astype(BF16), 0, w_pad)
    a_all, o_all, x_all = gather_first(sizes, a_part, o_part, tokens[0])
    a_all = a_all[:, :, :, :w_rows].reshape(D, width)
    wqkv = a_all[:, : 3 * hc]
    small_w = a_all[:, 3 * hc : 3 * hc + SMALL]
    wsm = pad_to(small_w, 1, LANES)
    wo = pad_to(o_all[:, :, :, :w_rows].reshape(D, D), 0, n_c * hc)
    lines = small_w[:, n_all + 4 : n_all + 8].astype(F32).T
    vec = pad_to(jnp.concatenate([lines[2:4], lines[0:2]], axis=0), 0, 8)

    documents = doc_ids[0]
    route_rows = routes[0]
    routes_t = pad_to(route_rows.T, 0, 8)
    prev = pad_to(prev_logits[0], 1, LANES)
    upstream = cotangent[0]
    (a1, q_t, k_h, v_h, mixed, h, a2, small, probs, gathered) = front(
        sizes,
        cfg,
        x_all.reshape(length, D),
        tokens[0],
        wqkv,
        wo,
        wsm,
        vec,
        documents[:, None],
        documents[None, :],
        route_rows,
        routes_t,
        prev,
        upstream,
    )
    if units % LANES:
        flat = gathered_w.transpose(1, 2, 3, 0, 4).reshape(1, 3, n_loc, D, n_d * units)
    else:
        flat = gathered_w
    results, grads = experts_pass(gathered.reshape(n_c, 2, n_e, n_loc, slots, D), flat)
    if units % LANES:
        grads = grads.reshape(3, n_loc, D, n_d, units).transpose(3, 0, 1, 2, 4)
    expert_grads = lax.psum_scatter(grads, "dp", scatter_dimension=0, tiled=False).astype(F32)

    block_rows, d_x, d_prev, g_qkv, g_o, g_small = backward(
        sizes,
        cfg,
        results.reshape(n_c // 2, 2, 2, n_e, n_loc * slots, D),
        h,
        a2,
        small,
        upstream,
        route_rows,
        routes_t,
        wo,
        wqkv,
        wsm,
        vec,
        mixed,
        a1,
        q_t,
        k_h,
        v_h,
        probs,
        tokens[0],
    )
    own = lax.psum_scatter(
        jnp.concatenate([g_o.astype(BF16), g_small.astype(BF16)], axis=1),
        ALL_AXES,
        scatter_dimension=0,
        tiled=True,
    ).astype(F32)
    blocks = (
        g_qkv.astype(BF16)
        .reshape(n_e, n_c, n_d, w_rows, 3 * hc)
        .transpose(0, 2, 1, 3, 4)
        .reshape(n_e * n_d * n_c * w_rows, 3 * hc)
    )
    mine = lax.psum_scatter(blocks, ("expert", "dp"), scatter_dimension=0, tiled=True)
    mine = lax.all_to_all(
        mine.reshape(n_c, w_rows, 3 * hc), "context", split_axis=0, concat_axis=0, tiled=True
    ).astype(F32)
    q_grad, k_grad, v_grad = [
        mine[:, :, n * hc : (n + 1) * hc].transpose(1, 0, 2).reshape(w_rows, n_c * hc)[:, :D]
        for n in range(3)
    ]
    s_own = own[:, D:]
    return (
        block_rows[None],
        d_x[None],
        d_prev[None, :, :n_all],
        q_grad,
        k_grad,
        v_grad,
        own[:, :D],
        s_own[:, :n_all],
        s_own[:, n_all : n_all + 4],
        s_own[:, n_all + 4 : n_all + 6],
        s_own[:, n_all + 6 : n_all + 8],
        expert_grads[0],
        expert_grads[1],
        expert_grads[2],
    )


def solution(mesh):
    rows = P(("expert", "dp"), "context", None)
    weights = P(ALL_AXES, None)
    units = P("expert", None, ("context", "dp"))
    return jax.shard_map(
        body,
        mesh=mesh,
        in_specs=(rows, P(("expert", "dp"), None), rows, rows, rows)
        + (weights,) * 8
        + (units,) * 3,
        out_specs=(rows,) * 3 + (weights,) * 8 + (units,) * 3,
        check_vma=False,
    )
```

time: 1560 us -> 461 us (0.30)
  waiting for transfers between devices: 901 us -> 235 us
  blocking collectives: 296 us -> 0 us
  matrix products: 194 us -> 0 us
  Pallas kernels: 0 us -> 171 us
  local copies, waits for them, and re-layouts: 71.9 us -> 24.6 us
  other arithmetic: 48 us -> 9 us
    reduce_scatter x9 -> x2, waiting for transfers between devices: 807 us -> 143 us  [the longest x1 80 us: body(): lax.psum_scatter(grads, 'dp', scatter_dimension=0, tiled=False).astype(F32)]
    all_gather x4 -> x0, blocking collectives: 256 us -> none  [the longest x1 66.8 us: body(): lax.all_gather(const_value.astype(jnp.bfloat16), ('expert', 'context', 'd...]
    dot_general x111 -> x0, matrix products: 194 us -> none  [the longest x42 56.5 us: times_transposed(): lax.dot_general(left_side, right_side, (((1,), (1,)), ((), ())), preferre...]
    pallas_call x0 -> x4, Pallas kernels: none -> 171 us  [the longest x1 68.7 us: backward(): pl.pallas_call(functools.partial(back_kernel, sizes, cfg), out_shape=(sha...]
    unnamed x18 -> x5, waiting for transfers between devices: 0.96 us -> 86.3 us
    all_gather x9 -> x1, waiting for transfers between devices: 88.8 us -> 6.18 us  [body(): gathered_w = lax.all_gather(pieces, 'dp', axis=0)]
    unnamed x1 -> x0, blocking collectives: 39.7 us -> none
    reduce_sum x24 -> x0, other arithmetic: 25.4 us -> none  [the longest x1 14.3 us: body(): d_gate_w = jnp.sum(upstream[:, None, :] * picked, axis=-1)]
  transfers between devices with their start and end apart: 22 -> 5, of which waited for: 12 -> 4; matrix products, arithmetic and copies ran while one was open for 11% -> 4% of each run, Pallas kernels for 0% -> 19%
where the time goes in v1:
time: 461 us; the launch traced here: 459 us
  waiting for transfers between devices  235 us (51%)
  Pallas kernels  171 us (37%)
  local copies, waits for them, and re-layouts  24.6 us (5%)
  between operations  14.2 us (3%)
  other arithmetic  9 us (2%)
  starting transfers between devices  5.72 us (1%)
    unnamed x5, waiting for transfers between devices  86.3 us
    reduce_scatter x1, waiting for transfers between devices, body(): lax.psum_scatter(grads, 'dp', scatter_dimension=0, tiled=False).astype(F32)  80 us
    pallas_call x1, Pallas kernels, backward(): pl.pallas_call(functools.partial(back_kernel, sizes, cfg), out_shape=(sha...  68.7 us
    reduce_scatter x1, waiting for transfers between devices, body(): lax.psum_scatter(blocks, ('expert', 'dp'), scatter_dimension=0, tiled=True)  62.6 us
    pallas_call x1, Pallas kernels, gather_first(): pl.pallas_call(functools.partial(gather_kernel, sizes), out_shape=(jax.Sh...  47.2 us
    pallas_call x1, Pallas kernels, front(): pl.pallas_call(functools.partial(front_kernel, sizes, cfg), out_shape=(sh...  42.1 us
    pallas_call x1, Pallas kernels, experts_pass(): pl.pallas_call(expert_kernel, grid=(n_loc, n_c // take), out_shape=(jax.S...  12.9 us
  transfers between devices with their start and end apart: 5, of which 4 were waited for; matrix products, arithmetic and copies ran while one was open for 4% of the time, Pallas kernels for 19%

profile of v1, /device:TPU:1, one launch (start us, length us, event | category | flops | bytes accessed | tf_op | source)
XLA Modules:
  0.0 459.5 jit_solution(12288405737133559693)
XLA Ops:
  7.2 1.2 convert_bitcast_fusion.2
  8.6 1.2 convert_bitcast_fusion
  9.9 1.2 pad_maximum_fusion.1
  13.4 0.8 copy.84.routes_ref
  14.3 1.0 copy.83.dcol_ref
  15.3 47.2 %gather_first.1 = (bf16[2,4,4,32,640]{4,3,2,1,0:T(8,128)(2,1)}, bf16[2,4,4,32,768]{4,3,2,1,0:T(8,128)(2,1)}, bf16[4,256,768]{2,1,0:T(8,128)(2,1)}) custom-call(bf16[4,32,640]{2,1,0:T(8,128)(2,1)} %pad.29.a_ref, bf16[32,768]{1,0:T(8,128)(2,1)} %pad.30.o_ref, bf16[256,768]{1,0:T(8,128)(2,1)} %bitcast.53), custom_call_target="tpu_custom_call" | custom-call | tf_op jit(solution)/shard_map/gather_first/pallas_call | solution.py:205
  62.6 1.4 slice.66
  64.2 0.9 pad.31.wsm_ref
  65.3 1.2 slice.68
  68.4 42.1 %front.1 = (bf16[1024,768]{1,0:T(8,128)(2,1)}, bf16[192,1024]{1,0:T(8,128)(2,1)}, bf16[3,1024,64]{2,1,0:T(8,128)(2,1)}, bf16[3,1024,64]{2,1,0:T(8,128)(2,1)}, bf...) custom-call(bf16[1024,768]{1,0:T(8,128)(2,1)} %bitcast.59, ...), custom_call_target="tpu_custom_call" | custom-call | tf_op jit(solution)/shard_map/front/pallas_call | solution.py:446
  110.5 6.2 %all-gather.2.cloned.1.call-done.w_ref = bf16[4,3,2,768,128]{4,3,2,1,0:T(8,128)(2,1)} async-done(((bf16[1,3,2,768,128]{4,3,2,1,0:T(8,128)(2,1)}), bf16[4,3,2,768,128]{4,3,2,1,0:T(8,128)(2,1)}) %all-gather.2.cloned.1.call-update) | async-done | bytes 4718608 | tf_op jit(solution)/shard_map/all_gather | solution.py:985
  116.7 12.9 %experts_pass.1 = (bf16[4,2,2,2,64,768]{5,4,3,2,1,0:T(8,128)(2,1)}, bf16[4,3,2,768,128]{4,3,2,1,0:T(8,128)(2,1)}) custom-call(bf16[4,2,2,2,64,768]{5,4,3,2,1,0:T(8,128)(2,1)} %bitcast.43, bf16[4,2,2,2,64,768]{5,4,3,2,1,0:T(8,128)(2,1)} %bitcast.44, bf16[4,3,2,768,128]{4,3,2,1,0:T(8,128)(2,1)} %all-gather.2.cloned.1.call-done.w_ref), custom_call_target="tpu_custom_call" | custom-call | tf_op jit(solution)/shard_map/experts_pass/pallas_call | solution.py:528
  129.6 68.7 %backward.1 = (f32[256,768]{1,0:T(8,128)}, f32[256,768]{1,0:T(8,128)}, f32[256,128]{1,0:T(8,128)}, f32[768,576]{1,0:T(8,128)}, f32[768,768]{1,0:T(8,128)}, /*index=5*/f32[768,128]{1,0:T(8,128)}) custom-call(bf16[2,2,2,2,128,768]{5,4,3,2,1,0:T(8,128)(2,1)} %bitcast.58, f32[256,768]{1,0:T(8,128)} %get-tuple-element.40.h_ref, ...), custom_call_target="tpu_custom_call" | custom-call | tf_op jit(solution)/shard_map/backward/pallas_call | solution.py:898
  198.3 1.7 convert_element_type.57
  199.9 1.1 copy.86
  201.1 1.0 copy-done.1
  202.2 1.2 pad_maximum_fusion
  205.1 62.6 %reduce-scatter.6.cloned.1.call-done = bf16[96,576]{1,0:T(8,128)(2,1)} async-done(((bf16[768,576]{1,0:T(8,128)(2,1)}), bf16[96,576]{1,0:T(8,128)(2,1)}) %reduce-scatter.6.cloned.1.call-update) | async-done | bytes 110608 | tf_op jit(solution)/shard_map/reduce_scatter | solution.py:1072
  267.6 5.6 %all-to-all-start = ((bf16[4,24,576]{2,1,0:T(8,128)(2,1)}), bf16[4,24,576]{2,1,0:T(8,128)(2,1)S(1)}, u32[]{:S(2)}, u32[]{:S(2)}) async-start(bf16[4,24,576]{2,1,0:T(8,128)(2,1)} %bitcast.63), calls=%async_computation.1 | async-start | bytes 245760 | tf_op jit(solution)/shard_map/all_to_all | solution.py:1073
  273.2 85.8 %reduce-scatter.10.cloned.1.call-done = bf16[24,896]{1,0:T(8,128)(2,1)} async-done(((bf16[768,896]{1,0:T(8,128)(2,1)}), bf16[24,896]{1,0:T(8,128)(2,1)}) %reduce-scatter.10.cloned.1.call-update) | async-done | bytes 43024
  359.0 0.8 fusion
  359.8 0.8 slice.95
  361.3 0.7 slice.94
  363.9 1.4 slice.93
  365.5 0.7 reshape.139
  366.2 0.7 reshape.138
  367.0 0.7 reshape.137
  367.8 80.0 %reduce-scatter.8.cloned.1.call-done = bf16[1,3,2,768,128]{4,3,2,1,0:T(8,128)(2,1)} async-done(((bf16[4,3,2,768,128]{4,3,2,1,0:T(8,128)(2,1)}), bf16[1,3,2,768,128]{4,3,2,1,0:T(8,128)(2,1)}) %reduce-scatter.8.cloned.1.call-update) | async-done | bytes 1179664 | tf_op jit(solution)/shard_map/reduce_scatter | solution.py:1036
  447.7 1.4 convert_element_type.62
  449.2 1.4 slice_bitcast_fusion
  450.7 0.9 copy.100
  452.1 0.9 copy.101
  (88 shorter events, 9.9 us)
Async XLA Ops:
  7.2 1.4 copy-start.5
  7.2 109.5 %all-gather.2.cloned.1.call-start = ((), (), s32[]{:S(2)}) async-start(), calls=%async_computation.4 | async-start | bytes 5898240 | tf_op jit(solution)/shard_map/all_gather | solution.py:985
  9.8 1.4 copy-start.17
  9.8 1.4 copy-start.18
  9.8 1.4 copy-start.16
  9.8 1.4 copy-start.15
  9.8 1.5 copy-start.8
  9.8 1.6 copy-start.9
  9.9 1.8 copy-start.10
  11.1 0.9 copy-start.11
  11.1 2.3 copy-start.13
  11.1 3.1 copy-start.14
  11.1 3.2 copy-start.12
  11.1 256.5 %reduce-scatter.6.cloned.1.call-start = ((), (), s32[]{:S(2)}) async-start(), calls=%async_computation.5 | async-start | bytes 1105920 | tf_op jit(solution)/shard_map/reduce_scatter | solution.py:1072
  62.6 2.7 copy-start.2
  64.0 2.5 copy-start
  199.9 1.2 copy-start.6
  199.9 2.2 copy-start.1
  201.0 158.0 %reduce-scatter.10.cloned.1.call-start = ((), (), s32[]{:S(2)}) async-start(), calls=%async_computation.7 | async-start | bytes 1419264
  203.4 244.3 %reduce-scatter.8.cloned.1.call-start = ((), (), s32[]{:S(2)}) async-start(), calls=%async_computation.6 | async-start | bytes 5898240 | tf_op jit(solution)/shard_map/reduce_scatter | solution.py:1036
  203.5 0.9 copy-start.7
  267.6 97.7 %all-to-all-start = ((bf16[4,24,576]{2,1,0:T(8,128)(2,1)}), bf16[4,24,576]{2,1,0:T(8,128)(2,1)S(1)}, u32[]{:S(2)}, u32[]{:S(2)}) async-start(bf16[4,24,576]{2,1,0:T(8,128)(2,1)} %bitcast.63), calls=%async_computation.1 | async-start | bytes 245760 | tf_op jit(solution)/shard_map/all_to_all | solution.py:1073
  449.2 1.5 copy-start.4
  450.6 1.4 copy-start.3
Sparse Core Ops, SparseCore 0:
  11.2 105.4 all-gather.1
  201.1 66.4 reduce-scatter.5
  273.8 85.1 reduce-scatter.9
  361.1 86.5 reduce-scatter.7

commit v2 on v1

--- a/solution.py
+++ b/solution.py
@@ -13,7 +13,7 @@
 EPS = 1e-06
 SMALL = 64
 LANES = 128
-VMEM_LIMIT = 60 * 2**20
+VMEM_LIMIT = 63 * 2**20
 MESH = pl.DeviceIdType.MESH
 F32 = jnp.float32
 BF16 = jnp.bfloat16
@@ -61,6 +61,27 @@
 def expert_peers(sizes, place):
     e, c, d = place
     return [(lax.rem(e + j, sizes[0]), c, d) for j in range(1, sizes[0])]
+
+
+class Courier:
+    def __init__(self, send, recv):
+        self.send, self.recv = send, recv
+        self.copies = []
+
+    def carry(self, src, dst, device):
+        n = len(self.copies)
+        copy = remote(src, dst, self.send.at[n], self.recv.at[n], device)
+        copy.start()
+        self.copies.append(copy)
+        return copy
+
+    def finish(self):
+        for copy in self.copies:
+            copy.wait_send()
+
+
+def up_to(count, step):
+    return -(-count // step) * step
 
 
 class ContextGather:
@@ -569,13 +590,19 @@
     kh_ref,
     vh_ref,
     p_ref,
-    x_ref,
+    xg_ref,
+    gw_ref,
     block_ref,
     dx_ref,
     dprev_ref,
-    gqkv_ref,
+    gq_ref,
+    gk_ref,
+    gv_ref,
     go_ref,
     gsmall_ref,
+    egate_ref,
+    eup_ref,
+    edown_ref,
     inn,
     osum,
     outr,
@@ -592,6 +619,23 @@
     da_in,
     da_sum,
     da_out,
+    x_scr,
+    ew_own,
+    ew_in,
+    t_send,
+    t_recv,
+    t_z,
+    t_zr,
+    t_c,
+    t_cr,
+    o_own,
+    o_in,
+    o_sum,
+    o_out,
+    o_x,
+    o_xr,
+    o_z,
+    o_zr,
     l_sem,
     s_in,
     r_in,
@@ -604,6 +648,12 @@
     p_sem,
     s_d,
     r_d,
+    s_w,
+    r_w,
+    s_t,
+    r_t,
+    s_q,
+    r_q,
 ):
     n_e, n_c, n_d = sizes
     hp, n_ff, n_all, n_loc, slots = cfg
@@ -612,6 +662,10 @@
     pairs = n_c // 2
     outer, inner = c // 2, c % 2
     rows = h_ref.shape[0]
+    w_rows = go_ref.shape[0]
+    shift = 3 * hc % LANES
+    chunks = up_to(3 * hc + SMALL, LANES) // LANES
+    d_peers = [(e, c, lax.rem(d + k, n_d)) for k in range(1, n_d)]
     length = rows * n_c
     peers = context_peers(sizes, place)
     e_peers = expert_peers(sizes, place)
@@ -620,7 +674,87 @@
     if in_vmem:
         take = pltpu.make_async_copy(res_ref.at[:, inner], stage, l_sem.at[0])
         take.start()
-    greet(peers + e_peers)
+    bring = pltpu.make_async_copy(gw_ref, ew_own, l_sem.at[1])
+    bring.start()
+
+    def fetch_x(b, slot):
+        return pltpu.make_async_copy(xg_ref.at[b], x_scr.at[slot], l_sem.at[2 + slot])
+
+    fetch_x(c, 2).start()
+    fetch_x(0, 0).start()
+    greet(peers + e_peers + d_peers)
+
+    def expert_send(way, step, src):
+        there = d + 1 if way == 0 else d - 1
+        return remote(
+            src,
+            ew_in.at[way, step - 1],
+            s_w.at[way, step - 1],
+            r_w.at[way, step - 1],
+            (e, c, there),
+        )
+
+    def expert_place(way):
+        return d if way == 0 else n_d - 1 - d
+
+    def add_own(way, step, part):
+        size = ew_own.shape[1]
+        tile = size // 8 if size % 128 == 0 else size
+
+        def one(n, carry):
+            at = pl.ds(pl.multiple_of(n * tile, tile), tile)
+            total = ew_in[way, step - 1, at, :].astype(F32) + ew_own[part, at, :].astype(F32)
+            ew_in[way, step - 1, at, :] = total.astype(BF16)
+            return carry
+
+        lax.fori_loop(0, size // tile, one, 0)
+
+    def expert_step(step):
+        for way in range(2):
+            at = expert_place(way)
+            far = n_d + at - step
+            part = far if way == 0 else n_d - 1 - far
+
+            @pl.when(at == 0)
+            def _():
+                expert_send(way, step, ew_own.at[part]).start()
+
+            if step > 1:
+
+                @pl.when((at > 0) & (at < step))
+                def _():
+                    src = ew_in.at[way, step - 2]
+                    expert_send(way, step - 1, src).wait_recv()
+                    add_own(way, step - 1, part)
+                    expert_send(way, step, src).start()
+
+    def expert_end():
+        last = n_d - 1
+        for way in range(2):
+
+            @pl.when(expert_place(way) > 0)
+            def _():
+                expert_send(way, last, ew_own.at[0]).wait_recv()
+
+        size = ew_own.shape[1] // 3
+        for n, ref in enumerate((egate_ref, eup_ref, edown_ref)):
+            at = pl.ds(n * size, size)
+            ref[...] = ew_own[d, at, :].astype(F32)
+            for way in range(2):
+
+                @pl.when(expert_place(way) > 0)
+                def _():
+                    ref[...] += ew_in[way, last - 1, at, :].astype(F32)
+
+        for way in range(2):
+            for step in range(1, n_d):
+
+                @pl.when(expert_place(way) < step)
+                def _():
+                    expert_send(way, step, ew_own.at[0]).wait_send()
+
+    bring.wait()
+    expert_step(1)
 
     def load(ref, slot=0):
         if in_vmem:
@@ -734,7 +868,7 @@
         picks[0] * (w_pair[0] * (d_weight[0] - center))
         + picks[1] * (w_pair[1] * (d_weight[1] - center))
     )
-    dprev_ref[...] = d_logits
+    dprev_ref[...] = d_logits[:, :n_all]
     lane = lax.broadcasted_iota(jnp.int32, (rows, LANES), 1)
     d_small = d_logits
     for base, pair, weight, g_value in (
@@ -774,7 +908,70 @@
     )
     gather.start()
     dx_ref[...] = d_h
-    go_ref[...] = dot(mixed_ref[...].reshape(n_c * hc, rows), d_hb)[:D]
+    if n_d > 2:
+        expert_step(2)
+    g_o = dot(mixed_ref[...].reshape(n_c * hc, rows), d_hb)
+    run = n_d * w_rows
+    for b in range(n_c):
+        for k in range(n_e):
+            o_own[b, k, :run, :] = g_o[(k * n_c + b) * run : (k * n_c + b + 1) * run].astype(BF16)
+    parcel = Courier(s_q, r_q)
+    o_pair = {}
+    for k in [*range(1, pairs), 0]:
+        there = lax.rem(outer + k, pairs)
+        o_pair[k] = parcel.carry(
+            o_own.at[there * 2 + 1 - inner], o_in.at[there], peers[0]
+        )
+    o_state = {}
+
+    def o_outer():
+        o_state["outer"] = []
+        for k in range(1, pairs):
+            there = lax.rem(outer + k, pairs)
+            o_pair[k].wait_recv()
+            o_sum[k - 1] = (
+                o_own[there * 2 + inner].astype(F32) + o_in[there].astype(F32)
+            ).astype(BF16)
+            o_state["outer"].append(
+                parcel.carry(o_sum.at[k - 1], o_out.at[k - 1], peers[k])
+            )
+
+    def o_across():
+        o_pair[0].wait_recv()
+        total = o_own[c].astype(F32) + o_in[outer].astype(F32)
+        for k, copy in enumerate(o_state["outer"]):
+            copy.wait_recv()
+            total = total + o_out[k].astype(F32)
+        o_x[...] = total.astype(BF16)
+        o_state["across"] = [
+            parcel.carry(o_x.at[lax.rem(e + j, n_e)], o_xr.at[j - 1], e_peers[j - 1])
+            for j in range(1, n_e)
+        ]
+
+    def o_along():
+        total = o_x[e].astype(F32)
+        for j, copy in enumerate(o_state["across"]):
+            copy.wait_recv()
+            total = total + o_xr[j].astype(F32)
+        for k in range(n_d):
+            o_z[k, :w_rows, :] = total[k * w_rows : (k + 1) * w_rows].astype(BF16)
+        o_state["along"] = [
+            parcel.carry(o_z.at[lax.rem(d + k, n_d)], o_zr.at[k - 1], d_peers[k - 1])
+            for k in range(1, n_d)
+        ]
+
+    def o_end():
+        total = o_z[d].astype(F32)
+        for k, copy in enumerate(o_state["along"]):
+            copy.wait_recv()
+            total = total + o_zr[k].astype(F32)
+        go_ref[...] = total[:w_rows]
+        parcel.finish()
+
+    if shift:
+        d_small = jnp.concatenate(
+            [jnp.zeros((rows, shift), BF16), d_small[:, : LANES - shift]], axis=1
+        )
     g_small = dot(a2_ref[...], d_small, 0, 0)
     dk_acc[...] = jnp.zeros_like(dk_acc)
     dv_acc[...] = jnp.zeros_like(dv_acc)
@@ -788,6 +985,7 @@
     fetch(0).start()
     gather.forward()
     gather.finish()
+    o_outer()
     wo_part = wo_ref[pl.ds(pl.multiple_of(c * hc, hc), hc), :]
     for b in range(n_c):
         dht_scr[:, b * rows : (b + 1) * rows] = dot(wo_part, dhg[b], 1, 1).astype(BF16)
@@ -795,6 +993,10 @@
         reach = (b + 1) * rows
         head = slice(j * HEAD_DIM, (j + 1) * HEAD_DIM)
         mine_q = slice(b * rows, reach)
+        if n == len(order) // 4:
+            o_across()
+        if n == len(order) // 2:
+            o_along()
         if n + 1 < len(order):
             fetch(n + 1).start()
         fetch(n).wait()
@@ -812,10 +1014,37 @@
         at = j * HEAD_DIM
         dqkv[:, hc + at : hc + at + HEAD_DIM] = dk_acc[j].astype(BF16)
         dqkv[:, 2 * hc + at : 2 * hc + at + HEAD_DIM] = dv_acc[j].astype(BF16)
+    dqkv[:, 3 * hc :] = jnp.zeros((length, dqkv.shape[1] - 3 * hc), BF16)
     d_all = dqkv[...]
+    bag = Courier(s_t, r_t)
+    across = {}
+    g_all = dot(a1_ref[...], d_all, 0, 0)
+    half = D // n_e
+
+    def send_chunk(k, value):
+        for n in range(n_e):
+            t_send[k, n] = value[n * half : (n + 1) * half].astype(BF16)
+        across[k] = [
+            bag.carry(t_send.at[k, lax.rem(e + j, n_e)], t_recv.at[k, j - 1], e_peers[j - 1])
+            for j in range(1, n_e)
+        ]
+
+    for k in range(chunks - 1):
+        send_chunk(k, g_all[:, k * LANES : (k + 1) * LANES])
+    for step in range(3, n_d):
+        expert_step(step)
     wqkv = wqkv_ref[...]
+    gain_one = vec_ref[0:1, :]
+    d_gain_one = jnp.zeros((1, D), F32)
     for b in range(n_c):
-        dhg[b] = dot(d_all[b * rows : (b + 1) * rows], wqkv, 1, 1).astype(BF16)
+        part = dot(d_all[b * rows : (b + 1) * rows, : 3 * hc], wqkv, 1, 1)
+        dhg[b] = part.astype(BF16)
+        if b + 1 < n_c:
+            fetch_x(b + 1, (b + 1) % 2).start()
+        fetch_x(b, b % 2).wait()
+        x = x_scr[b % 2].astype(F32)
+        inverse = lax.rsqrt(jnp.mean(x * x, axis=-1, keepdims=True) + EPS)
+        d_gain_one = d_gain_one + jnp.sum(part * x * inverse, axis=0, keepdims=True)
     to_pair = []
     for k in [*range(1, pairs), 0]:
         there = lax.rem(outer + k, pairs)
@@ -824,6 +1053,11 @@
         )
         copy.start()
         to_pair.append((k, copy))
+    spot = lax.broadcasted_iota(jnp.int32, (LANES, D), 0)
+    tall = jnp.zeros((LANES, D), F32)
+    for n, row in enumerate((d_const_one, d_const_two, d_gain_one, d_gain_two)):
+        tall = tall + jnp.where(spot == shift + n_all + 4 + n, row, 0.0)
+    send_chunk(chunks - 1, g_all[:, (chunks - 1) * LANES :] + g_small + tall.T)
     along = []
     for k, copy in to_pair:
         if k == 0:
@@ -842,25 +1076,62 @@
         )
         onward.start()
         along.append(onward)
-    gqkv_ref[...] = dot(a1_ref[...], d_all, 0, 0)
+    down = {}
+    for k in range(chunks):
+        total = t_send[k, e].astype(F32)
+        for j, copy in enumerate(across[k]):
+            copy.wait_recv()
+            total = total + t_recv[k, j].astype(F32)
+        for n in range(n_d):
+            t_z[k, n, : n_c * w_rows, :] = jnp.concatenate(
+                [
+                    total[(b * n_d + n) * w_rows : (b * n_d + n + 1) * w_rows]
+                    for b in range(n_c)
+                ],
+                axis=0,
+            ).astype(BF16)
+        down[k] = [
+            bag.carry(t_z.at[k, lax.rem(d + n, n_d)], t_zr.at[k, n - 1], d_peers[n - 1])
+            for n in range(1, n_d)
+        ]
+    o_end()
     to_pair[-1][1].wait_recv()
     d_a1 = dhg[c].astype(F32) + da_in[outer].astype(F32)
     for k, copy in enumerate(along):
         copy.wait_recv()
         d_a1 = d_a1 + da_out[k].astype(F32)
-    x = x_ref[...].astype(F32)
-    gain_one = vec_ref[0:1, :]
+    fetch_x(c, 2).wait()
+    x = x_scr[2].astype(F32)
     inverse_one = lax.rsqrt(jnp.mean(x * x, axis=-1, keepdims=True) + EPS)
-    d_gain_one = jnp.sum(d_a1 * x * inverse_one, axis=0, keepdims=True)
     scaled = gain_one * d_a1
     dx_ref[...] += inverse_one * scaled - x * inverse_one**3 * jnp.mean(
         scaled * x, axis=-1, keepdims=True
     )
-    spot = lax.broadcasted_iota(jnp.int32, (LANES, D), 0)
-    tall = jnp.zeros((LANES, D), F32)
-    for n, row in enumerate((d_const_one, d_const_two, d_gain_one, d_gain_two)):
-        tall = tall + jnp.where(spot == n_all + 4 + n, row, 0.0)
-    gsmall_ref[...] = g_small + tall.T
+    for k in range(chunks):
+        total = t_z[k, d].astype(F32)
+        for n, copy in enumerate(down[k]):
+            copy.wait_recv()
+            total = total + t_zr[k, n].astype(F32)
+        for b in range(n_c):
+            t_c[b, k, :w_rows, :] = total[b * w_rows : (b + 1) * w_rows]
+    t_cr[pl.ds(c, 1)] = t_c[pl.ds(c, 1)]
+    turned = [
+        bag.carry(t_c.at[lax.rem(c + k, n_c)], t_cr.at[c], (e, lax.rem(c + k, n_c), d))
+        for k in range(1, n_c)
+    ]
+    expert_end()
+    for copy in turned:
+        copy.wait_recv()
+    s_total = jnp.zeros((w_rows, SMALL), F32)
+    for b in range(n_c):
+        line = jnp.concatenate([t_cr[b, k] for k in range(chunks)], axis=1)[:w_rows]
+        for n, ref in enumerate((gq_ref, gk_ref, gv_ref)):
+            width = min(hc, D - b * hc)
+            if width > 0:
+                ref[:, b * hc : b * hc + width] = line[:, n * hc : n * hc + width]
+        s_total = s_total + line[:, 3 * hc : 3 * hc + SMALL]
+    gsmall_ref[...] = s_total
+    bag.finish()
     for copy in first_copies.values():
         copy.wait_send()
     for copy in second.values():
@@ -886,10 +1157,19 @@
     anywhere = pl.BlockSpec(memory_space=pl.ANY)
     shape = jax.ShapeDtypeStruct
     n_in = 2 * n_e * pairs
+    part = operands[18].shape[1]
+    w_rows = D // (n_e * n_c * n_d)
+    chunks = up_to(3 * hc + SMALL, LANES) // LANES
+    run = up_to(n_d * w_rows, 16)
+    turn = up_to(n_c * w_rows, 16)
+    few = up_to(w_rows, 16)
+    few_wide = up_to(w_rows, 8)
+    bags = chunks * (n_e - 1 + n_d - 1) + n_c - 1
+    parcels = 2 * pairs - 1 + n_e - 1 + n_d - 1
     n_more = max(1, pairs - 1)
     in_specs = [vmem] * len(operands)
     in_specs[0] = anywhere
-    in_specs[16] = anywhere
+    in_specs[16] = in_specs[17] = in_specs[18] = anywhere
     arriving = [(pairs, 2, n_e, per, D), (n_more, 2, n_e, per, D), (n_more, 2, n_e, per, D)]
     roomy = 2 * pairs * n_e * per * D <= 2**21
     held = [pltpu.VMEM(dims, BF16) for dims in arriving] if roomy else []
@@ -900,14 +1180,14 @@
         out_shape=(
             shape((rows, D), F32),
             shape((rows, D), F32),
-            shape((rows, LANES), F32),
-            shape((D, 3 * hc), F32),
-            shape((D, D), F32),
-            shape((D, LANES), F32),
+            shape((rows, n_all), F32),
+            *[shape((w_rows, D), F32)] * 4,
+            shape((w_rows, SMALL), F32),
+            *[shape((part // 3, LANES), F32)] * 3,
             *extra,
         ),
         in_specs=in_specs,
-        out_specs=(vmem,) * 6 + (anywhere,) * len(extra),
+        out_specs=(vmem,) * 11 + (anywhere,) * len(extra),
         scratch_shapes=[
             *held,
             pltpu.VMEM((2, n_e, per, D), BF16),
@@ -919,11 +1199,28 @@
             pltpu.VMEM((hp, length, HEAD_DIM), F32),
             pltpu.VMEM((hp, length, HEAD_DIM), F32),
             pltpu.VMEM((hc, length), F32),
-            pltpu.VMEM((length, 3 * hc), BF16),
+            pltpu.VMEM((length, chunks * LANES), BF16),
             pltpu.VMEM((pairs, rows, D), BF16),
             pltpu.VMEM((n_more, rows, D), BF16),
             pltpu.VMEM((n_more, rows, D), BF16),
-            dma((1,)),
+            pltpu.VMEM((3, rows, D), BF16),
+            pltpu.VMEM((n_d, part, LANES), BF16),
+            pltpu.VMEM((2, n_d - 1, part, LANES), BF16),
+            pltpu.VMEM((chunks, n_e, D // n_e, LANES), BF16),
+            pltpu.VMEM((chunks, n_e - 1, D // n_e, LANES), BF16),
+            pltpu.VMEM((chunks, n_d, turn, LANES), BF16),
+            pltpu.VMEM((chunks, n_d - 1, turn, LANES), BF16),
+            pltpu.VMEM((n_c, chunks, few_wide, LANES), F32),
+            pltpu.VMEM((n_c, chunks, few_wide, LANES), F32),
+            pltpu.VMEM((n_c, n_e, run, D), BF16),
+            pltpu.VMEM((pairs, n_e, run, D), BF16),
+            pltpu.VMEM((n_more, n_e, run, D), BF16),
+            pltpu.VMEM((n_more, n_e, run, D), BF16),
+            pltpu.VMEM((n_e, run, D), BF16),
+            pltpu.VMEM((n_e - 1, run, D), BF16),
+            pltpu.VMEM((n_d, few, D), BF16),
+            pltpu.VMEM((n_d - 1, few, D), BF16),
+            dma((5,)),
             dma((n_in,)),
             dma((n_in,)),
             dma((n_in,)),
@@ -935,12 +1232,18 @@
             dma((2,)),
             dma((n_c,)),
             dma((n_c,)),
+            dma((2, n_d - 1)),
+            dma((2, n_d - 1)),
+            dma((bags,)),
+            dma((bags,)),
+            dma((parcels,)),
+            dma((parcels,)),
         ],
         compiler_params=pltpu.CompilerParams(
             collective_id=2, has_side_effects=True, vmem_limit_bytes=VMEM_LIMIT
         ),
         name="backward",
-    )(*operands)[:6]
+    )(*operands)[:11]
 
 
 def pad_to(array, axis, size):
@@ -1033,9 +1336,7 @@
     results, grads = experts_pass(gathered.reshape(n_c, 2, n_e, n_loc, slots, D), flat)
     if units % LANES:
         grads = grads.reshape(3, n_loc, D, n_d, units).transpose(3, 0, 1, 2, 4)
-    expert_grads = lax.psum_scatter(grads, "dp", scatter_dimension=0, tiled=False).astype(F32)
-
-    block_rows, d_x, d_prev, g_qkv, g_o, g_small = backward(
+    (block_rows, d_x, d_prev, q_grad, k_grad, v_grad, o_grad, s_grad, *expert_grads) = backward(
         sizes,
         cfg,
         results.reshape(n_c // 2, 2, 2, n_e, n_loc * slots, D),
@@ -1055,44 +1356,22 @@
         k_h,
         v_h,
         probs,
-        tokens[0],
-    )
-    own = lax.psum_scatter(
-        jnp.concatenate([g_o.astype(BF16), g_small.astype(BF16)], axis=1),
-        ALL_AXES,
-        scatter_dimension=0,
-        tiled=True,
-    ).astype(F32)
-    blocks = (
-        g_qkv.astype(BF16)
-        .reshape(n_e, n_c, n_d, w_rows, 3 * hc)
-        .transpose(0, 2, 1, 3, 4)
-        .reshape(n_e * n_d * n_c * w_rows, 3 * hc)
-    )
-    mine = lax.psum_scatter(blocks, ("expert", "dp"), scatter_dimension=0, tiled=True)
-    mine = lax.all_to_all(
-        mine.reshape(n_c, w_rows, 3 * hc), "context", split_axis=0, concat_axis=0, tiled=True
-    ).astype(F32)
-    q_grad, k_grad, v_grad = [
-        mine[:, :, n * hc : (n + 1) * hc].transpose(1, 0, 2).reshape(w_rows, n_c * hc)[:, :D]
-        for n in range(3)
-    ]
-    s_own = own[:, D:]
+        x_all,
+        grads.reshape(n_d, 3 * n_loc * D * units // LANES, LANES),
+    )
     return (
         block_rows[None],
         d_x[None],
-        d_prev[None, :, :n_all],
+        d_prev[None],
         q_grad,
         k_grad,
         v_grad,
-        own[:, :D],
-        s_own[:, :n_all],
-        s_own[:, n_all : n_all + 4],
-        s_own[:, n_all + 4 : n_all + 6],
-        s_own[:, n_all + 6 : n_all + 8],
-        expert_grads[0],
-        expert_grads[1],
-        expert_grads[2],
+        o_grad,
+        s_grad[:, :n_all],
+        s_grad[:, n_all : n_all + 4],
+        s_grad[:, n_all + 4 : n_all + 6],
+        s_grad[:, n_all + 6 : n_all + 8],
+        *[part.reshape(n_loc, D, units) for part in expert_grads],
     )
 
 

time: 461 us -> 267 us (0.58)
  waiting for transfers between devices: 235 us -> 6.24 us
  Pallas kernels: 171 us -> 217 us
  starting transfers between devices: 5.72 us -> 0.04 us
    reduce_scatter x2 -> x0, waiting for transfers between devices: 143 us -> none  [the longest x1 80 us: body(): lax.psum_scatter(grads, 'dp', scatter_dimension=0, tiled=False).astype(F32)]
    unnamed x5 -> x1, waiting for transfers between devices: 86.3 us -> 0.02 us
    pallas_call x1, Pallas kernels: 68.7 us -> 115 us  [backward(): pl.pallas_call(functools.partial(back_kernel, sizes, cfg), out_shape=(sha...]
    unnamed x48 -> x61, local copies, waits for them, and re-layouts: 7.56 us -> 13.8 us
    all_to_all x1 -> x0, starting transfers between devices: 5.56 us -> none  [body(): lax.all_to_all(mine.reshape(n_c, w_rows, 3 * hc), 'context', split_axis=0...]
  transfers between devices with their start and end apart: 5 -> 1, of which waited for: 4 -> 1; matrix products, arithmetic and copies ran while one was open for 4% -> 4% of each run, Pallas kernels for 19% -> 34%
where the time goes in v2:
time: 267 us; the launch traced here: 266 us
  Pallas kernels  217 us (81%)
  local copies, waits for them, and re-layouts  23.8 us (9%)
  between operations  14.4 us (5%)
  waiting for transfers between devices  6.24 us (2%)
  other arithmetic  4.5 us (2%)
    pallas_call x1, Pallas kernels, backward(): pl.pallas_call(functools.partial(back_kernel, sizes, cfg), out_shape=(sha...  115 us
    pallas_call x1, Pallas kernels, gather_first(): pl.pallas_call(functools.partial(gather_kernel, sizes), out_shape=(jax.Sh...  47.2 us
    pallas_call x1, Pallas kernels, front(): pl.pallas_call(functools.partial(front_kernel, sizes, cfg), out_shape=(sh...  42.1 us
    unnamed x61, local copies, waits for them, and re-layouts  13.8 us
    pallas_call x1, Pallas kernels, experts_pass(): pl.pallas_call(expert_kernel, grid=(n_loc, n_c // take), out_shape=(jax.S...  12.8 us
    all_gather x1, waiting for transfers between devices, body(): gathered_w = lax.all_gather(pieces, 'dp', axis=0)  6.22 us
  transfers between devices with their start and end apart: 1, of which 1 were waited for; matrix products, arithmetic and copies ran while one was open for 4% of the time, Pallas kernels for 34%

profile of v2, /device:TPU:1, one launch (start us, length us, event | category | flops | bytes accessed | tf_op | source)
XLA Modules:
  0.0 266.0 jit_solution(772571295245562288)
XLA Ops:
  7.2 1.2 convert_bitcast_fusion.2
  8.6 1.2 convert_bitcast_fusion
  9.9 1.1 pad_maximum_fusion
  11.9 0.6 pad.30.o_ref
  12.6 0.7 pad.29.a_ref
  13.3 0.8 copy.65.routes_ref
  14.3 1.0 copy.64.dcol_ref
  15.3 47.2 %gather_first.1 = (bf16[2,4,4,32,640]{4,3,2,1,0:T(8,128)(2,1)}, bf16[2,4,4,32,768]{4,3,2,1,0:T(8,128)(2,1)}, bf16[4,256,768]{2,1,0:T(8,128)(2,1)}) custom-call(bf16[4,32,640]{2,1,0:T(8,128)(2,1)} %pad.29.a_ref, bf16[32,768]{1,0:T(8,128)(2,1)} %pad.30.o_ref, bf16[256,768]{1,0:T(8,128)(2,1)} %bitcast.43), custom_call_target="tpu_custom_call" | custom-call | tf_op jit(solution)/shard_map/gather_first/pallas_call | solution.py:226
  62.5 1.4 slice.34
  64.1 0.9 pad.31.wsm_ref
  65.2 1.2 slice.36
  67.0 0.7 pad.34.prev_ref
  68.3 42.1 %front.1 = (bf16[1024,768]{1,0:T(8,128)(2,1)}, bf16[192,1024]{1,0:T(8,128)(2,1)}, bf16[3,1024,64]{2,1,0:T(8,128)(2,1)}, bf16[3,1024,64]{2,1,0:T(8,128)(2,1)}, bf...) custom-call(bf16[1024,768]{1,0:T(8,128)(2,1)} %bitcast.38, ...), custom_call_target="tpu_custom_call" | custom-call | tf_op jit(solution)/shard_map/front/pallas_call | solution.py:467
  110.4 6.2 %all-gather.2.cloned.1.call-done.w_ref = bf16[4,3,2,768,128]{4,3,2,1,0:T(8,128)(2,1)} async-done(((bf16[1,3,2,768,128]{4,3,2,1,0:T(8,128)(2,1)}), bf16[4,3,2,768,128]{4,3,2,1,0:T(8,128)(2,1)}) %all-gather.2.cloned.1.call-update) | async-done | bytes 4718608 | tf_op jit(solution)/shard_map/all_gather | solution.py:1288
  116.6 12.8 %experts_pass.1 = (bf16[4,2,2,2,64,768]{5,4,3,2,1,0:T(8,128)(2,1)}, bf16[4,3,2,768,128]{4,3,2,1,0:T(8,128)(2,1)}) custom-call(bf16[4,2,2,2,64,768]{5,4,3,2,1,0:T(8,128)(2,1)} %bitcast.30, bf16[4,2,2,2,64,768]{5,4,3,2,1,0:T(8,128)(2,1)} %bitcast.31, bf16[4,3,2,768,128]{4,3,2,1,0:T(8,128)(2,1)} %all-gather.2.cloned.1.call-done.w_ref), custom_call_target="tpu_custom_call" | custom-call | tf_op jit(solution)/shard_map/experts_pass/pallas_call | solution.py:549
  129.5 114.9 %backward.1 = (f32[256,768]{1,0:T(8,128)}, f32[256,768]{1,0:T(8,128)}, f32[256,8]{1,0:T(8,128)}, f32[24,768]{1,0:T(8,128)}, f32[24,768]{1,0:T(8,128)}, /*index=5...) custom-call(bf16[2,2,2,2,128,768]{5,4,3,2,1,0:T(8,128)(2,1)} %bitcas, ...), custom_call_target="tpu_custom_call" | custom-call | tf_op jit(solution)/shard_map/backward/pallas_call | solution.py:1178
  244.4 0.9 slice.42
  245.2 0.9 fusion
  246.1 1.4 copy.68
  247.4 1.6 copy.67
  249.0 0.7 copy.69
  249.7 0.6 copy.71
  250.3 0.6 copy.70
  251.0 2.2 copy.84
  253.1 0.9 copy.85
  254.0 0.6 copy.86
  254.6 0.6 copy.87
  255.3 0.6 copy.88
  255.9 0.6 copy.89
  256.5 0.9 copy.90
  257.4 0.9 copy.91
  258.3 0.9 copy.92
  (72 shorter events, 2.7 us)
Async XLA Ops:
  7.2 1.4 copy-start.6
  7.2 109.5 %all-gather.2.cloned.1.call-start = ((), (), s32[]{:S(2)}) async-start(), calls=%async_computation | async-start | bytes 5898240 | tf_op jit(solution)/shard_map/all_gather | solution.py:1288
  9.8 1.3 copy-start.20
  9.8 1.3 copy-start.21
  9.8 1.3 copy-start.19
  9.8 1.3 copy-start.18
  9.8 1.4 copy-start.7
  9.8 1.5 copy-start.8
  9.9 1.7 copy-start.9
  11.0 0.9 copy-start.10
  11.0 2.3 copy-start.16
  11.0 3.1 %copy-start.17 = (f32[1,256,8]{1,2,0:T(8,128)S(1)}, f32[1,256,8]{1,2,0:T(8,128)}, u32[]{:S(2)}) copy-start(f32[1,256,8]{1,2,0:T(8,128)} %param.19) | copy-start | bytes 24580
  11.0 3.2 %copy-start.15 = (s32[1,1024]{1,0:T(1,128)S(1)}, s32[1,1024]{1,0:T(1,128)}, u32[]{:S(2)}) copy-start(s32[1,1024]{1,0:T(1,128)} %drow_ref.1) | copy-start | bytes 12292
  62.5 2.7 %copy-start.1 = (bf16[2,4,4,32,768]{4,3,2,1,0:T(8,128)(2,1)S(1)}, bf16[2,4,4,32,768]{4,3,2,1,0:T(8,128)(2,1)}, u32[]{:S(2)}) copy-start(bf16[2,4,4,32,768]{4,3,2,1,0:T(8,128)(2,1)} %get-tuple-element.42) | copy-start | bytes 4718596
  64.0 2.5 copy-start
  244.4 8.8 %copy-start.5 = (f32[256,768]{1,0:T(8,128)S(1)}, f32[256,768]{1,0:T(8,128)}, u32[]{:S(2)}) copy-start(f32[256,768]{1,0:T(8,128)} %get-tuple-element.56) | copy-start | bytes 2359300
  250.9 3.1 %copy-start.14 = (f32[24,768]{1,0:T(8,128)S(1)}, f32[24,768]{1,0:T(8,128)}, u32[]{:S(2)}) copy-start(f32[24,768]{1,0:T(8,128)} %get-tuple-element.131) | copy-start | bytes 221188
  250.9 3.7 %copy-start.13 = (f32[24,768]{1,0:T(8,128)S(1)}, f32[24,768]{1,0:T(8,128)}, u32[]{:S(2)}) copy-start(f32[24,768]{1,0:T(8,128)} %get-tuple-element.132) | copy-start | bytes 221188
  250.9 4.3 %copy-start.12 = (f32[24,768]{1,0:T(8,128)S(1)}, f32[24,768]{1,0:T(8,128)}, u32[]{:S(2)}) copy-start(f32[24,768]{1,0:T(8,128)} %get-tuple-element.133) | copy-start | bytes 221188
  250.9 5.0 %copy-start.11 = (f32[24,768]{1,0:T(8,128)S(1)}, f32[24,768]{1,0:T(8,128)}, u32[]{:S(2)}) copy-start(f32[24,768]{1,0:T(8,128)} %get-tuple-element.134) | copy-start | bytes 221188
  251.0 5.6 %copy-start.4 = (f32[1536,128]{1,0:T(8,128)S(1)}, f32[1536,128]{1,0:T(8,128)}, u32[]{:S(2)}) copy-start(f32[1536,128]{1,0:T(8,128)} %get-tuple-element.63) | copy-start | bytes 2359300
  253.1 4.3 %copy-start.3 = (f32[1536,128]{1,0:T(8,128)S(1)}, f32[1536,128]{1,0:T(8,128)}, u32[]{:S(2)}) copy-start(f32[1536,128]{1,0:T(8,128)} %get-tuple-element.64) | copy-start | bytes 2359300
  256.5 1.8 copy-start.2
Sparse Core Ops, SparseCore 0:
  11.2 105.4 all-gather.1

commit v3 on v2

--- a/solution.py
+++ b/solution.py
@@ -63,6 +63,26 @@
     return [(lax.rem(e + j, sizes[0]), c, d) for j in range(1, sizes[0])]
 
 
+def crossing_only(sizes, n_loc, place):
+    _, there, _ = homes(sizes, n_loc, place)
+    return [device for j, (_, device) in enumerate(there) if j // n_loc and j % n_loc]
+
+
+def homes(sizes, n_loc, place):
+    n_e, n_c, n_d = sizes
+    e, c, d = place
+    size = n_d // n_loc
+    group, seat = d // size, lax.rem(d, size)
+    there, back = [], []
+    for j in range(n_e * n_loc):
+        je, jg = j // n_loc, j % n_loc
+        to_e, to_g = lax.rem(e + je, n_e), lax.rem(group + jg, n_loc)
+        from_e, from_g = lax.rem(e - je + n_e, n_e), lax.rem(group - jg + n_loc, n_loc)
+        there.append((to_e * n_loc + to_g, (to_e, c, to_g * size + seat)))
+        back.append(from_e * n_loc + from_g)
+    return e * n_loc + group, there, back
+
+
 class Courier:
     def __init__(self, send, recv):
         self.send, self.recv = send, recv
@@ -125,117 +145,35 @@
             copy.wait()
 
 
-def gather_kernel(
-    sizes, a_ref, o_ref, x_ref, ag_ref, og_ref, xg_ref, local, s_a, r_a, s_b, r_b, s_o, r_o, s_x, r_x
-):
+class Spread:
+    def __init__(self, sizes, place, courier, own, slot):
+        self.sizes, self.place, self.courier = sizes, place, courier
+        self.slot = slot
+        n_e, n_c, n_d = sizes
+        e, c, d = place
+        self.across_to = expert_peers(sizes, place)
+        self.along = [
+            courier.carry(own, slot(e, d), (e, c, lax.rem(d + k, n_d))) for k in range(1, n_d)
+        ]
+        self.across = [courier.carry(own, slot(e, d), device) for device in self.across_to]
+
+    def onward(self):
+        e, c, d = self.place
+        n_d = self.sizes[2]
+        for k in range(1, n_d):
+            self.along[k - 1].wait_recv()
+            block = self.slot(e, lax.rem(d - k + n_d, n_d))
+            for device in self.across_to:
+                self.across.append(self.courier.carry(block, block, device))
+
+    def arrive(self):
+        for copy in self.across:
+            copy.wait_recv()
+
+
+def spread_count(sizes):
     n_e, n_c, n_d = sizes
-    place = e, c, d = position()
-    pairs = n_c // 2
-    keep = [
-        pltpu.make_async_copy(a_ref.at[c], ag_ref.at[e, c, d], local.at[0]),
-        pltpu.make_async_copy(o_ref, og_ref.at[e, c, d], local.at[1]),
-        pltpu.make_async_copy(x_ref, xg_ref.at[c], local.at[2]),
-    ]
-    for copy in keep:
-        copy.start()
-    c_peers = [(e, lax.rem(c + k, n_c), d) for k in range(1, n_c)]
-    d_peers = [(e, c, lax.rem(d + k, n_d)) for k in range(1, n_d)]
-    e_peers = expert_peers(sizes, place)
-    greet(c_peers + d_peers + e_peers)
-    turn = []
-    for k in range(1, n_c):
-        copy = remote(
-            a_ref.at[lax.rem(c + k, n_c)],
-            ag_ref.at[e, c, d],
-            s_a.at[k - 1],
-            r_a.at[k - 1],
-            c_peers[k - 1],
-        )
-        copy.start()
-        turn.append(copy)
-    rows = ContextGather(
-        sizes, place, x_ref, lambda j: xg_ref.at[j], lambda k: s_x.at[k], lambda k: r_x.at[k]
-    )
-    rows.start()
-
-    def spread(own, slot, send, recv, base):
-        along = []
-        for k in range(1, n_d):
-            copy = remote(
-                own, slot(e, d), send.at[base + k - 1], recv.at[base + k - 1], d_peers[k - 1]
-            )
-            copy.start()
-            along.append(copy)
-        across = []
-        for j in range(1, n_e):
-            n = base + n_d - 1 + (j - 1) * n_d
-            copy = remote(own, slot(e, d), send.at[n], recv.at[n], e_peers[j - 1])
-            copy.start()
-            across.append(copy)
-        return along, across
-
-    def onward(parts, slot, send, recv, base):
-        along, across = parts
-        for k in range(1, n_d):
-            along[k - 1].wait_recv()
-            block = slot(e, lax.rem(d - k + n_d, n_d))
-            for j in range(1, n_e):
-                n = base + n_d - 1 + (j - 1) * n_d + k
-                copy = remote(block, block, send.at[n], recv.at[n], e_peers[j - 1])
-                copy.start()
-                across.append(copy)
-
-    o_slot = lambda j, k: og_ref.at[j, c, k]
-    a_slot = lambda j, k: ag_ref.at[j, :, k]
-    o_parts = spread(o_ref, o_slot, s_o, r_o, 0)
-    for copy in turn:
-        copy.wait()
-    for copy in keep:
-        copy.wait()
-    a_parts = spread(ag_ref.at[e, :, d], a_slot, s_b, r_b, 0)
-    onward(o_parts, o_slot, s_o, r_o, 0)
-    rows.forward()
-    for copy in o_parts[1]:
-        copy.wait_recv()
-    base = (n_d - 1) + (n_e - 1) * n_d
-    whole = ContextGather(
-        sizes,
-        place,
-        og_ref.at[:, c],
-        lambda j: og_ref.at[:, j],
-        lambda k: s_o.at[base + k],
-        lambda k: r_o.at[base + k],
-    )
-    whole.start()
-    onward(a_parts, a_slot, s_b, r_b, 0)
-    whole.forward()
-    for copy in a_parts[1]:
-        copy.wait()
-    for copy in [*a_parts[0], *o_parts[0], *o_parts[1]]:
-        copy.wait_send()
-    rows.finish()
-    whole.finish()
-
-
-def gather_first(sizes, a_part, o_part, x_part):
-    n_e, n_c, n_d = sizes
-    dma = pltpu.SemaphoreType.DMA
-    spread = (n_d - 1) + (n_e - 1) * n_d
-    counts = [n_c - 1, n_c - 1, spread, spread, spread + n_c - 1, spread + n_c - 1, n_c - 1, n_c - 1]
-    anywhere = pl.BlockSpec(memory_space=pl.ANY)
-    return pl.pallas_call(
-        functools.partial(gather_kernel, sizes),
-        out_shape=(
-            jax.ShapeDtypeStruct((n_e, n_c, n_d, *a_part.shape[1:]), BF16),
-            jax.ShapeDtypeStruct((n_e, n_c, n_d, *o_part.shape), BF16),
-            jax.ShapeDtypeStruct((n_c, *x_part.shape), BF16),
-        ),
-        in_specs=[anywhere] * 3,
-        out_specs=(anywhere,) * 3,
-        scratch_shapes=[dma((3,))] + [dma((n,)) for n in counts],
-        compiler_params=pltpu.CompilerParams(collective_id=0, has_side_effects=True),
-        name="gather_first",
-    )(a_part, o_part, x_part)
+    return (n_d - 1) + (n_e - 1) * n_d
 
 
 def softmax_pair(left, right):
@@ -245,8 +183,15 @@
     return left / total, right / total
 
 
-def route_parts(routes_t, routes, small, n_ff, n_all, slots):
-    rows = routes.shape[0]
+def tall(array, height):
+    return jnp.concatenate(
+        [array, jnp.zeros((height - array.shape[0], *array.shape[1:]), array.dtype)], axis=0
+    )
+
+
+def route_parts(routes_t, small, n_ff, n_all, slots):
+    rows = routes_t.shape[1]
+    routes = tall(routes_t.astype(F32), LANES).T
     hot = lax.broadcasted_iota(jnp.int32, (LANES, rows), 0)
     marks = [(hot == routes_t[k : k + 1, :]) & (hot < n_ff) for k in range(2)]
     both = (marks[0] | marks[1]).astype(F32)
@@ -264,7 +209,7 @@
             ).astype(BF16)
         )
     lane = lax.broadcasted_iota(jnp.int32, (rows, LANES), 1)
-    picks = [(lane == routes[:, k : k + 1]).astype(F32) for k in range(2)]
+    picks = [(lane.astype(F32) == routes[:, k : k + 1]).astype(F32) for k in range(2)]
     chosen = [
         jnp.sum(jnp.where(picks[k] > 0, small, 0.0), axis=1, keepdims=True) for k in range(2)
     ]
@@ -277,18 +222,27 @@
 def front_kernel(
     sizes,
     cfg,
+    wq_ref,
+    wk_ref,
+    wv_ref,
+    wout_ref,
+    router_ref,
+    coef_ref,
+    value_ref,
+    gains_ref,
+    xown_ref,
+    gate_ref,
+    up_ref,
+    down_ref,
+    drow_ref,
+    routest_ref,
+    prev_ref,
+    g_ref,
     xg_ref,
-    xown_ref,
     wqkv_ref,
     wo_ref,
     wsm_ref,
     vec_ref,
-    dcol_ref,
-    drow_ref,
-    routes_ref,
-    routest_ref,
-    prev_ref,
-    g_ref,
     a1_ref,
     qt_ref,
     kh_ref,
@@ -299,6 +253,13 @@
     small_ref,
     p_ref,
     slots_ref,
+    ew_ref,
+    small_scr,
+    a_ref,
+    ow_ref,
+    ag,
+    og,
+    ew_own,
     o_scr,
     vt_scr,
     p_scr,
@@ -312,25 +273,126 @@
     s_g,
     r_g,
     l_g,
+    s_c,
+    r_c,
+    s_ow,
+    r_ow,
+    s_xg,
+    r_xg,
 ):
     n_e, n_c, n_d = sizes
     hp, n_ff, n_all, n_loc, slots = cfg
     hc = hp * HEAD_DIM
     place = e, c, d = position()
-    length = xg_ref.shape[0]
-    rows = length // n_c
+    rows = xown_ref.shape[0]
+    length = rows * n_c
     c_all = [(e, lax.rem(c + k, n_c), d) for k in range(1, n_c)]
-    e_peers = expert_peers(sizes, place)
-    greet(c_all + e_peers)
+    n_s = n_e * n_loc
+    me, there, back = homes(sizes, n_loc, place)
+    d_peers = [(e, c, lax.rem(d + k, n_d)) for k in range(1, n_d)]
+    w_rows = wq_ref.shape[0]
+    small_scr[...] = jnp.zeros_like(small_scr)
+    at = 0
+    for ref in (router_ref, coef_ref, value_ref, gains_ref):
+        small_scr[at : at + ref.shape[0], :w_rows] = ref[...]
+        at += ref.shape[0]
+    w_small = small_scr[...].T[:w_rows, : a_ref.shape[2] - 3 * hc].astype(BF16)
+    a_ref[...] = jnp.zeros_like(a_ref)
+    ow_ref[...] = jnp.zeros_like(ow_ref)
+    ow_ref[:w_rows, :] = wout_ref[...].astype(BF16)
+    for b in range(n_c):
+        for n, ref in enumerate((wq_ref, wk_ref, wv_ref)):
+            wide = min(hc, D - b * hc)
+            if wide > 0:
+                a_ref[b, :w_rows, n * hc : n * hc + wide] = ref[:, b * hc : b * hc + wide].astype(
+                    BF16
+                )
+        a_ref[b, :w_rows, 3 * hc :] = w_small
+    greet(c_all + d_peers + expert_peers(sizes, place) + crossing_only(sizes, n_loc, place))
+    post = Courier(s_c, r_c)
+    turned = [
+        post.carry(a_ref.at[lax.rem(c + k, n_c)], ag.at[e, c, d], device)
+        for k, device in enumerate(c_all, 1)
+    ]
+    x_rows = ContextGather(
+        sizes,
+        place,
+        xown_ref,
+        lambda k: xg_ref.at[k],
+        lambda k: s_xg.at[k],
+        lambda k: r_xg.at[k],
+    )
+    x_rows.start()
+    ow_spread = Spread(sizes, place, post, ow_ref, lambda j, k: og.at[j, c, k])
+    ag[e, c, d] = a_ref[c]
+    og[e, c, d] = ow_ref[...]
+    xg_ref[pl.ds(c, 1)] = xown_ref[...][None]
+    for n, ref in enumerate((gate_ref, up_ref, down_ref)):
+        size = ref.shape[1]
+        ew_own[:, n * size : (n + 1) * size, :] = ref[...].astype(BF16)
+    for copy in turned:
+        copy.wait_recv()
+    a_spread = Spread(sizes, place, post, ag.at[e, :, d], lambda j, k: ag.at[j, :, k])
+    size = n_d // n_loc
+    group, seat = d // size, lax.rem(d, size)
+    mates = [(e, c, group * size + lax.rem(seat + k, size)) for k in range(1, size)]
+    keep_w = pltpu.make_async_copy(ew_own.at[group], ew_ref.at[d], l_g.at[2 * n_s])
+    keep_w.start()
+    w_near = [post.carry(ew_own.at[group], ew_ref.at[d], device) for device in mates]
+    w_far = []
+    for k in range(1, n_loc):
+        to = lax.rem(group + k, n_loc)
+        w_far.append(post.carry(ew_own.at[to], ew_ref.at[d], (e, c, to * size + seat)))
+
+    def pass_weights():
+        for k, copy in enumerate(w_far, 1):
+            copy.wait_recv()
+            block = ew_ref.at[lax.rem(group - k + n_loc, n_loc) * size + seat]
+            w_near.extend([post.carry(block, block, device) for device in mates])
+
+    ow_spread.onward()
+    x_rows.forward()
+    ow_spread.arrive()
+    ow_rows = ContextGather(
+        sizes,
+        place,
+        og.at[:, c],
+        lambda k: og.at[:, k],
+        lambda k: s_ow.at[k],
+        lambda k: r_ow.at[k],
+    )
+    ow_rows.start()
+    a_spread.onward()
+    x_rows.finish()
+    a_spread.arrive()
+
+    padded = a_ref.shape[1]
+    at_row = lax.broadcasted_iota(jnp.int32, (D // n_e, n_c * n_d * padded), 0)
+    at_slab = lax.broadcasted_iota(jnp.int32, (D // n_e, n_c * n_d * padded), 1)
+    unpad = jnp.where(
+        at_slab == at_row // w_rows * padded + lax.rem(at_row, w_rows), 1.0, 0.0
+    ).astype(BF16)
+    weights = jnp.concatenate(
+        [dot(unpad, ag[k].reshape(n_c * n_d * padded, ag.shape[-1])) for k in range(n_e)], axis=0
+    )
+    wqkv = weights[:, : 3 * hc].astype(BF16)
+    wqkv_ref[...] = wqkv
+    w_small = jnp.concatenate(
+        [weights[:, 3 * hc : 3 * hc + SMALL], jnp.zeros((D, LANES - SMALL), F32)], axis=1
+    )
+    wsm_ref[...] = w_small.astype(BF16)
+    w_lines = w_small.T
+    vec_ref[0:2, :] = w_lines[n_all + 6 : n_all + 8, :]
+    vec_ref[2:4, :] = w_lines[n_all + 4 : n_all + 6, :]
+    vec_ref[4:8, :] = jnp.zeros((4, D), F32)
 
     gain_one = vec_ref[0:1, :]
     for b in range(n_c):
-        part = pl.ds(b * rows, rows)
-        x = xg_ref[part, :].astype(F32)
+        x = xg_ref[b].astype(F32)
         inverse = lax.rsqrt(jnp.mean(x * x, axis=-1, keepdims=True) + EPS)
-        a1_ref[part, :] = (x * inverse * gain_one).astype(BF16)
+        a1_ref[b * rows : (b + 1) * rows, :] = (x * inverse * gain_one).astype(BF16)
     a1 = a1_ref[...]
-    wqkv = wqkv_ref[...]
+    ow_rows.forward()
     q_t = dot(wqkv[:, :hc], a1, 0, 1).astype(BF16) * jnp.asarray(HEAD_DIM**-0.5, BF16)
     qt_ref[...] = q_t
     kv = dot(a1, wqkv[:, hc:]).astype(BF16)
@@ -339,13 +401,15 @@
         vh_ref[j] = kv[:, hc + j * HEAD_DIM : hc + (j + 1) * HEAD_DIM]
     vt_scr[...] = dot(wqkv[:, 2 * hc :], a1, 0, 1).astype(BF16)
 
+    documents = drow_ref[...].astype(F32)
+    document_of = jnp.broadcast_to(documents, (LANES, length)).T[:, :1]
     turn = 0
     p_copies = {}
     for b in reversed(range(n_c)):
         reach = (b + 1) * rows
         key_place = lax.broadcasted_iota(jnp.int32, (reach, rows), 0)
         q_place = lax.broadcasted_iota(jnp.int32, (reach, rows), 1) + b * rows
-        allowed = (dcol_ref[:reach, :] == drow_ref[:, b * rows : reach]) & (key_place <= q_place)
+        allowed = (document_of[:reach] == documents[:, b * rows : reach]) & (key_place <= q_place)
         bias = jnp.where(allowed, 0.0, -1e30)
         for j in range(hp):
             head = slice(j * HEAD_DIM, (j + 1) * HEAD_DIM)
@@ -372,8 +436,16 @@
                 o_scr.at[b], mixed_ref.at[c], s_o.at[b], r_o.at[c], (e, b, d)
             ).start()
 
+    pass_weights()
     for n in range(max(0, turn - 2), turn):
         p_copies[n].wait()
+    ow_rows.finish()
+    if n_c * hc > D:
+        wo_ref[D:, :] = jnp.zeros((n_c * hc - D, D), BF16)
+    for k in range(n_e):
+        wo_ref[k * (D // n_e) : (k + 1) * (D // n_e), :] = dot(
+            unpad, og[k].reshape(n_c * n_d * padded, D)
+        ).astype(BF16)
     mixed_ref[pl.ds(c, 1)] = o_scr[pl.ds(c, 1)]
     for b in range(n_c):
 
@@ -389,12 +461,9 @@
     inverse = lax.rsqrt(jnp.mean(h * h, axis=-1, keepdims=True) + EPS)
     a2 = (h * inverse * vec_ref[1:2, :]).astype(BF16)
     a2_ref[...] = a2
-    small = dot(a2, wsm_ref[...]) + prev_ref[...]
+    small = dot(a2, wsm_ref[...]) + tall(prev_ref[...], LANES).T
     small_ref[...] = small
-    tables, _, w_pair, _, _ = route_parts(
-        routest_ref[...], routes_ref[...], small, n_ff, n_all, slots
-    )
-    per = n_loc * slots
+    tables, _, w_pair, _, _ = route_parts(routest_ref[...], small, n_ff, n_all, slots)
     crossing = {}
     gathers = {}
     g = g_ref[...]
@@ -406,24 +475,19 @@
                 tables[1], (w_pair[1] * g).astype(BF16)
             )
             block = block.astype(BF16)
-        for k in range(n_e):
-            sbuf[t, k] = block[k * per : (k + 1) * per, :]
-        for j in range(1, n_e):
-            n = t * n_e + j
-            copy = remote(
-                sbuf.at[t, lax.rem(e + j, n_e)],
-                xin.at[t, e],
-                s_x.at[n],
-                r_x.at[n],
-                e_peers[j - 1],
-            )
+        for k in range(n_s):
+            sbuf[t, k] = block[k * slots : (k + 1) * slots, :]
+        for j in reversed(range(1, n_s)):
+            n = t * n_s + j
+            part, device = there[j]
+            copy = remote(sbuf.at[t, part], xin.at[t, me], s_x.at[n], r_x.at[n], device)
             copy.start()
             crossing[t, j] = copy
 
         def gather(j, own, t=t):
-            src = lax.rem(e - j + n_e, n_e)
-            base = (t * n_e + j) * (n_c - 1)
-            keep = pltpu.make_async_copy(own, slots_ref.at[c, t, src], l_g.at[t * n_e + j])
+            src = back[j]
+            base = (t * n_s + j) * (n_c - 1)
+            keep = pltpu.make_async_copy(own, slots_ref.at[c, t, src], l_g.at[t * n_s + j])
             keep.start()
             made = ContextGather(
                 sizes,
@@ -436,37 +500,50 @@
             made.start()
             gathers[t, j] = (made, keep)
 
-        gather(0, sbuf.at[t, e])
+        gather(0, sbuf.at[t, me])
         crossing[t, 0] = gather
     for t in range(2):
-        for j in range(1, n_e):
+        for j in range(1, n_s):
             crossing[t, j].wait_recv()
-            crossing[t, 0](j, xin.at[t, lax.rem(e - j + n_e, n_e)])
+            crossing[t, 0](j, xin.at[t, back[j]])
     for made, _ in gathers.values():
         made.forward()
     for made, keep in gathers.values():
         made.finish()
         keep.wait()
     for t in range(2):
-        for j in range(1, n_e):
+        for j in range(1, n_s):
             crossing[t, j].wait_send()
+    for copy in w_near:
+        copy.wait_recv()
+    keep_w.wait()
+    post.finish()
 
 
 def front(sizes, cfg, *operands):
     n_e, n_c, n_d = sizes
     hp, n_ff, n_all, n_loc, slots = cfg
     hc = hp * HEAD_DIM
-    length = operands[0].shape[0]
-    rows = length // n_c
-    per = n_loc * slots
+    rows = operands[8].shape[0]
+    length = rows * n_c
+    padded = up_to(operands[0].shape[0], 16)
+    width = up_to(3 * hc + SMALL, LANES)
+    part = operands[9].shape[1]
+    posts = (n_c - 1) + 2 * spread_count(sizes) + n_d - 1
+    n_s = n_e * n_loc
     dma = pltpu.SemaphoreType.DMA
     vmem = pl.BlockSpec(memory_space=pltpu.VMEM)
     anywhere = pl.BlockSpec(memory_space=pl.ANY)
     shape = jax.ShapeDtypeStruct
-    gathers = 2 * n_e * (n_c - 1)
+    gathers = 2 * n_s * (n_c - 1)
     return pl.pallas_call(
         functools.partial(front_kernel, sizes, cfg),
         out_shape=(
+            shape((n_c, rows, D), BF16),
+            shape((D, 3 * hc), BF16),
+            shape((n_c * hc, D), BF16),
+            shape((D, LANES), BF16),
+            shape((8, D), F32),
             shape((length, D), BF16),
             shape((hc, length), BF16),
             shape((hp, length, HEAD_DIM), BF16),
@@ -476,40 +553,50 @@
             shape((rows, D), BF16),
             shape((rows, LANES), F32),
             shape((hp, n_c, length, rows), BF16),
-            shape((n_c, 2, n_e, per, D), BF16),
+            shape((n_c, 2, n_s, slots, D), BF16),
+            shape((n_d, 3 * part, LANES), BF16),
         ),
         in_specs=[vmem] * len(operands),
-        out_specs=(vmem,) * 8 + (anywhere,) * 2,
+        out_specs=(vmem,) * 13 + (anywhere,) * 3,
         scratch_shapes=[
+            pltpu.VMEM((LANES, LANES), F32),
+            pltpu.VMEM((n_c, padded, width), BF16),
+            pltpu.VMEM((padded, D), BF16),
+            pltpu.VMEM((n_e, n_c, n_d, padded, width), BF16),
+            pltpu.VMEM((n_e, n_c, n_d, padded, D), BF16),
+            pltpu.VMEM((n_loc, 3 * part, LANES), BF16),
             pltpu.VMEM((n_c, hc, rows), BF16),
             pltpu.VMEM((hc, length), BF16),
             pltpu.VMEM((2, length, rows), BF16),
-            pltpu.VMEM((2, n_e, per, D), BF16),
-            pltpu.VMEM((2, n_e, per, D), BF16),
+            pltpu.VMEM((2, n_s, slots, D), BF16),
+            pltpu.VMEM((2, n_s, slots, D), BF16),
             dma((2,)),
             dma((n_c,)),
             dma((n_c,)),
-            dma((2 * n_e,)),
-            dma((2 * n_e,)),
+            dma((2 * n_s,)),
+            dma((2 * n_s,)),
             dma((gathers,)),
             dma((gathers,)),
-            dma((2 * n_e,)),
+            dma((2 * n_s + 1,)),
+            dma((posts,)),
+            dma((posts,)),
+            *[dma((n_c - 1,))] * 4,
         ],
         compiler_params=pltpu.CompilerParams(
-            collective_id=1, has_side_effects=True, vmem_limit_bytes=VMEM_LIMIT
+            collective_id=0, has_side_effects=True, vmem_limit_bytes=VMEM_LIMIT
         ),
         name="front",
     )(*operands)
 
 
 def expert_kernel(x_ref, dy_ref, w_ref, out_ref, gw_ref, total):
-    step = pl.program_id(1)
+    step = pl.program_id(0)
     parts = w_ref.shape[0]
     x = x_ref[...].reshape(-1, D)
     dy = dy_ref[...].reshape(-1, D)
     block = out_ref.shape[0:1] + out_ref.shape[2:]
     gate, up, down = [
-        jnp.concatenate([w_ref[k, n, 0] for k in range(parts)], axis=1) for n in range(3)
+        jnp.concatenate([w_ref[k, n] for k in range(parts)], axis=1) for n in range(3)
     ]
     gate_pre = dot(x, gate)
     up_pre = dot(x, up)
@@ -534,37 +621,37 @@
         for n in range(3):
             total[n] += grads[n]
 
-    @pl.when(step == pl.num_programs(1) - 1)
+    @pl.when(step == pl.num_programs(0) - 1)
     def _():
         width = gate.shape[1] // parts
         for n in range(3):
             for k in range(parts):
-                gw_ref[k, n, 0] = total[n, :, k * width : (k + 1) * width].astype(BF16)
+                gw_ref[k, n] = total[n, :, k * width : (k + 1) * width].astype(BF16)
 
 
 def experts_pass(gathered, weights):
-    n_c, _, n_e, n_loc, slots, _ = gathered.shape
-    parts, _, _, _, units = weights.shape
-    take = max(1, min(n_c, 512 // (n_e * slots)))
+    n_c, _, n_s, slots, _ = gathered.shape
+    parts, _, _, units = weights.shape
+    take = max(1, min(n_c, 512 // (n_s * slots)))
     return pl.pallas_call(
         expert_kernel,
-        grid=(n_loc, n_c // take),
+        grid=(n_c // take,),
         out_shape=(
             jax.ShapeDtypeStruct(gathered.shape, BF16),
             jax.ShapeDtypeStruct(weights.shape, BF16),
         ),
         in_specs=[
-            pl.BlockSpec((take, 1, n_e, 1, slots, D), lambda i, j: (j, 0, 0, i, 0, 0)),
-            pl.BlockSpec((take, 1, n_e, 1, slots, D), lambda i, j: (j, 1, 0, i, 0, 0)),
-            pl.BlockSpec((parts, 3, 1, D, units), lambda i, j: (0, 0, i, 0, 0)),
+            pl.BlockSpec((take, 1, n_s, slots, D), lambda i: (i, 0, 0, 0, 0)),
+            pl.BlockSpec((take, 1, n_s, slots, D), lambda i: (i, 1, 0, 0, 0)),
+            pl.BlockSpec((parts, 3, D, units), lambda i: (0, 0, 0, 0)),
         ],
         out_specs=(
-            pl.BlockSpec((take, 2, n_e, 1, slots, D), lambda i, j: (j, 0, 0, i, 0, 0)),
-            pl.BlockSpec((parts, 3, 1, D, units), lambda i, j: (0, 0, i, 0, 0)),
+            pl.BlockSpec((take, 2, n_s, slots, D), lambda i: (i, 0, 0, 0, 0)),
+            pl.BlockSpec((parts, 3, D, units), lambda i: (0, 0, 0, 0)),
         ),
         scratch_shapes=[pltpu.VMEM((3, D, parts * units), F32)],
         compiler_params=pltpu.CompilerParams(
-            dimension_semantics=("arbitrary", "arbitrary"), vmem_limit_bytes=VMEM_LIMIT
+            dimension_semantics=("arbitrary",), vmem_limit_bytes=VMEM_LIMIT
         ),
         name="experts_pass",
     )(gathered, gathered, weights)
@@ -578,7 +665,6 @@
     a2_ref,
     small_ref,
     g_ref,
-    routes_ref,
     routest_ref,
     wo_ref,
     wqkv_ref,
@@ -599,7 +685,10 @@
     gk_ref,
     gv_ref,
     go_ref,
-    gsmall_ref,
+    grouter_ref,
+    gcoef_ref,
+    gvalue_ref,
+    ggains_ref,
     egate_ref,
     eup_ref,
     edown_ref,
@@ -622,6 +711,8 @@
     x_scr,
     ew_own,
     ew_in,
+    ew_mid,
+    ew_out,
     t_send,
     t_recv,
     t_z,
@@ -682,79 +773,64 @@
 
     fetch_x(c, 2).start()
     fetch_x(0, 0).start()
-    greet(peers + e_peers + d_peers)
-
-    def expert_send(way, step, src):
-        there = d + 1 if way == 0 else d - 1
-        return remote(
-            src,
-            ew_in.at[way, step - 1],
-            s_w.at[way, step - 1],
-            r_w.at[way, step - 1],
-            (e, c, there),
-        )
-
-    def expert_place(way):
-        return d if way == 0 else n_d - 1 - d
-
-    def add_own(way, step, part):
-        size = ew_own.shape[1]
-        tile = size // 8 if size % 128 == 0 else size
-
-        def one(n, carry):
-            at = pl.ds(pl.multiple_of(n * tile, tile), tile)
-            total = ew_in[way, step - 1, at, :].astype(F32) + ew_own[part, at, :].astype(F32)
-            ew_in[way, step - 1, at, :] = total.astype(BF16)
-            return carry
-
-        lax.fori_loop(0, size // tile, one, 0)
-
-    def expert_step(step):
-        for way in range(2):
-            at = expert_place(way)
-            far = n_d + at - step
-            part = far if way == 0 else n_d - 1 - far
-
-            @pl.when(at == 0)
-            def _():
-                expert_send(way, step, ew_own.at[part]).start()
-
-            if step > 1:
-
-                @pl.when((at > 0) & (at < step))
-                def _():
-                    src = ew_in.at[way, step - 2]
-                    expert_send(way, step - 1, src).wait_recv()
-                    add_own(way, step - 1, part)
-                    expert_send(way, step, src).start()
+    n_s = n_e * n_loc
+    me, there_s, _ = homes(sizes, n_loc, place)
+    greet(peers + e_peers + d_peers + crossing_only(sizes, n_loc, place))
+
+    size = n_d // n_loc
+    group, seat = d // size, lax.rem(d, size)
+    mates = [(e, c, group * size + lax.rem(seat + k, size)) for k in range(1, size)]
+    others = [lax.rem(group + k, n_loc) for k in range(1, n_loc)]
+    freight = Courier(s_w, r_w)
+    e_near = {}
+    e_far = []
+
+    def expert_start():
+        for k, mate in enumerate(mates):
+            for r, other in enumerate(others):
+                e_near[k, r] = freight.carry(
+                    ew_own.at[other * size + lax.rem(seat + k + 1, size)], ew_mid.at[k, r], mate
+                )
+            e_near[k, -1] = freight.carry(ew_own.at[mate[2]], ew_in.at[k], mate)
+
+    def expert_cross():
+        for r, other in enumerate(others):
+            target = other * size + seat
+            for k in range(size - 1):
+                e_near[k, r].wait_recv()
+
+            def one(n, carry):
+                at = pl.ds(pl.multiple_of(n * tile, tile), tile)
+                total = ew_own[target, at, :].astype(F32)
+                for k in range(size - 1):
+                    total = total + ew_mid[k, r, at, :].astype(F32)
+                ew_out[r, at, :] = total.astype(BF16)
+                return carry
+
+            tile = ew_own.shape[1] // 9
+            lax.fori_loop(0, 9, one, 0)
+            e_far.append(freight.carry(ew_out.at[r], ew_in.at[size - 1 + r], (e, c, target)))
 
     def expert_end():
-        last = n_d - 1
-        for way in range(2):
-
-            @pl.when(expert_place(way) > 0)
-            def _():
-                expert_send(way, last, ew_own.at[0]).wait_recv()
-
-        size = ew_own.shape[1] // 3
+        for k in range(size - 1):
+            e_near[k, -1].wait_recv()
+        for copy in e_far:
+            copy.wait_recv()
+        part = ew_own.shape[1] // 3
         for n, ref in enumerate((egate_ref, eup_ref, edown_ref)):
-            at = pl.ds(n * size, size)
-            ref[...] = ew_own[d, at, :].astype(F32)
-            for way in range(2):
-
-                @pl.when(expert_place(way) > 0)
-                def _():
-                    ref[...] += ew_in[way, last - 1, at, :].astype(F32)
-
-        for way in range(2):
-            for step in range(1, n_d):
-
-                @pl.when(expert_place(way) < step)
-                def _():
-                    expert_send(way, step, ew_own.at[0]).wait_send()
+            at = slice(n * part, (n + 1) * part)
+            total = ew_own[d, at, :].astype(F32)
+            for k in range(size - 1):
+                total = total + ew_in[k, at, :].astype(F32)
+            ref[pl.ds(group, 1)] = total[None]
+            for r in range(n_loc - 1):
+                ref[pl.ds(lax.rem(group - r - 1 + n_loc, n_loc), 1)] = ew_in[
+                    size - 1 + r, at, :
+                ].astype(F32)[None]
+        freight.finish()
 
     bring.wait()
-    expert_step(1)
+    expert_start()
 
     def load(ref, slot=0):
         if in_vmem:
@@ -778,12 +854,12 @@
             copy.start()
             copy.wait()
 
-    pieces = [(t, j) for j in [*range(1, n_e), 0] for t in range(2)]
+    pieces = [(t, j) for j in [*reversed(range(1, n_s)), 0] for t in range(2)]
     first_copies = {}
     for t, j in pieces:
-        src = lax.rem(e + j, n_e)
+        src = there_s[j][0]
         for k in [*range(1, pairs), 0]:
-            n = (t * n_e + j) * pairs + k
+            n = (t * n_s + j) * pairs + k
             there = lax.rem(outer + k, pairs)
             copy = remote(
                 res_ref.at[there, 1 - inner, t, src],
@@ -798,9 +874,9 @@
         take.wait()
     second = {}
     for t, j in pieces:
-        src = lax.rem(e + j, n_e)
+        src = there_s[j][0]
         for k in range(1, pairs):
-            n = (t * n_e + j) * pairs + k
+            n = (t * n_s + j) * pairs + k
             there = lax.rem(outer + k, pairs)
             first_copies[t, j, k].wait_recv()
             total = own_part(there, t, src) + load(inn.at[there, t, src], 1)
@@ -812,30 +888,31 @@
             second[t, j, k] = copy
     home = {}
     for t, j in pieces:
-        src = lax.rem(e + j, n_e)
+        src = there_s[j][0]
         first_copies[t, j, 0].wait_recv()
         total = own_part(outer, t, src) + load(inn.at[outer, t, src], 1)
         for k in range(1, pairs):
             second[t, j, k].wait_recv()
             total = total + load(outr.at[k - 1, t, src], 2)
         if j == 0:
-            back[t, e] = total.astype(BF16)
+            back[t, me] = total.astype(BF16)
         else:
             xsum[t, src] = total.astype(BF16)
-            n = t * n_e + j
+            n = t * n_s + j
             copy = remote(
-                xsum.at[t, src], back.at[t, e], s_x.at[n], r_x.at[n], e_peers[j - 1]
+                xsum.at[t, src], back.at[t, me], s_x.at[n], r_x.at[n], there_s[j][1]
             )
             copy.start()
             home[t, j] = copy
 
+    expert_cross()
     h = h_ref[...]
     a2 = a2_ref[...].astype(F32)
     g = g_ref[...]
     small = small_ref[...]
     value_one, value_two = vec_ref[2:3, :], vec_ref[3:4, :]
     tables, picks, w_pair, first, other = route_parts(
-        routest_ref[...], routes_ref[...], small, n_ff, n_all, slots
+        routest_ref[...], small, n_ff, n_all, slots
     )
     copy_on, one_on, two_on = [
         [picks[k][:, n_ff + n : n_ff + n + 1] for k in range(2)] for n in (1, 2, 3)
@@ -868,7 +945,7 @@
         picks[0] * (w_pair[0] * (d_weight[0] - center))
         + picks[1] * (w_pair[1] * (d_weight[1] - center))
     )
-    dprev_ref[...] = d_logits[:, :n_all]
+    dprev_ref[...] = d_logits.T[:n_all, :]
     lane = lax.broadcasted_iota(jnp.int32, (rows, LANES), 1)
     d_small = d_logits
     for base, pair, weight, g_value in (
@@ -908,8 +985,6 @@
     )
     gather.start()
     dx_ref[...] = d_h
-    if n_d > 2:
-        expert_step(2)
     g_o = dot(mixed_ref[...].reshape(n_c * hc, rows), d_hb)
     run = n_d * w_rows
     for b in range(n_c):
@@ -1031,8 +1106,6 @@
 
     for k in range(chunks - 1):
         send_chunk(k, g_all[:, k * LANES : (k + 1) * LANES])
-    for step in range(3, n_d):
-        expert_step(step)
     wqkv = wqkv_ref[...]
     gain_one = vec_ref[0:1, :]
     d_gain_one = jnp.zeros((1, D), F32)
@@ -1054,10 +1127,10 @@
         copy.start()
         to_pair.append((k, copy))
     spot = lax.broadcasted_iota(jnp.int32, (LANES, D), 0)
-    tall = jnp.zeros((LANES, D), F32)
+    lines = jnp.zeros((LANES, D), F32)
     for n, row in enumerate((d_const_one, d_const_two, d_gain_one, d_gain_two)):
-        tall = tall + jnp.where(spot == shift + n_all + 4 + n, row, 0.0)
-    send_chunk(chunks - 1, g_all[:, (chunks - 1) * LANES :] + g_small + tall.T)
+        lines = lines + jnp.where(spot == shift + n_all + 4 + n, row, 0.0)
+    send_chunk(chunks - 1, g_all[:, (chunks - 1) * LANES :] + g_small + lines.T)
     along = []
     for k, copy in to_pair:
         if k == 0:
@@ -1130,7 +1203,12 @@
             if width > 0:
                 ref[:, b * hc : b * hc + width] = line[:, n * hc : n * hc + width]
         s_total = s_total + line[:, 3 * hc : 3 * hc + SMALL]
-    gsmall_ref[...] = s_total
+    s_lines = jnp.concatenate([s_total, jnp.zeros((w_rows, LANES - SMALL), F32)], axis=1)
+    s_lines = tall(s_lines, LANES).T
+    at = 0
+    for ref in (grouter_ref, gcoef_ref, gvalue_ref, ggains_ref):
+        ref[...] = s_lines[at : at + ref.shape[0], :w_rows]
+        at += ref.shape[0]
     bag.finish()
     for copy in first_copies.values():
         copy.wait_send()
@@ -1151,27 +1229,30 @@
     rows = operands[1].shape[0]
     length = rows * n_c
     pairs = n_c // 2
-    per = n_loc * slots
+    per = slots
     dma = pltpu.SemaphoreType.DMA
     vmem = pl.BlockSpec(memory_space=pltpu.VMEM)
     anywhere = pl.BlockSpec(memory_space=pl.ANY)
     shape = jax.ShapeDtypeStruct
-    n_in = 2 * n_e * pairs
-    part = operands[18].shape[1]
+    n_s = n_e * n_loc
+    n_in = 2 * n_s * pairs
+    part = operands[17].shape[1]
     w_rows = D // (n_e * n_c * n_d)
     chunks = up_to(3 * hc + SMALL, LANES) // LANES
     run = up_to(n_d * w_rows, 16)
     turn = up_to(n_c * w_rows, 16)
     few = up_to(w_rows, 16)
     few_wide = up_to(w_rows, 8)
+    size = n_d // n_loc
+    loads = (size - 1) * n_loc + n_loc - 1
     bags = chunks * (n_e - 1 + n_d - 1) + n_c - 1
     parcels = 2 * pairs - 1 + n_e - 1 + n_d - 1
     n_more = max(1, pairs - 1)
     in_specs = [vmem] * len(operands)
     in_specs[0] = anywhere
-    in_specs[16] = in_specs[17] = in_specs[18] = anywhere
-    arriving = [(pairs, 2, n_e, per, D), (n_more, 2, n_e, per, D), (n_more, 2, n_e, per, D)]
-    roomy = 2 * pairs * n_e * per * D <= 2**21
+    in_specs[15] = in_specs[16] = in_specs[17] = anywhere
+    arriving = [(pairs, 2, n_s, per, D), (n_more, 2, n_s, per, D), (n_more, 2, n_s, per, D)]
+    roomy = 2 * pairs * n_s * per * D <= 2**21
     held = [pltpu.VMEM(dims, BF16) for dims in arriving] if roomy else []
     extra = [] if roomy else [shape(dims, BF16) for dims in arriving]
     stage = pltpu.VMEM(arriving[0] if roomy else (4, per, D), BF16)
@@ -1180,18 +1261,18 @@
         out_shape=(
             shape((rows, D), F32),
             shape((rows, D), F32),
-            shape((rows, n_all), F32),
+            shape((n_all, rows), F32),
             *[shape((w_rows, D), F32)] * 4,
-            shape((w_rows, SMALL), F32),
-            *[shape((part // 3, LANES), F32)] * 3,
+            *[shape((n, w_rows), F32) for n in (n_all, 4, 2, 2)],
+            *[shape((n_loc, part // 3, LANES), F32)] * 3,
             *extra,
         ),
         in_specs=in_specs,
-        out_specs=(vmem,) * 11 + (anywhere,) * len(extra),
+        out_specs=(vmem,) * 14 + (anywhere,) * len(extra),
         scratch_shapes=[
             *held,
-            pltpu.VMEM((2, n_e, per, D), BF16),
-            pltpu.VMEM((2, n_e, per, D), BF16),
+            pltpu.VMEM((2, n_s, per, D), BF16),
+            pltpu.VMEM((2, n_s, per, D), BF16),
             stage,
             pltpu.VMEM((n_c, rows, D), BF16),
             pltpu.VMEM((hc, length), BF16),
@@ -1205,7 +1286,9 @@
             pltpu.VMEM((n_more, rows, D), BF16),
             pltpu.VMEM((3, rows, D), BF16),
             pltpu.VMEM((n_d, part, LANES), BF16),
-            pltpu.VMEM((2, n_d - 1, part, LANES), BF16),
+            pltpu.VMEM((size + n_loc - 2, part, LANES), BF16),
+            pltpu.VMEM((max(1, size - 1), max(1, n_loc - 1), part, LANES), BF16),
+            pltpu.VMEM((max(1, n_loc - 1), part, LANES), BF16),
             pltpu.VMEM((chunks, n_e, D // n_e, LANES), BF16),
             pltpu.VMEM((chunks, n_e - 1, D // n_e, LANES), BF16),
             pltpu.VMEM((chunks, n_d, turn, LANES), BF16),
@@ -1225,31 +1308,54 @@
             dma((n_in,)),
             dma((n_in,)),
             dma((n_in,)),
-            dma((2 * n_e,)),
-            dma((2 * n_e,)),
+            dma((2 * n_s,)),
+            dma((2 * n_s,)),
             dma((n_c - 1,)),
             dma((n_c - 1,)),
             dma((2,)),
             dma((n_c,)),
             dma((n_c,)),
-            dma((2, n_d - 1)),
-            dma((2, n_d - 1)),
+            dma((loads,)),
+            dma((loads,)),
             dma((bags,)),
             dma((bags,)),
             dma((parcels,)),
             dma((parcels,)),
         ],
         compiler_params=pltpu.CompilerParams(
-            collective_id=2, has_side_effects=True, vmem_limit_bytes=VMEM_LIMIT
+            collective_id=1, has_side_effects=True, vmem_limit_bytes=VMEM_LIMIT
         ),
         name="backward",
-    )(*operands)[:11]
-
-
-def pad_to(array, axis, size):
-    widths = [(0, 0)] * array.ndim
-    widths[axis] = (0, size - array.shape[axis])
-    return jnp.pad(array, widths)
+    )(*operands)[:14]
+
+
+def hand_out_kernel(*refs):
+    count = (len(refs) - 2) // 3
+    sources, results, held = refs[:count], refs[count : 2 * count], refs[2 * count : 3 * count]
+    in_sems, out_sems = refs[-2:]
+    takes = [pltpu.make_async_copy(sources[n], held[n], in_sems.at[n]) for n in range(count)]
+    gives = [pltpu.make_async_copy(held[n], results[n], out_sems.at[n]) for n in range(count)]
+    for copy in takes:
+        copy.start()
+    for take, give in zip(takes, gives):
+        take.wait()
+        give.start()
+    for copy in gives:
+        copy.wait()
+
+
+def hand_out(results):
+    anywhere = pl.BlockSpec(memory_space=pl.ANY)
+    dma = pltpu.SemaphoreType.DMA((len(results),))
+    return pl.pallas_call(
+        hand_out_kernel,
+        out_shape=tuple(jax.ShapeDtypeStruct(r.shape, r.dtype) for r in results),
+        in_specs=[anywhere] * len(results),
+        out_specs=(anywhere,) * len(results),
+        scratch_shapes=[*[pltpu.VMEM(r.shape, r.dtype) for r in results], dma, dma],
+        compiler_params=pltpu.CompilerParams(vmem_limit_bytes=VMEM_LIMIT),
+        name="hand_out",
+    )(*results)
 
 
 def body(
@@ -1278,73 +1384,63 @@
     n_all = w_router.shape[1]
     slots = rows // 4
     hp = -(-HEADS // n_c)
-    hc = hp * HEAD_DIM
     cfg = (hp, n_ff, n_all, n_loc, slots)
-    w_rows = w_query.shape[0]
-    w_pad = -(-w_rows // 16) * 16
-    width = -(-(3 * hc + SMALL) // LANES) * LANES
-
-    pieces = jnp.stack([expert_gate, expert_up, expert_down]).astype(BF16)
-    gathered_w = lax.all_gather(pieces, "dp", axis=0)
-
-    small_w = jnp.concatenate([w_router, const_coef, const_value, norm_gains], axis=1).astype(BF16)
-    slices = [
-        pad_to(w.astype(BF16), 1, n_c * hc).reshape(w_rows, n_c, hc)
-        for w in (w_query, w_key, w_value)
-    ]
-    slices.append(
-        jnp.broadcast_to(
-            pad_to(small_w, 1, width - 3 * hc)[:, None, :], (w_rows, n_c, width - 3 * hc)
-        )
-    )
-    a_part = pad_to(jnp.concatenate(slices, axis=2).transpose(1, 0, 2), 1, w_pad)
-    o_part = pad_to(w_out.astype(BF16), 0, w_pad)
-    a_all, o_all, x_all = gather_first(sizes, a_part, o_part, tokens[0])
-    a_all = a_all[:, :, :, :w_rows].reshape(D, width)
-    wqkv = a_all[:, : 3 * hc]
-    small_w = a_all[:, 3 * hc : 3 * hc + SMALL]
-    wsm = pad_to(small_w, 1, LANES)
-    wo = pad_to(o_all[:, :, :, :w_rows].reshape(D, D), 0, n_c * hc)
-    lines = small_w[:, n_all + 4 : n_all + 8].astype(F32).T
-    vec = pad_to(jnp.concatenate([lines[2:4], lines[0:2]], axis=0), 0, 8)
-
-    documents = doc_ids[0]
-    route_rows = routes[0]
-    routes_t = pad_to(route_rows.T, 0, 8)
-    prev = pad_to(prev_logits[0], 1, LANES)
+    routes_t = routes[0].T
     upstream = cotangent[0]
-    (a1, q_t, k_h, v_h, mixed, h, a2, small, probs, gathered) = front(
-        sizes,
-        cfg,
-        x_all.reshape(length, D),
-        tokens[0],
+    (
+        x_all,
         wqkv,
         wo,
         wsm,
         vec,
-        documents[:, None],
-        documents[None, :],
-        route_rows,
+        a1,
+        q_t,
+        k_h,
+        v_h,
+        mixed,
+        h,
+        a2,
+        small,
+        probs,
+        gathered,
+        gathered_w,
+    ) = front(
+        sizes,
+        cfg,
+        w_query,
+        w_key,
+        w_value,
+        w_out,
+        w_router.T,
+        const_coef.T,
+        const_value.T,
+        norm_gains.T,
+        tokens[0],
+        *[
+            w.reshape(n_loc, D * units // LANES, LANES)
+            for w in (expert_gate, expert_up, expert_down)
+        ],
+        doc_ids,
         routes_t,
-        prev,
+        prev_logits[0].T,
         upstream,
     )
+    gathered_w = gathered_w.reshape(n_d, 3, D, units)
     if units % LANES:
-        flat = gathered_w.transpose(1, 2, 3, 0, 4).reshape(1, 3, n_loc, D, n_d * units)
+        flat = gathered_w.transpose(1, 2, 0, 3).reshape(1, 3, D, n_d * units)
     else:
         flat = gathered_w
-    results, grads = experts_pass(gathered.reshape(n_c, 2, n_e, n_loc, slots, D), flat)
+    results, grads = experts_pass(gathered, flat)
     if units % LANES:
-        grads = grads.reshape(3, n_loc, D, n_d, units).transpose(3, 0, 1, 2, 4)
-    (block_rows, d_x, d_prev, q_grad, k_grad, v_grad, o_grad, s_grad, *expert_grads) = backward(
+        grads = grads.reshape(3, D, n_d, units).transpose(2, 0, 1, 3)
+    results = backward(
         sizes,
         cfg,
-        results.reshape(n_c // 2, 2, 2, n_e, n_loc * slots, D),
+        results.reshape(n_c // 2, 2, 2, n_e * n_loc, slots, D),
         h,
         a2,
         small,
         upstream,
-        route_rows,
         routes_t,
         wo,
         wqkv,
@@ -1357,21 +1453,17 @@
         v_h,
         probs,
         x_all,
-        grads.reshape(n_d, 3 * n_loc * D * units // LANES, LANES),
-    )
+        grads.reshape(n_d, 3 * D * units // LANES, LANES),
+    )
+    block_rows, d_x, d_prev, *square = hand_out(results)
+    narrow = square[4:8]
     return (
         block_rows[None],
         d_x[None],
-        d_prev[None],
-        q_grad,
-        k_grad,
-        v_grad,
-        o_grad,
-        s_grad[:, :n_all],
-        s_grad[:, n_all : n_all + 4],
-        s_grad[:, n_all + 4 : n_all + 6],
-        s_grad[:, n_all + 6 : n_all + 8],
-        *[part.reshape(n_loc, D, units) for part in expert_grads],
+        d_prev.T[None],
+        *square[:4],
+        *[grad.T for grad in narrow],
+        *[grad.reshape(n_loc, D, units) for grad in square[8:]],
     )
 
 

time: 267 us -> 209 us (0.78)
  local copies, waits for them, and re-layouts: 23.8 us -> 0 us
  between operations: 14.4 us -> 0.85 us
  Pallas kernels: 217 us -> 208 us
  waiting for transfers between devices: 6.24 us -> 0 us
  other arithmetic: 4.5 us -> 0 us
    pallas_call x2, Pallas kernels: 60.1 us -> 17.9 us  [the longest x1 14.2 us: experts_pass(): pl.pallas_call(expert_kernel, grid=(n_c // take,), out_shape=(jax.ShapeDt...]
    pallas_call x1, Pallas kernels: 42.1 us -> 79.6 us  [front(): pl.pallas_call(functools.partial(front_kernel, sizes, cfg), out_shape=(sh...]
    unnamed x61 -> x0, local copies, waits for them, and re-layouts: 13.8 us -> none
    all_gather x1 -> x0, waiting for transfers between devices: 6.22 us -> none  [body(): gathered_w = lax.all_gather(pieces, 'dp', axis=0)]
    pallas_call x1, Pallas kernels: 115 us -> 110 us  [backward(): pl.pallas_call(functools.partial(back_kernel, sizes, cfg), out_shape=(sha...]
    slice x6 -> x0, local copies, waits for them, and re-layouts: 4.45 us -> none  [the longest x1 1.43 us: body(): a_all = a_all[:, :, :, :w_rows].reshape(D, width)]
    another operation x7 -> x0, other arithmetic: 3.63 us -> none  [the longest x3 3.62 us: body(): pieces = jnp.stack([expert_gate, expert_up, expert_down]).astype(BF16)]
    pad x6 -> x0, local copies, waits for them, and re-layouts: 3.45 us -> none  [pad_to(): return jnp.pad(array, widths)]
  transfers between devices with their start and end apart: 1 -> 0, of which waited for: 1 -> 0; matrix products, arithmetic and copies ran while one was open for 4% -> 0% of each run, Pallas kernels for 34% -> 0%
where the time goes in v3:
time: 209 us
  Pallas kernels  208 us (100%)
    pallas_call x1, Pallas kernels, backward(): pl.pallas_call(functools.partial(back_kernel, sizes, cfg), out_shape=(sha...  110 us
    pallas_call x1, Pallas kernels, front(): pl.pallas_call(functools.partial(front_kernel, sizes, cfg), out_shape=(sh...  79.6 us
    pallas_call x1, Pallas kernels, experts_pass(): pl.pallas_call(expert_kernel, grid=(n_c // take,), out_shape=(jax.ShapeDt...  14.2 us

profile of v3, /device:TPU:1, one launch (start us, length us, event | category | flops | bytes accessed | tf_op | source)
XLA Modules:
  0.0 208.5 jit_solution(17576923652613558404)
XLA Ops:
  0.7 79.6 %front.1 = (bf16[4,256,768]{2,1,0:T(8,128)(2,1)}, bf16[768,576]{1,0:T(8,128)(2,1)}, bf16[768,768]{1,0:T(8,128)(2,1)}, bf16[768,128]{1,0:T(8,128)(2,1)}, f32[8,76...) custom-call(f32[24,768]{1,0:T(8,128)} %wq_ref.1, ...), custom_call_target="tpu_custom_call" | custom-call | tf_op jit(solution)/shard_map/front/pallas_call | solution.py:539
  80.3 14.2 %experts_pass.1 = (bf16[4,2,4,64,768]{4,3,2,1,0:T(8,128)(2,1)}, bf16[4,3,768,128]{3,2,1,0:T(8,128)(2,1)}) custom-call(bf16[4,2,4,64,768]{4,3,2,1,0:T(8,128)(2,1)} %get-tuple-element.60.x_ref.dy_ref, bf16[4,2,4,64,768]{4,3,2,1,0:T(8,128)(2,1)} %get-tuple-element.60.x_ref.dy_ref, bf16[4,3,768,128]{3,2,1,0:T(8,128)(2,1)} %bitcast.28), custom_call_target="tpu_custom_call" | custom-call | tf_op jit(solution)/shard_map/experts_pass/pallas_call | solution.py:636
  94.4 110.2 %backward.1 = (f32[256,768]{1,0:T(8,128)}, f32[256,768]{1,0:T(8,128)}, f32[8,256]{1,0:T(8,128)}, f32[24,768]{1,0:T(8,128)}, f32[24,768]{1,0:T(8,128)}, /*index=5...) custom-call(bf16[2,2,2,4,64,768]{5,4,3,2,1,0:T(8,128)(2,1)} %bitcast, ...), custom_call_target="tpu_custom_call" | custom-call | tf_op jit(solution)/shard_map/backward/pallas_call | solution.py:1259
  204.6 3.7 %hand_out.1 = (f32[256,768]{1,0:T(8,128)}, f32[256,768]{1,0:T(8,128)}, f32[8,256]{1,0:T(8,128)}, f32[24,768]{1,0:T(8,128)}, f32[24,768]{1,0:T(8,128)}, /*index=5...) custom-call(f32[256,768]{1,0:T(8,128)} %get-tuple-element.78.refs_0_, ...), custom_call_target="tpu_custom_call" | custom-call | tf_op jit(solution)/shard_map/hand_out/pallas_call | solution.py:1350

commit v4 on v3

--- a/solution.py
+++ b/solution.py
@@ -41,11 +41,14 @@
     )
 
 
-def greet(devices):
+def hail(devices):
     barrier = pltpu.get_barrier_semaphore()
     for device in devices:
         pl.semaphore_signal(barrier, inc=1, device_id=device, device_id_type=MESH)
-    pl.semaphore_wait(barrier, len(devices))
+
+
+def await_hails(devices):
+    pl.semaphore_wait(pltpu.get_barrier_semaphore(), len(devices))
 
 
 def context_peers(sizes, place):
@@ -251,8 +254,20 @@
     h_ref,
     a2_ref,
     small_ref,
+    back_ref,
+    gw_ref,
     p_ref,
     slots_ref,
+    res,
+    inn,
+    osum,
+    outr,
+    stage,
+    blk,
+    gate_scr,
+    up_scr,
+    hid_scr,
+    acc_scr,
     ew_ref,
     small_scr,
     a_ref,
@@ -279,6 +294,13 @@
     r_ow,
     s_xg,
     r_xg,
+    b_sem,
+    s_in,
+    r_in,
+    s_out,
+    r_out,
+    s_h,
+    r_h,
 ):
     n_e, n_c, n_d = sizes
     hp, n_ff, n_all, n_loc, slots = cfg
@@ -290,6 +312,10 @@
     n_s = n_e * n_loc
     me, there, back = homes(sizes, n_loc, place)
     d_peers = [(e, c, lax.rem(d + k, n_d)) for k in range(1, n_d)]
+    neighbours = (
+        c_all + d_peers + expert_peers(sizes, place) + crossing_only(sizes, n_loc, place)
+    )
+    hail(neighbours)
     w_rows = wq_ref.shape[0]
     small_scr[...] = jnp.zeros_like(small_scr)
     at = 0
@@ -308,7 +334,7 @@
                     BF16
                 )
         a_ref[b, :w_rows, 3 * hc :] = w_small
-    greet(c_all + d_peers + expert_peers(sizes, place) + crossing_only(sizes, n_loc, place))
+    await_hails(neighbours)
     post = Courier(s_c, r_c)
     turned = [
         post.carry(a_ref.at[lax.rem(c + k, n_c)], ag.at[e, c, d], device)
@@ -328,8 +354,7 @@
     og[e, c, d] = ow_ref[...]
     xg_ref[pl.ds(c, 1)] = xown_ref[...][None]
     for n, ref in enumerate((gate_ref, up_ref, down_ref)):
-        size = ref.shape[1]
-        ew_own[:, n * size : (n + 1) * size, :] = ref[...].astype(BF16)
+        ew_own[:, n] = ref[...].astype(BF16)
     for copy in turned:
         copy.wait_recv()
     a_spread = Spread(sizes, place, post, ag.at[e, :, d], lambda j, k: ag.at[j, :, k])
@@ -338,16 +363,19 @@
     mates = [(e, c, group * size + lax.rem(seat + k, size)) for k in range(1, size)]
     keep_w = pltpu.make_async_copy(ew_own.at[group], ew_ref.at[d], l_g.at[2 * n_s])
     keep_w.start()
+    w_far = {}
+    for n in range(3):
+        for k in range(1, n_loc):
+            to = lax.rem(group + k, n_loc)
+            w_far[n, k] = post.carry(
+                ew_own.at[to, n], ew_ref.at[d, n], (e, c, to * size + seat)
+            )
     w_near = [post.carry(ew_own.at[group], ew_ref.at[d], device) for device in mates]
-    w_far = []
-    for k in range(1, n_loc):
-        to = lax.rem(group + k, n_loc)
-        w_far.append(post.carry(ew_own.at[to], ew_ref.at[d], (e, c, to * size + seat)))
-
-    def pass_weights():
-        for k, copy in enumerate(w_far, 1):
-            copy.wait_recv()
-            block = ew_ref.at[lax.rem(group - k + n_loc, n_loc) * size + seat]
+
+    def pass_weights(n):
+        for k in range(1, n_loc):
+            w_far[n, k].wait_recv()
+            block = ew_ref.at[lax.rem(group - k + n_loc, n_loc) * size + seat, n]
             w_near.extend([post.carry(block, block, device) for device in mates])
 
     ow_spread.onward()
@@ -401,6 +429,7 @@
         vh_ref[j] = kv[:, hc + j * HEAD_DIM : hc + (j + 1) * HEAD_DIM]
     vt_scr[...] = dot(wqkv[:, 2 * hc :], a1, 0, 1).astype(BF16)
 
+    pass_weights(0)
     documents = drow_ref[...].astype(F32)
     document_of = jnp.broadcast_to(documents, (LANES, length)).T[:, :1]
     turn = 0
@@ -436,7 +465,7 @@
                 o_scr.at[b], mixed_ref.at[c], s_o.at[b], r_o.at[c], (e, b, d)
             ).start()
 
-    pass_weights()
+    pass_weights(1)
     for n in range(max(0, turn - 2), turn):
         p_copies[n].wait()
     ow_rows.finish()
@@ -506,17 +535,174 @@
         for j in range(1, n_s):
             crossing[t, j].wait_recv()
             crossing[t, 0](j, xin.at[t, back[j]])
-    for made, _ in gathers.values():
-        made.forward()
-    for made, keep in gathers.values():
-        made.finish()
-        keep.wait()
+        if t == 0:
+            pass_weights(2)
+
+    def gathered(t):
+        for j in range(n_s):
+            gathers[t, j][0].forward()
+        for j in range(n_s):
+            gathers[t, j][0].finish()
+            gathers[t, j][1].wait()
+
+    roomy = len(stage.shape) == 2
+    take = blk.shape[1]
+    blocks = n_c // take
+    pairs = n_c // 2
+    outer, inner = c // 2, c % 2
+    peers = context_peers(sizes, place)
+
+    def load_rows(t, n):
+        if roomy:
+            return slots_ref[n * take : (n + 1) * take, t].reshape(-1, D)
+        copy = pltpu.make_async_copy(slots_ref.at[pl.ds(n * take, take), t], blk.at[t], b_sem.at[0])
+        copy.start()
+        copy.wait()
+        return blk[t].reshape(-1, D)
+
+    def store_rows(t, n, value):
+        value = value.astype(BF16).reshape(take, n_s, slots, D)
+        if roomy:
+            res[n * take : (n + 1) * take, t] = value
+        else:
+            blk[2] = value
+            copy = pltpu.make_async_copy(blk.at[2], res.at[pl.ds(n * take, take), t], b_sem.at[0])
+            copy.start()
+            copy.wait()
+
+    def load(ref, slot=0):
+        if roomy:
+            return ref[...].astype(F32)
+        copy = pltpu.make_async_copy(ref, stage.at[slot], b_sem.at[0])
+        copy.start()
+        copy.wait()
+        return stage[slot].astype(F32)
+
+    def store(ref, value):
+        if roomy:
+            ref[...] = value
+        else:
+            stage[3] = value
+            copy = pltpu.make_async_copy(stage.at[3], ref, b_sem.at[0])
+            copy.start()
+            copy.wait()
+
+    order = [*reversed(range(1, n_s)), 0]
+    to_pair, along, home = {}, {}, {}
+
+    def sum_pair(t):
+        for j in order:
+            src = there[j][0]
+            for k in [*range(1, pairs), 0]:
+                n = (t * n_s + j) * pairs + k
+                far = lax.rem(outer + k, pairs)
+                copy = remote(
+                    res.at[far * 2 + 1 - inner, t, src],
+                    inn.at[far, t, src],
+                    s_in.at[n],
+                    r_in.at[n],
+                    peers[0],
+                )
+                copy.start()
+                to_pair[t, j, k] = copy
+
+    def sum_along(t):
+        for j in order:
+            src = there[j][0]
+            for k in range(1, pairs):
+                n = (t * n_s + j) * pairs + k
+                far = lax.rem(outer + k, pairs)
+                to_pair[t, j, k].wait_recv()
+                value = load(res.at[far * 2 + inner, t, src]) + load(inn.at[far, t, src], 1)
+                store(osum.at[k - 1, t, src], value.astype(BF16))
+                copy = remote(
+                    osum.at[k - 1, t, src],
+                    outr.at[k - 1, t, src],
+                    s_out.at[n],
+                    r_out.at[n],
+                    peers[k],
+                )
+                copy.start()
+                along[t, j, k] = copy
+
+    def send_home(t):
+        for j in order:
+            src, device = there[j]
+            to_pair[t, j, 0].wait_recv()
+            value = load(res.at[c, t, src]) + load(inn.at[outer, t, src], 1)
+            for k in range(1, pairs):
+                along[t, j, k].wait_recv()
+                value = value + load(outr.at[k - 1, t, src], 2)
+            if j == 0:
+                back_ref[t, me] = value.astype(BF16)
+            else:
+                xin[t, src] = value.astype(BF16)
+                n = t * n_s + j
+                copy = remote(xin.at[t, src], back_ref.at[t, me], s_h.at[n], r_h.at[n], device)
+                copy.start()
+                home[t, j] = copy
+
+    gathered(0)
+    for copy in w_near:
+        copy.wait_recv()
+    keep_w.wait()
+    parts, units = ew_ref.shape[0], ew_ref.shape[3]
+    gate, up, down = [
+        jnp.concatenate([ew_ref[k, n] for k in range(parts)], axis=1) for n in range(3)
+    ]
+    def hidden_of(n):
+        x = load_rows(0, n)
+        gate_pre = dot(x, gate)
+        up_pre = dot(x, up)
+        return gate_pre, up_pre, (gate_pre * jax.nn.sigmoid(gate_pre) * up_pre).astype(BF16)
+
+    for n in range(blocks):
+        gate_pre, up_pre, hidden = hidden_of(n)
+        if blocks == 1:
+            gate_scr[...] = gate_pre
+            up_scr[...] = up_pre
+            hid_scr[...] = hidden
+        store_rows(0, n, dot(hidden, down, 1, 1))
+    sum_pair(0)
+    gathered(1)
+    for n in range(blocks):
+        dy = load_rows(1, n)
+        d_hidden = dot(dy, down)
+        if n == 0:
+            sum_along(0)
+        if blocks == 1:
+            gate_pre, up_pre, hidden = gate_scr[...], up_scr[...], hid_scr[...]
+        else:
+            gate_pre, up_pre, hidden = hidden_of(n)
+        sig = jax.nn.sigmoid(gate_pre)
+        d_gate = (d_hidden * up_pre * sig * (1.0 + gate_pre * (1.0 - sig))).astype(BF16)
+        d_up = (d_hidden * gate_pre * sig).astype(BF16)
+        store_rows(1, n, dot(d_gate, gate, 1, 1) + dot(d_up, up, 1, 1))
+        if n == blocks - 1:
+            sum_pair(1)
+        x = load_rows(0, n)
+        for m, (left, right) in enumerate(((x, d_gate), (x, d_up), (dy, hidden))):
+            part = dot(left, right, 0, 0)
+            if blocks > 1:
+                if n > 0:
+                    part = part + acc_scr[m]
+                if n < blocks - 1:
+                    acc_scr[m] = part
+            if n == blocks - 1:
+                for k in range(parts):
+                    gw_ref[k, m] = part[:, k * units : (k + 1) * units].astype(BF16)
+            if n == blocks - 1 and m == 0:
+                sum_along(1)
+            if n == blocks - 1 and m == 1:
+                send_home(0)
+    send_home(1)
+    for copy in home.values():
+        copy.wait()
+    for copy in [*to_pair.values(), *along.values()]:
+        copy.wait_send()
     for t in range(2):
         for j in range(1, n_s):
             crossing[t, j].wait_send()
-    for copy in w_near:
-        copy.wait_recv()
-    keep_w.wait()
     post.finish()
 
 
@@ -528,14 +714,23 @@
     length = rows * n_c
     padded = up_to(operands[0].shape[0], 16)
     width = up_to(3 * hc + SMALL, LANES)
-    part = operands[9].shape[1]
-    posts = (n_c - 1) + 2 * spread_count(sizes) + n_d - 1
+    units = operands[9].shape[2]
+    size = n_d // n_loc
+    posts = (n_c - 1) + 2 * spread_count(sizes) + size - 1 + 3 * (n_loc - 1) * size
     n_s = n_e * n_loc
     dma = pltpu.SemaphoreType.DMA
     vmem = pl.BlockSpec(memory_space=pltpu.VMEM)
     anywhere = pl.BlockSpec(memory_space=pl.ANY)
     shape = jax.ShapeDtypeStruct
     gathers = 2 * n_s * (n_c - 1)
+    pairs = n_c // 2
+    more = max(1, pairs - 1)
+    wide = [(n_c, 2), (n_c, 2), (pairs, 2), (more, 2), (more, 2)]
+    wide = [(*dims, n_s, slots, D) for dims in wide]
+    roomy = n_c * n_s * slots * D <= 2**20
+    held = [pltpu.VMEM(dims, BF16) for dims in wide] if roomy else []
+    extra = [] if roomy else [shape(dims, BF16) for dims in wide]
+    take = n_c if n_c * n_s * slots <= 1024 else max(1, 512 // (n_s * slots))
     return pl.pallas_call(
         functools.partial(front_kernel, sizes, cfg),
         out_shape=(
@@ -552,19 +747,29 @@
             shape((rows, D), F32),
             shape((rows, D), BF16),
             shape((rows, LANES), F32),
+            shape((2, n_s, slots, D), BF16),
+            shape((n_d, 3, D, units), BF16),
             shape((hp, n_c, length, rows), BF16),
-            shape((n_c, 2, n_s, slots, D), BF16),
-            shape((n_d, 3 * part, LANES), BF16),
+            *extra,
         ),
         in_specs=[vmem] * len(operands),
-        out_specs=(vmem,) * 13 + (anywhere,) * 3,
+        out_specs=(vmem,) * 15 + (anywhere,) * (1 + len(extra)),
         scratch_shapes=[
+            *held,
+            pltpu.VMEM((8, LANES) if roomy else (4, slots, D), BF16),
+            pltpu.VMEM((3, take, n_s, *((8, LANES) if roomy else (slots, D))), BF16),
+            *[
+                pltpu.VMEM((n_c * n_s * slots, n_d * units) if take == n_c else (16, LANES), kind)
+                for kind in (F32, F32, BF16)
+            ],
+            pltpu.VMEM((3, D, n_d * units) if take < n_c else (8, LANES), F32),
+            pltpu.VMEM((n_d, 3, D, units), BF16),
             pltpu.VMEM((LANES, LANES), F32),
             pltpu.VMEM((n_c, padded, width), BF16),
             pltpu.VMEM((padded, D), BF16),
             pltpu.VMEM((n_e, n_c, n_d, padded, width), BF16),
             pltpu.VMEM((n_e, n_c, n_d, padded, D), BF16),
-            pltpu.VMEM((n_loc, 3 * part, LANES), BF16),
+            pltpu.VMEM((n_loc, 3, D, units), BF16),
             pltpu.VMEM((n_c, hc, rows), BF16),
             pltpu.VMEM((hc, length), BF16),
             pltpu.VMEM((2, length, rows), BF16),
@@ -581,6 +786,9 @@
             dma((posts,)),
             dma((posts,)),
             *[dma((n_c - 1,))] * 4,
+            dma((1,)),
+            *[dma((2 * n_s * pairs,))] * 4,
+            *[dma((2 * n_s,))] * 2,
         ],
         compiler_params=pltpu.CompilerParams(
             collective_id=0, has_side_effects=True, vmem_limit_bytes=VMEM_LIMIT
@@ -589,78 +797,10 @@
     )(*operands)
 
 
-def expert_kernel(x_ref, dy_ref, w_ref, out_ref, gw_ref, total):
-    step = pl.program_id(0)
-    parts = w_ref.shape[0]
-    x = x_ref[...].reshape(-1, D)
-    dy = dy_ref[...].reshape(-1, D)
-    block = out_ref.shape[0:1] + out_ref.shape[2:]
-    gate, up, down = [
-        jnp.concatenate([w_ref[k, n] for k in range(parts)], axis=1) for n in range(3)
-    ]
-    gate_pre = dot(x, gate)
-    up_pre = dot(x, up)
-    sig = jax.nn.sigmoid(gate_pre)
-    hidden = (gate_pre * sig * up_pre).astype(BF16)
-    result = dot(hidden, down, 1, 1).astype(BF16)
-    out_ref[:, 0] = result.reshape(block)
-    d_hidden = dot(dy, down)
-    d_gate = (d_hidden * up_pre * sig * (1.0 + gate_pre * (1.0 - sig))).astype(BF16)
-    d_up = (d_hidden * gate_pre * sig).astype(BF16)
-    d_x = dot(d_gate, gate, 1, 1) + dot(d_up, up, 1, 1)
-    out_ref[:, 1] = d_x.astype(BF16).reshape(block)
-    grads = (dot(x, d_gate, 0, 0), dot(x, d_up, 0, 0), dot(dy, hidden, 0, 0))
-
-    @pl.when(step == 0)
-    def _():
-        for n in range(3):
-            total[n] = grads[n]
-
-    @pl.when(step > 0)
-    def _():
-        for n in range(3):
-            total[n] += grads[n]
-
-    @pl.when(step == pl.num_programs(0) - 1)
-    def _():
-        width = gate.shape[1] // parts
-        for n in range(3):
-            for k in range(parts):
-                gw_ref[k, n] = total[n, :, k * width : (k + 1) * width].astype(BF16)
-
-
-def experts_pass(gathered, weights):
-    n_c, _, n_s, slots, _ = gathered.shape
-    parts, _, _, units = weights.shape
-    take = max(1, min(n_c, 512 // (n_s * slots)))
-    return pl.pallas_call(
-        expert_kernel,
-        grid=(n_c // take,),
-        out_shape=(
-            jax.ShapeDtypeStruct(gathered.shape, BF16),
-            jax.ShapeDtypeStruct(weights.shape, BF16),
-        ),
-        in_specs=[
-            pl.BlockSpec((take, 1, n_s, slots, D), lambda i: (i, 0, 0, 0, 0)),
-            pl.BlockSpec((take, 1, n_s, slots, D), lambda i: (i, 1, 0, 0, 0)),
-            pl.BlockSpec((parts, 3, D, units), lambda i: (0, 0, 0, 0)),
-        ],
-        out_specs=(
-            pl.BlockSpec((take, 2, n_s, slots, D), lambda i: (i, 0, 0, 0, 0)),
-            pl.BlockSpec((parts, 3, D, units), lambda i: (0, 0, 0, 0)),
-        ),
-        scratch_shapes=[pltpu.VMEM((3, D, parts * units), F32)],
-        compiler_params=pltpu.CompilerParams(
-            dimension_semantics=("arbitrary",), vmem_limit_bytes=VMEM_LIMIT
-        ),
-        name="experts_pass",
-    )(gathered, gathered, weights)
-
-
 def back_kernel(
     sizes,
     cfg,
-    res_ref,
+    ret_ref,
     h_ref,
     a2_ref,
     small_ref,
@@ -692,12 +832,6 @@
     egate_ref,
     eup_ref,
     edown_ref,
-    inn,
-    osum,
-    outr,
-    back,
-    xsum,
-    stage,
     dhg,
     dht_scr,
     p_scr,
@@ -728,12 +862,6 @@
     o_z,
     o_zr,
     l_sem,
-    s_in,
-    r_in,
-    s_out,
-    r_out,
-    s_x,
-    r_x,
     s_g,
     r_g,
     p_sem,
@@ -761,10 +889,6 @@
     peers = context_peers(sizes, place)
     e_peers = expert_peers(sizes, place)
 
-    in_vmem = len(stage.shape) == 5
-    if in_vmem:
-        take = pltpu.make_async_copy(res_ref.at[:, inner], stage, l_sem.at[0])
-        take.start()
     bring = pltpu.make_async_copy(gw_ref, ew_own, l_sem.at[1])
     bring.start()
 
@@ -773,9 +897,7 @@
 
     fetch_x(c, 2).start()
     fetch_x(0, 0).start()
-    n_s = n_e * n_loc
-    me, there_s, _ = homes(sizes, n_loc, place)
-    greet(peers + e_peers + d_peers + crossing_only(sizes, n_loc, place))
+    hail(peers + e_peers + d_peers)
 
     size = n_d // n_loc
     group, seat = d // size, lax.rem(d, size)
@@ -791,9 +913,10 @@
                 e_near[k, r] = freight.carry(
                     ew_own.at[other * size + lax.rem(seat + k + 1, size)], ew_mid.at[k, r], mate
                 )
+
+    def expert_cross():
+        for k, mate in enumerate(mates):
             e_near[k, -1] = freight.carry(ew_own.at[mate[2]], ew_in.at[k], mate)
-
-    def expert_cross():
         for r, other in enumerate(others):
             target = other * size + seat
             for k in range(size - 1):
@@ -829,83 +952,9 @@
                 ].astype(F32)[None]
         freight.finish()
 
+    await_hails(peers + e_peers + d_peers)
     bring.wait()
     expert_start()
-
-    def load(ref, slot=0):
-        if in_vmem:
-            return ref[...].astype(F32)
-        copy = pltpu.make_async_copy(ref, stage.at[slot], l_sem.at[0])
-        copy.start()
-        copy.wait()
-        return stage[slot].astype(F32)
-
-    def own_part(there, t, src):
-        if in_vmem:
-            return stage[there, t, src].astype(F32)
-        return load(res_ref.at[there, inner, t, src])
-
-    def store(ref, value):
-        if in_vmem:
-            ref[...] = value
-        else:
-            stage[3] = value
-            copy = pltpu.make_async_copy(stage.at[3], ref, l_sem.at[0])
-            copy.start()
-            copy.wait()
-
-    pieces = [(t, j) for j in [*reversed(range(1, n_s)), 0] for t in range(2)]
-    first_copies = {}
-    for t, j in pieces:
-        src = there_s[j][0]
-        for k in [*range(1, pairs), 0]:
-            n = (t * n_s + j) * pairs + k
-            there = lax.rem(outer + k, pairs)
-            copy = remote(
-                res_ref.at[there, 1 - inner, t, src],
-                inn.at[there, t, src],
-                s_in.at[n],
-                r_in.at[n],
-                peers[0],
-            )
-            copy.start()
-            first_copies[t, j, k] = copy
-    if in_vmem:
-        take.wait()
-    second = {}
-    for t, j in pieces:
-        src = there_s[j][0]
-        for k in range(1, pairs):
-            n = (t * n_s + j) * pairs + k
-            there = lax.rem(outer + k, pairs)
-            first_copies[t, j, k].wait_recv()
-            total = own_part(there, t, src) + load(inn.at[there, t, src], 1)
-            store(osum.at[k - 1, t, src], total.astype(BF16))
-            copy = remote(
-                osum.at[k - 1, t, src], outr.at[k - 1, t, src], s_out.at[n], r_out.at[n], peers[k]
-            )
-            copy.start()
-            second[t, j, k] = copy
-    home = {}
-    for t, j in pieces:
-        src = there_s[j][0]
-        first_copies[t, j, 0].wait_recv()
-        total = own_part(outer, t, src) + load(inn.at[outer, t, src], 1)
-        for k in range(1, pairs):
-            second[t, j, k].wait_recv()
-            total = total + load(outr.at[k - 1, t, src], 2)
-        if j == 0:
-            back[t, me] = total.astype(BF16)
-        else:
-            xsum[t, src] = total.astype(BF16)
-            n = t * n_s + j
-            copy = remote(
-                xsum.at[t, src], back.at[t, me], s_x.at[n], r_x.at[n], there_s[j][1]
-            )
-            copy.start()
-            home[t, j] = copy
-
-    expert_cross()
     h = h_ref[...]
     a2 = a2_ref[...].astype(F32)
     g = g_ref[...]
@@ -924,9 +973,7 @@
     a_weight = alpha[0] * w_pair[0] + alpha[1] * w_pair[1]
     one_weight = one_on[0] * w_pair[0] + one_on[1] * w_pair[1]
     two_weight = two_on[0] * w_pair[0] + two_on[1] * w_pair[1]
-    for copy in home.values():
-        copy.wait_recv()
-    returned = [back[t].reshape(n_ff * slots, D) for t in range(2)]
+    returned = [ret_ref[t].reshape(n_ff * slots, D) for t in range(2)]
     block = h
     d_weight = []
     for k in range(2):
@@ -985,6 +1032,7 @@
     )
     gather.start()
     dx_ref[...] = d_h
+    expert_cross()
     g_o = dot(mixed_ref[...].reshape(n_c * hc, rows), d_hb)
     run = n_d * w_rows
     for b in range(n_c):
@@ -1210,12 +1258,6 @@
         ref[...] = s_lines[at : at + ref.shape[0], :w_rows]
         at += ref.shape[0]
     bag.finish()
-    for copy in first_copies.values():
-        copy.wait_send()
-    for copy in second.values():
-        copy.wait_send()
-    for copy in home.values():
-        copy.wait_send()
     for _, copy in to_pair:
         copy.wait_send()
     for copy in along:
@@ -1229,13 +1271,10 @@
     rows = operands[1].shape[0]
     length = rows * n_c
     pairs = n_c // 2
-    per = slots
     dma = pltpu.SemaphoreType.DMA
     vmem = pl.BlockSpec(memory_space=pltpu.VMEM)
     anywhere = pl.BlockSpec(memory_space=pl.ANY)
     shape = jax.ShapeDtypeStruct
-    n_s = n_e * n_loc
-    n_in = 2 * n_s * pairs
     part = operands[17].shape[1]
     w_rows = D // (n_e * n_c * n_d)
     chunks = up_to(3 * hc + SMALL, LANES) // LANES
@@ -1249,13 +1288,7 @@
     parcels = 2 * pairs - 1 + n_e - 1 + n_d - 1
     n_more = max(1, pairs - 1)
     in_specs = [vmem] * len(operands)
-    in_specs[0] = anywhere
     in_specs[15] = in_specs[16] = in_specs[17] = anywhere
-    arriving = [(pairs, 2, n_s, per, D), (n_more, 2, n_s, per, D), (n_more, 2, n_s, per, D)]
-    roomy = 2 * pairs * n_s * per * D <= 2**21
-    held = [pltpu.VMEM(dims, BF16) for dims in arriving] if roomy else []
-    extra = [] if roomy else [shape(dims, BF16) for dims in arriving]
-    stage = pltpu.VMEM(arriving[0] if roomy else (4, per, D), BF16)
     return pl.pallas_call(
         functools.partial(back_kernel, sizes, cfg),
         out_shape=(
@@ -1265,15 +1298,10 @@
             *[shape((w_rows, D), F32)] * 4,
             *[shape((n, w_rows), F32) for n in (n_all, 4, 2, 2)],
             *[shape((n_loc, part // 3, LANES), F32)] * 3,
-            *extra,
         ),
         in_specs=in_specs,
-        out_specs=(vmem,) * 14 + (anywhere,) * len(extra),
+        out_specs=(vmem,) * 14,
         scratch_shapes=[
-            *held,
-            pltpu.VMEM((2, n_s, per, D), BF16),
-            pltpu.VMEM((2, n_s, per, D), BF16),
-            stage,
             pltpu.VMEM((n_c, rows, D), BF16),
             pltpu.VMEM((hc, length), BF16),
             pltpu.VMEM((2, length, rows), BF16),
@@ -1304,12 +1332,6 @@
             pltpu.VMEM((n_d, few, D), BF16),
             pltpu.VMEM((n_d - 1, few, D), BF16),
             dma((5,)),
-            dma((n_in,)),
-            dma((n_in,)),
-            dma((n_in,)),
-            dma((n_in,)),
-            dma((2 * n_s,)),
-            dma((2 * n_s,)),
             dma((n_c - 1,)),
             dma((n_c - 1,)),
             dma((2,)),
@@ -1326,7 +1348,7 @@
             collective_id=1, has_side_effects=True, vmem_limit_bytes=VMEM_LIMIT
         ),
         name="backward",
-    )(*operands)[:14]
+    )(*operands)
 
 
 def hand_out_kernel(*refs):
@@ -1401,9 +1423,10 @@
         h,
         a2,
         small,
+        returned,
+        grads,
         probs,
-        gathered,
-        gathered_w,
+        *_,
     ) = front(
         sizes,
         cfg,
@@ -1416,27 +1439,18 @@
         const_value.T,
         norm_gains.T,
         tokens[0],
-        *[
-            w.reshape(n_loc, D * units // LANES, LANES)
-            for w in (expert_gate, expert_up, expert_down)
-        ],
+        expert_gate,
+        expert_up,
+        expert_down,
         doc_ids,
         routes_t,
         prev_logits[0].T,
         upstream,
     )
-    gathered_w = gathered_w.reshape(n_d, 3, D, units)
-    if units % LANES:
-        flat = gathered_w.transpose(1, 2, 0, 3).reshape(1, 3, D, n_d * units)
-    else:
-        flat = gathered_w
-    results, grads = experts_pass(gathered, flat)
-    if units % LANES:
-        grads = grads.reshape(3, D, n_d, units).transpose(2, 0, 1, 3)
     results = backward(
         sizes,
         cfg,
-        results.reshape(n_c // 2, 2, 2, n_e * n_loc, slots, D),
+        returned,
         h,
         a2,
         small,

time: 209 us -> 205 us (0.981); the launches traced: 209 us -> 201 us
  Pallas kernels: 208 us -> 200 us
    pallas_call x1, Pallas kernels: 79.6 us -> 118 us  [front(): pl.pallas_call(functools.partial(front_kernel, sizes, cfg), out_shape=(sh...]
    pallas_call x1, Pallas kernels: 110 us -> 78.3 us  [backward(): pl.pallas_call(functools.partial(back_kernel, sizes, cfg), out_shape=(sha...]
    pallas_call x1 -> x0, Pallas kernels: 14.2 us -> none  [experts_pass(): pl.pallas_call(expert_kernel, grid=(n_c // take,), out_shape=(jax.ShapeDt...]
where the time goes in v4:
time: 205 us; the launch traced here: 201 us
  Pallas kernels  200 us (98%)
    pallas_call x1, Pallas kernels, front(): pl.pallas_call(functools.partial(front_kernel, sizes, cfg), out_shape=(sh...  118 us
    pallas_call x1, Pallas kernels, backward(): pl.pallas_call(functools.partial(back_kernel, sizes, cfg), out_shape=(sha...  78.3 us

profile of v4, /device:TPU:1, one launch (start us, length us, event | category | flops | bytes accessed | tf_op | source)
XLA Modules:
  0.0 200.8 jit_solution(2384111585631138915)
XLA Ops:
  0.7 118.0 %front.1 = (bf16[4,256,768]{2,1,0:T(8,128)(2,1)}, bf16[768,576]{1,0:T(8,128)(2,1)}, bf16[768,768]{1,0:T(8,128)(2,1)}, bf16[768,128]{1,0:T(8,128)(2,1)}, f32[8,76...) custom-call(f32[24,768]{1,0:T(8,128)} %wq_ref.1, ...), custom_call_target="tpu_custom_call" | custom-call | tf_op jit(solution)/shard_map/front/pallas_call | solution.py:734
  118.6 78.3 %backward.1 = (f32[256,768]{1,0:T(8,128)}, f32[256,768]{1,0:T(8,128)}, f32[8,256]{1,0:T(8,128)}, f32[24,768]{1,0:T(8,128)}, f32[24,768]{1,0:T(8,128)}, /*index=5...) custom-call(bf16[2,4,64,768]{3,2,1,0:T(8,128)(2,1)} %get-tuple-eleme, ...), custom_call_target="tpu_custom_call" | custom-call | tf_op jit(solution)/shard_map/backward/pallas_call | solution.py:1292
  196.9 3.7 %hand_out.1 = (f32[256,768]{1,0:T(8,128)}, f32[256,768]{1,0:T(8,128)}, f32[8,256]{1,0:T(8,128)}, f32[24,768]{1,0:T(8,128)}, f32[24,768]{1,0:T(8,128)}, /*index=5...) custom-call(f32[256,768]{1,0:T(8,128)} %get-tuple-element.74.refs_0_, ...), custom_call_target="tpu_custom_call" | custom-call | tf_op jit(solution)/shard_map/hand_out/pallas_call | solution.py:1372
